TPU v7x, 32 devices: a whole 2x2x4 slice. The times are simulated.
32 devices in a mesh: rows: 8 (over z, x), heads: 4 (over y, core).
Axes of the slice: x: 2, y: 2, z: 4, core: 2. Of those that a mesh axis runs over, the one named last changes fastest.
Arguments:
- latents: bfloat16 [8, 16, 32, 1280], P('rows', None, None, 'heads'), may hold values from -6 to 6
- text: bfloat16 [4, 77, 2048], replicated, may hold values from -6 to 6
- step_count: int32 [4], replicated, may hold values from 1 to 4, as said below
- time_index: int32 [4], replicated, may hold values from 0 to 3, as said below
- conv1_w: bfloat16 [3, 3, 1280, 1280], P(None, None, 'rows', 'heads'), may hold values from -0.0546875 to 0.0546875
- conv2_w: bfloat16 [3, 3, 1280, 1280], P(None, None, 'rows', 'heads'), may hold values from -0.0546875 to 0.0546875
- time_w: bfloat16 [1280, 1280], P('rows', 'heads'), may hold values from -0.15625 to 0.15625
- proj_in_w: bfloat16 [1280, 1280], P('rows', 'heads'), may hold values from -0.15625 to 0.15625
- qkv_w: bfloat16 [1280, 3, 1280], P('rows', None, 'heads'), may hold values from -0.15625 to 0.15625
- self_out_w: bfloat16 [1280, 1280], P('heads', 'rows'), may hold values from -1.25 to 1.25
- cross_q_w: bfloat16 [1280, 1280], P('rows', 'heads'), may hold values from -0.15625 to 0.15625
- cross_kv_w: bfloat16 [2048, 2, 1280], P('rows', None, 'heads'), may hold values from -0.125 to 0.125
- cross_out_w: bfloat16 [1280, 1280], P('heads', 'rows'), may hold values from -0.625 to 0.625
- ff_in_w: bfloat16 [1280, 2, 5120], P('rows', None, 'heads'), may hold values from -0.15625 to 0.15625
- ff_out_w: bfloat16 [5120, 1280], P('heads', 'rows'), may hold values from -0.078125 to 0.078125
- proj_out_w: bfloat16 [1280, 1280], P('rows', 'heads'), may hold values from -0.15625 to 0.15625
- gn_params: float32 [3, 2, 1280], P(None, None, 'heads'), may hold values from -1 to 1.5, as said below
- ln_params: float32 [3, 2, 1280], P(None, None, 'heads'), may hold values from -1 to 1.5, as said below
- biases: float32 [8, 1280], P(None, 'heads'), may hold values from -1.5 to 1.5
- ff_bias: float32 [2, 5120], P(None, 'heads'), may hold values from -1.5 to 1.5
- cotangent: bfloat16 [8, 16, 32, 1280], P('rows', None, None, 'heads'), may hold values from -6 to 6
Outputs:
- output: bfloat16 [8, 16, 32, 1280], P('rows', None, None, 'heads')
- latents_grad: float32 [8, 16, 32, 1280], P('rows', None, None, 'heads')
- conv1_w_grad: float32 [3, 3, 1280, 1280], P(None, None, 'rows', 'heads')
- conv2_w_grad: float32 [3, 3, 1280, 1280], P(None, None, 'rows', 'heads')
- time_w_grad: float32 [1280, 1280], P('rows', 'heads')
- proj_in_w_grad: float32 [1280, 1280], P('rows', 'heads')
- qkv_w_grad: float32 [1280, 3, 1280], P('rows', None, 'heads')
- self_out_w_grad: float32 [1280, 1280], P('heads', 'rows')
- cross_q_w_grad: float32 [1280, 1280], P('rows', 'heads')
- cross_kv_w_grad: float32 [2048, 2, 1280], P('rows', None, 'heads')
- cross_out_w_grad: float32 [1280, 1280], P('heads', 'rows')
- ff_in_w_grad: float32 [1280, 2, 5120], P('rows', None, 'heads')
- ff_out_w_grad: float32 [5120, 1280], P('heads', 'rows')
- proj_out_w_grad: float32 [1280, 1280], P('rows', 'heads')
- gn_params_grad: float32 [3, 2, 1280], P(None, None, 'heads')
- ln_params_grad: float32 [3, 2, 1280], P(None, None, 'heads')
- biases_grad: float32 [8, 1280], P(None, 'heads')
- ff_bias_grad: float32 [2, 5120], P(None, 'heads')
Inputs may be any that keep to these rules, and one draw needn't show every extreme that they name: `step_count`: each image's number of student steps; some image has 4 and some image has 1. `time_index`: below the image's step_count. `gn_params`: gains (index 0 of the second dimension) lie in 0.5 to 1.5, shifts in -1 to 1. `ln_params`: gains (index 0 of the second dimension) lie in 0.5 to 1.5, shifts in -1 to 1.
All inputs are finite; a program needn't handle non-finite values.
Results may differ from a plain program's by a relative error of at most 0.025.
Values may be sent and summed in bfloat16 or wider, within the bound.
No kernel may reach another device: no remote copies, remote signals or barrier semaphores. Data moves between devices by JAX's collectives and lax.ppermute only.
A program may use at most 320 MiB of HBM per device.

v0:
```python
import math

import jax
import jax.numpy as jnp
from jax import lax
from jax.sharding import PartitionSpec as P

C = 1280
DH = 64
GROUPS = 32


EPS_RES = 1e-05
EPS_MID = 1e-06
EPS_LAYER = 1e-05
CONTRACT_ROWS = (((0,), (0,)), ((), ()))
CONTRACT_LAST = (((1,), (1,)), ((), ()))


def swapped(x, axis, stride):
    return lax.ppermute(x, axis, [(i, i ^ 1 << stride) for i in range(lax.axis_size(axis))])


def full_channels(tensor):
    return lax.all_gather(tensor, "heads", axis=1, tiled=True)


def channel_total(tensor):
    return lax.psum_scatter(
        tensor.astype(jnp.bfloat16), "heads", scatter_dimension=1, tiled=True
    ).astype(jnp.float32)


def pair_total(first_sum, second_sum):
    other_first, other_second = swapped((first_sum, second_sum), "rows", 0)
    return (first_sum + other_first, second_sum + other_second)


def token_total(first_sum, second_sum):
    return lax.psum((first_sum, second_sum), "heads")


def silu_slope(inputs):
    sigma_val = jax.nn.sigmoid(inputs)
    return sigma_val * (1.0 + inputs * (1.0 - sigma_val))


def group_forward(inputs, params, epsilon):
    tokens, local_width = inputs.shape
    member = C // GROUPS
    grouped = inputs.reshape(tokens, local_width // member, member)
    count_all = 2.0 * tokens * member
    total_sum, squares = pair_total(
        jnp.sum(grouped, axis=(0, 2)), jnp.sum(grouped * grouped, axis=(0, 2))
    )
    center = total_sum / count_all
    inverse = lax.rsqrt(squares / count_all - center * center + epsilon)
    normed = ((grouped - center[None, :, None]) * inverse[None, :, None]).reshape(
        tokens, local_width
    )
    return (normed * params[0] + params[1], (normed, inverse))


def group_backward(gradient, params, stored):
    normed, inverse = stored
    tokens, local_width = gradient.shape
    member = C // GROUPS
    scaled = (gradient * params[0]).reshape(tokens, local_width // member, member)
    flat_norm = normed.reshape(tokens, local_width // member, member)
    count_all = 2.0 * tokens * member
    first_sum, second_sum = pair_total(
        jnp.sum(scaled, axis=(0, 2)), jnp.sum(scaled * flat_norm, axis=(0, 2))
    )
    back_flow = inverse[None, :, None] * (
        scaled
        - first_sum[None, :, None] / count_all
        - flat_norm * second_sum[None, :, None] / count_all
    )
    param_grad = jnp.stack([jnp.sum(gradient * normed, axis=0), jnp.sum(gradient, axis=0)])
    return (back_flow.reshape(tokens, local_width), param_grad)


def layer_forward(inputs, params):
    total_sum, squares = token_total(jnp.sum(inputs, axis=1), jnp.sum(inputs * inputs, axis=1))
    center = total_sum / C
    inverse = lax.rsqrt(squares / C - center * center + EPS_LAYER)
    normed = (inputs - center[:, None]) * inverse[:, None]
    return (normed * params[0] + params[1], (normed, inverse))


def layer_backward(gradient, params, stored):
    normed, inverse = stored
    scaled = gradient * params[0]
    first_sum, second_sum = token_total(jnp.sum(scaled, axis=1), jnp.sum(scaled * normed, axis=1))
    back_flow = inverse[:, None] * (
        scaled - first_sum[:, None] / C - normed * second_sum[:, None] / C
    )
    param_grad = jnp.stack([jnp.sum(gradient * normed, axis=0), jnp.sum(gradient, axis=0)])
    return (back_flow, param_grad)


def conv_forward(acts, kernel, is_upper, height, columns):
    sending = jnp.where(is_upper, acts[-columns:], acts[:columns])
    arrived = swapped(sending, "rows", 0)
    whole = full_channels(jnp.concatenate([acts, arrived], axis=0))
    inner = whole[: height * columns].reshape(height, columns, -1)
    border = whole[height * columns :].reshape(1, columns, -1)
    blank = jnp.zeros_like(border)
    padded = jnp.concatenate(
        [jnp.where(is_upper, blank, border), inner, jnp.where(is_upper, border, blank)], axis=0
    )
    padded = jnp.pad(padded, ((0, 0), (1, 1), (0, 0)))
    result = jnp.zeros((height * columns, kernel.shape[3]), jnp.float32)
    for row_shift in range(3):
        for col_shift in range(3):
            tap_rows = padded[
                row_shift : row_shift + height, col_shift : col_shift + columns
            ].reshape(height * columns, -1)
            result = result + jnp.dot(
                tap_rows, kernel[row_shift, col_shift], preferred_element_type=jnp.float32
            )
    return (result, padded)


def conv_backward(gradient, padded, kernel, is_upper, height, columns):
    wide = padded.shape[2]
    spread = jnp.zeros((height + 2, columns + 2, wide), jnp.float32)
    kernel_parts = []
    for row_shift in range(3):
        for col_shift in range(3):
            tap_rows = padded[
                row_shift : row_shift + height, col_shift : col_shift + columns
            ].reshape(height * columns, wide)
            kernel_parts.append(
                lax.dot_general(
                    tap_rows, gradient, CONTRACT_ROWS, preferred_element_type=jnp.float32
                )
            )
            flowing = lax.dot_general(
                gradient,
                kernel[row_shift, col_shift],
                CONTRACT_LAST,
                preferred_element_type=jnp.float32,
            )
            spread = spread.at[row_shift : row_shift + height, col_shift : col_shift + columns].add(
                flowing.reshape(height, columns, wide)
            )
    kernel_grad = jnp.stack(kernel_parts).reshape(3, 3, wide, -1)
    inner = spread[1 : height + 1, 1 : columns + 1].reshape(height * columns, wide)
    border = jnp.where(is_upper, spread[height + 1, 1 : columns + 1], spread[0, 1 : columns + 1])
    summed = channel_total(jnp.concatenate([inner, border], axis=0))
    own_part = summed[: height * columns]
    arrived = swapped(summed[height * columns :].astype(jnp.bfloat16), "rows", 0).astype(
        jnp.float32
    )
    blank = jnp.zeros_like(arrived)
    own_part = own_part.at[:columns].add(jnp.where(is_upper, blank, arrived))
    own_part = own_part.at[height * columns - columns :].add(jnp.where(is_upper, arrived, blank))
    return (own_part, kernel_grad)


def attend(queries, key_rows, value_rows, head_count):
    q_heads = queries.reshape(queries.shape[0], head_count, DH)
    k_heads = key_rows.reshape(key_rows.shape[0], head_count, DH)
    v_heads = value_rows.reshape(value_rows.shape[0], head_count, DH)
    scores = jnp.einsum("qhd,khd->hqk", q_heads, k_heads, preferred_element_type=jnp.float32) * (
        1.0 / math.sqrt(DH)
    )
    peak = jnp.max(scores, axis=-1, keepdims=True)
    expd = jnp.exp(scores - peak)
    total_sum = jnp.sum(expd, axis=-1, keepdims=True)
    weights = (expd / total_sum).astype(jnp.bfloat16)
    joined = jnp.einsum("hqk,khd->qhd", weights, v_heads, preferred_element_type=jnp.float32)
    return (joined.reshape(queries.shape[0], -1).astype(jnp.bfloat16), peak + jnp.log(total_sum))


def attend_back(grad_out, queries, key_rows, value_rows, log_total, head_count):
    scaling = 1.0 / math.sqrt(DH)
    q_heads = queries.reshape(queries.shape[0], head_count, DH)
    k_heads = key_rows.reshape(key_rows.shape[0], head_count, DH)
    v_heads = value_rows.reshape(value_rows.shape[0], head_count, DH)
    g_heads = grad_out.reshape(grad_out.shape[0], head_count, DH)
    scores = (
        jnp.einsum("qhd,khd->hqk", q_heads, k_heads, preferred_element_type=jnp.float32) * scaling
    )
    probs = jnp.exp(scores - log_total)
    grad_probs = jnp.einsum("qhd,khd->hqk", g_heads, v_heads, preferred_element_type=jnp.float32)
    grad_scores = (
        probs * (grad_probs - jnp.sum(probs * grad_probs, axis=-1, keepdims=True))
    ).astype(jnp.bfloat16)
    grad_query = (
        jnp.einsum("hqk,khd->qhd", grad_scores, k_heads, preferred_element_type=jnp.float32)
        * scaling
    )
    grad_keys = (
        jnp.einsum("hqk,qhd->khd", grad_scores, q_heads, preferred_element_type=jnp.float32)
        * scaling
    )
    grad_values = jnp.einsum(
        "hqk,qhd->khd", probs.astype(jnp.bfloat16), g_heads, preferred_element_type=jnp.float32
    )
    return (
        grad_query.reshape(queries.shape[0], -1),
        grad_keys.reshape(key_rows.shape[0], -1),
        grad_values.reshape(value_rows.shape[0], -1),
    )


def on_device(
    latents,
    text,
    step_count,
    time_index,
    conv1_w,
    conv2_w,
    time_w,
    proj_in_w,
    qkv_w,
    self_out_w,
    cross_q_w,
    cross_kv_w,
    cross_out_w,
    ff_in_w,
    ff_out_w,
    proj_out_w,
    gn_params,
    ln_params,
    biases,
    ff_bias,
    cotangent,
):
    row_index = lax.axis_index("rows")
    is_upper = row_index % 2 == 0
    image_index = row_index // 2
    height = latents.shape[1]
    columns = latents.shape[2]
    local_width = latents.shape[3]
    tokens = height * columns
    head_count = local_width // DH
    sharded = (
        conv1_w,
        conv2_w,
        time_w,
        proj_in_w,
        qkv_w,
        self_out_w,
        cross_q_w,
        cross_kv_w,
        cross_out_w,
        ff_in_w,
        ff_out_w,
        proj_out_w,
    )
    gathered = (
        lax.all_gather(sharded[0], "rows", axis=2, tiled=True),
        lax.all_gather(sharded[1], "rows", axis=2, tiled=True),
        lax.all_gather(sharded[2], "rows", axis=0, tiled=True),
        lax.all_gather(sharded[3], "rows", axis=0, tiled=True),
        lax.all_gather(sharded[4], "rows", axis=0, tiled=True),
        lax.all_gather(sharded[5], "rows", axis=1, tiled=True),
        lax.all_gather(sharded[6], "rows", axis=0, tiled=True),
        lax.all_gather(sharded[7], "rows", axis=0, tiled=True),
        lax.all_gather(sharded[8], "rows", axis=1, tiled=True),
        lax.all_gather(sharded[9], "rows", axis=0, tiled=True),
        lax.all_gather(sharded[10], "rows", axis=1, tiled=True),
        lax.all_gather(sharded[11], "rows", axis=0, tiled=True),
    )
    (
        conv_one,
        conv_two,
        time_full,
        in_full,
        qkv_full,
        out_self,
        cross_query_w,
        cross_pair,
        cross_out,
        ff_wide,
        ff_narrow,
        out_full,
    ) = gathered
    steps_here = lax.dynamic_index_in_dim(step_count, image_index, 0, keepdims=False)
    stamp_here = lax.dynamic_index_in_dim(time_index, image_index, 0, keepdims=False)
    moment = (999 - 1000 * stamp_here // steps_here).astype(jnp.float32)
    half_width = C // 2
    frequency = jnp.exp(
        -math.log(10000.0) * jnp.arange(half_width).astype(jnp.float32) / half_width
    )
    embedding = jnp.concatenate([jnp.cos(moment * frequency), jnp.sin(moment * frequency)])
    temb_low = jax.nn.silu(embedding).astype(jnp.bfloat16)
    shift_time = (
        jnp.dot(temb_low[None, :], time_full, preferred_element_type=jnp.float32)[0] + biases[1]
    )
    source = latents.reshape(tokens, local_width).astype(jnp.float32)
    normed_one, stored_one = group_forward(source, gn_params[0], EPS_RES)
    act_one = jax.nn.silu(normed_one).astype(jnp.bfloat16)
    conv_sum_one, padded_one = conv_forward(act_one, conv_one, is_upper, height, columns)
    hidden_two = conv_sum_one + biases[0] + shift_time
    normed_two, stored_two = group_forward(hidden_two, gn_params[1], EPS_RES)
    act_two = jax.nn.silu(normed_two).astype(jnp.bfloat16)
    conv_sum_two, padded_two = conv_forward(act_two, conv_two, is_upper, height, columns)
    resid = source + (conv_sum_two + biases[2])
    normed_three, stored_three = group_forward(resid, gn_params[2], EPS_MID)
    gin_full = full_channels(normed_three.astype(jnp.bfloat16))
    stream_zero = jnp.dot(gin_full, in_full, preferred_element_type=jnp.float32) + biases[3]
    ln_one, stored_ln_one = layer_forward(stream_zero, ln_params[0])
    norm_full_one = full_channels(ln_one.astype(jnp.bfloat16))
    qkv_rows = jnp.einsum(
        "tc,cjd->tjd", norm_full_one, qkv_full, preferred_element_type=jnp.float32
    ).astype(jnp.bfloat16)
    queries = qkv_rows[:, 0]
    keys_own = qkv_rows[:, 1]
    values_own = qkv_rows[:, 2]
    keys_far, values_far = swapped((keys_own, values_own), "rows", 0)
    keys_all = jnp.concatenate([keys_own, keys_far], axis=0)
    values_all = jnp.concatenate([values_own, values_far], axis=0)
    attended, log_self = attend(queries, keys_all, values_all, head_count)
    stream_one = stream_zero + (
        channel_total(jnp.dot(attended, out_self, preferred_element_type=jnp.float32)) + biases[4]
    )
    ln_two, stored_ln_two = layer_forward(stream_one, ln_params[1])
    norm_full_two = full_channels(ln_two.astype(jnp.bfloat16))
    cross_query = jnp.dot(norm_full_two, cross_query_w, preferred_element_type=jnp.float32).astype(
        jnp.bfloat16
    )
    prompt = lax.dynamic_index_in_dim(text, image_index, 0, keepdims=False)
    cross_kv = jnp.einsum(
        "sc,cjd->sjd", prompt, cross_pair, preferred_element_type=jnp.float32
    ).astype(jnp.bfloat16)
    cross_att, log_cross = attend(cross_query, cross_kv[:, 0], cross_kv[:, 1], head_count)
    stream_two = stream_one + (
        channel_total(jnp.dot(cross_att, cross_out, preferred_element_type=jnp.float32)) + biases[5]
    )
    ln_three, stored_ln_three = layer_forward(stream_two, ln_params[2])
    norm_full_three = full_channels(ln_three.astype(jnp.bfloat16))
    gate_up = (
        jnp.einsum("tc,cjf->tjf", norm_full_three, ff_wide, preferred_element_type=jnp.float32)
        + ff_bias
    )
    gate_in = gate_up[:, 1]
    cdf_val = 0.5 * (1.0 + lax.erf(gate_in / math.sqrt(2.0)))
    gelu_val = gate_in * cdf_val
    mixed = (gate_up[:, 0] * gelu_val).astype(jnp.bfloat16)
    stream_three = stream_two + (
        channel_total(jnp.dot(mixed, ff_narrow, preferred_element_type=jnp.float32)) + biases[6]
    )
    three_full = full_channels(stream_three.astype(jnp.bfloat16))
    result = resid + (jnp.dot(three_full, out_full, preferred_element_type=jnp.float32) + biases[7])
    output = result.astype(jnp.bfloat16).reshape(latents.shape)
    weights_now = (
        lax.all_gather(sharded[0], "rows", axis=2, tiled=True),
        lax.all_gather(sharded[1], "rows", axis=2, tiled=True),
        lax.all_gather(sharded[2], "rows", axis=0, tiled=True),
        lax.all_gather(sharded[3], "rows", axis=0, tiled=True),
        lax.all_gather(sharded[4], "rows", axis=0, tiled=True),
        lax.all_gather(sharded[5], "rows", axis=1, tiled=True),
        lax.all_gather(sharded[6], "rows", axis=0, tiled=True),
        lax.all_gather(sharded[7], "rows", axis=0, tiled=True),
        lax.all_gather(sharded[8], "rows", axis=1, tiled=True),
        lax.all_gather(sharded[9], "rows", axis=0, tiled=True),
        lax.all_gather(sharded[10], "rows", axis=1, tiled=True),
        lax.all_gather(sharded[11], "rows", axis=0, tiled=True),
    )
    (
        conv_one,
        conv_two,
        time_full,
        in_full,
        qkv_full,
        out_self,
        cross_query_w,
        cross_pair,
        cross_out,
        ff_wide,
        ff_narrow,
        out_full,
    ) = weights_now
    grad_out = cotangent.reshape(tokens, local_width)
    out_full_grad = lax.dot_general(
        three_full, grad_out, CONTRACT_ROWS, preferred_element_type=jnp.float32
    )
    bias_seven = jnp.sum(grad_out.astype(jnp.float32), axis=0)
    grad_three = channel_total(
        lax.dot_general(grad_out, out_full, CONTRACT_LAST, preferred_element_type=jnp.float32)
    )
    grad_ff = grad_three.astype(jnp.bfloat16)
    grad_ff_full = full_channels(grad_ff)
    narrow_grad = lax.dot_general(
        mixed, grad_ff_full, CONTRACT_ROWS, preferred_element_type=jnp.float32
    )
    bias_six = jnp.sum(grad_ff.astype(jnp.float32), axis=0)
    grad_mixed = (
        lax.dot_general(grad_ff_full, ff_narrow, CONTRACT_LAST, preferred_element_type=jnp.float32)
        .astype(jnp.bfloat16)
        .astype(jnp.float32)
    )
    pdf_val = jnp.exp(-0.5 * gate_in * gate_in) / math.sqrt(2.0 * math.pi)
    grad_value_part = grad_mixed * gelu_val
    grad_gate_part = grad_mixed * gate_up[:, 0] * (cdf_val + gate_in * pdf_val)
    grad_gate_up = jnp.stack([grad_value_part, grad_gate_part], axis=1).astype(jnp.bfloat16)
    ffbias_grad = jnp.sum(grad_gate_up.astype(jnp.float32), axis=0)
    wide_grad = jnp.einsum(
        "tc,tjf->cjf", norm_full_three, grad_gate_up, preferred_element_type=jnp.float32
    )
    grad_ln_three = channel_total(
        jnp.einsum("tjf,cjf->tc", grad_gate_up, ff_wide, preferred_element_type=jnp.float32)
    )
    back_three, ln_grad_three = layer_backward(grad_ln_three, ln_params[2], stored_ln_three)
    grad_two = grad_three + back_three
    grad_cross = grad_two.astype(jnp.bfloat16)
    grad_cross_full = full_channels(grad_cross)
    cross_out_grad = lax.dot_general(
        cross_att, grad_cross_full, CONTRACT_ROWS, preferred_element_type=jnp.float32
    )
    bias_five = jnp.sum(grad_cross.astype(jnp.float32), axis=0)
    grad_cross_att = lax.dot_general(
        grad_cross_full, cross_out, CONTRACT_LAST, preferred_element_type=jnp.float32
    ).astype(jnp.bfloat16)
    grad_cq, grad_ck, grad_cv = attend_back(
        grad_cross_att, cross_query, cross_kv[:, 0], cross_kv[:, 1], log_cross, head_count
    )
    grad_cq = grad_cq.astype(jnp.bfloat16)
    grad_ckv = jnp.stack([grad_ck, grad_cv], axis=1).astype(jnp.bfloat16)
    cross_query_grad = lax.dot_general(
        norm_full_two, grad_cq, CONTRACT_ROWS, preferred_element_type=jnp.float32
    )
    cross_pair_grad = jnp.einsum(
        "sc,sjd->cjd", prompt, grad_ckv, preferred_element_type=jnp.float32
    )
    grad_ln_two = channel_total(
        lax.dot_general(grad_cq, cross_query_w, CONTRACT_LAST, preferred_element_type=jnp.float32)
    )
    back_two, ln_grad_two = layer_backward(grad_ln_two, ln_params[1], stored_ln_two)
    grad_one = grad_two + back_two
    grad_self = grad_one.astype(jnp.bfloat16)
    grad_self_full = full_channels(grad_self)
    out_self_grad = lax.dot_general(
        attended, grad_self_full, CONTRACT_ROWS, preferred_element_type=jnp.float32
    )
    bias_four = jnp.sum(grad_self.astype(jnp.float32), axis=0)
    grad_attended = lax.dot_general(
        grad_self_full, out_self, CONTRACT_LAST, preferred_element_type=jnp.float32
    ).astype(jnp.bfloat16)
    grad_q, grad_k, grad_v = attend_back(
        grad_attended, queries, keys_all, values_all, log_self, head_count
    )
    far_k, far_v = (
        swapped(grad_k[tokens:].astype(jnp.bfloat16), "rows", 0).astype(jnp.float32),
        swapped(grad_v[tokens:].astype(jnp.bfloat16), "rows", 0).astype(jnp.float32),
    )
    grad_qkv = jnp.stack([grad_q, grad_k[:tokens] + far_k, grad_v[:tokens] + far_v], axis=1).astype(
        jnp.bfloat16
    )
    qkv_grad = jnp.einsum(
        "tc,tjd->cjd", norm_full_one, grad_qkv, preferred_element_type=jnp.float32
    )
    grad_ln_one = channel_total(
        jnp.einsum("tjd,cjd->tc", grad_qkv, qkv_full, preferred_element_type=jnp.float32)
    )
    back_one, ln_grad_one = layer_backward(grad_ln_one, ln_params[0], stored_ln_one)
    grad_zero = (grad_one + back_one).astype(jnp.bfloat16)
    in_grad = lax.dot_general(
        gin_full, grad_zero, CONTRACT_ROWS, preferred_element_type=jnp.float32
    )
    bias_three = jnp.sum(grad_zero.astype(jnp.float32), axis=0)
    grad_gin = channel_total(
        lax.dot_general(grad_zero, in_full, CONTRACT_LAST, preferred_element_type=jnp.float32)
    )
    back_gn_three, gn_grad_three = group_backward(grad_gin, gn_params[2], stored_three)
    grad_resid = grad_out.astype(jnp.float32) + back_gn_three
    grad_c_two = grad_resid.astype(jnp.bfloat16)
    bias_two = jnp.sum(grad_c_two.astype(jnp.float32), axis=0)
    grad_act_two, conv_two_grad = conv_backward(
        grad_c_two, padded_two, conv_two, is_upper, height, columns
    )
    grad_hidden, gn_grad_two = group_backward(
        grad_act_two * silu_slope(normed_two), gn_params[1], stored_two
    )
    image_sum = jnp.sum(grad_hidden, axis=0)
    time_grad = temb_low.astype(jnp.float32)[:, None] * image_sum[None, :]
    grad_c_one = grad_hidden.astype(jnp.bfloat16)
    bias_zero = jnp.sum(grad_c_one.astype(jnp.float32), axis=0)
    grad_act_one, conv_one_grad = conv_backward(
        grad_c_one, padded_one, conv_one, is_upper, height, columns
    )
    back_gn_one, gn_grad_one = group_backward(
        grad_act_one * silu_slope(normed_one), gn_params[0], stored_one
    )
    latents_grad = (grad_resid + back_gn_one).reshape(latents.shape)
    local_grads = (
        conv_one_grad,
        conv_two_grad,
        time_grad,
        in_grad,
        qkv_grad,
        out_self_grad,
        cross_query_grad,
        cross_pair_grad,
        cross_out_grad,
        wide_grad,
        narrow_grad,
        out_full_grad,
    )
    weight_sums = (
        lax.psum_scatter(local_grads[0], "rows", scatter_dimension=2, tiled=True),
        lax.psum_scatter(local_grads[1], "rows", scatter_dimension=2, tiled=True),
        lax.psum_scatter(local_grads[2], "rows", scatter_dimension=0, tiled=True),
        lax.psum_scatter(local_grads[3], "rows", scatter_dimension=0, tiled=True),
        lax.psum_scatter(local_grads[4], "rows", scatter_dimension=0, tiled=True),
        lax.psum_scatter(local_grads[5], "rows", scatter_dimension=1, tiled=True),
        lax.psum_scatter(local_grads[6], "rows", scatter_dimension=0, tiled=True),
        lax.psum_scatter(local_grads[7], "rows", scatter_dimension=0, tiled=True),
        lax.psum_scatter(local_grads[8], "rows", scatter_dimension=1, tiled=True),
        lax.psum_scatter(local_grads[9], "rows", scatter_dimension=0, tiled=True),
        lax.psum_scatter(local_grads[10], "rows", scatter_dimension=1, tiled=True),
        lax.psum_scatter(local_grads[11], "rows", scatter_dimension=0, tiled=True),
    )
    gn_stack = jnp.stack([gn_grad_one, gn_grad_two, gn_grad_three])
    ln_stack = jnp.stack([ln_grad_one, ln_grad_two, ln_grad_three])
    bias_stack = jnp.stack(
        [bias_zero, image_sum, bias_two, bias_three, bias_four, bias_five, bias_six, bias_seven]
    )
    gn_total, ln_total, bias_total, ffbias_total = lax.psum(
        (gn_stack, ln_stack, bias_stack, ffbias_grad), "rows"
    )
    return (
        output,
        latents_grad,
        weight_sums[0],
        weight_sums[1],
        weight_sums[2],
        weight_sums[3],
        weight_sums[4],
        weight_sums[5],
        weight_sums[6],
        weight_sums[7],
        weight_sums[8],
        weight_sums[9],
        weight_sums[10],
        weight_sums[11],
        gn_total,
        ln_total,
        bias_total,
        ffbias_total,
    )


def solution(mesh):
    return jax.shard_map(
        on_device,
        mesh=mesh,
        in_specs=(
            P("rows", None, None, "heads"),
            P(),
            P(),
            P(),
            P(None, None, "rows", "heads"),
            P(None, None, "rows", "heads"),
            P("rows", "heads"),
            P("rows", "heads"),
            P("rows", None, "heads"),
            P("heads", "rows"),
            P("rows", "heads"),
            P("rows", None, "heads"),
            P("heads", "rows"),
            P("rows", None, "heads"),
            P("heads", "rows"),
            P("rows", "heads"),
            P(None, None, "heads"),
            P(None, None, "heads"),
            P(None, "heads"),
            P(None, "heads"),
            P("rows", None, None, "heads"),
        ),
        out_specs=(
            P("rows", None, None, "heads"),
            P("rows", None, None, "heads"),
            P(None, None, "rows", "heads"),
            P(None, None, "rows", "heads"),
            P("rows", "heads"),
            P("rows", "heads"),
            P("rows", None, "heads"),
            P("heads", "rows"),
            P("rows", "heads"),
            P("rows", None, "heads"),
            P("heads", "rows"),
            P("rows", None, "heads"),
            P("heads", "rows"),
            P("rows", "heads"),
            P(None, None, "heads"),
            P(None, None, "heads"),
            P(None, "heads"),
            P(None, "heads"),
        ),
        check_vma=False,
    )
```

profile of v0, /device:TPU:0, one launch (start us, length us, event | category | flops | bytes accessed | tf_op | source)
XLA Modules:
  0.0 4113.2 jit_solution(15662797828497282531)
XLA Ops:
  27.6 33.4 all_gather.78
  74.8 101.6 %all-gather.19.cloned.1.call-done = bf16[3,3,1280,320]{3,2,1,0:T(8,128)(2,1)} async-done(((bf16[3,3,160,320]{3,2,1,0:T(8,128)(2,1)}), bf16[3,3,1280,320]{3,2,1,0:T(8,128)(2,1)}) %all-gather.19.cloned.1.call-update) | async-done | bytes 7372816 | tf_op jit(solution)/shard_map/all_gather | solution.py:255
  233.1 120.0 %all-gather.23.cloned.1.call-done = bf16[3,3,1280,320]{3,2,1,0:T(8,128)(2,1)} async-done(((bf16[3,3,160,320]{3,2,1,0:T(8,128)(2,1)}), bf16[3,3,1280,320]{3,2,1,0:T(8,128)(2,1)}) %all-gather.23.cloned.1.call-update) | async-done | bytes 7372816 | tf_op jit(solution)/shard_map/all_gather | solution.py:256
  374.2 35.2 all_gather.82
  419.4 32.1 all-gather.29.cloned.1.call-done
  476.0 36.9 all_gather.85
  525.9 25.6 reduce-scatter.23.cloned.1.call-done
  559.5 35.1 all_gather.94
  598.2 36.3 all_gather.88
  634.5 34.5 all_gather.89
  690.5 26.1 reduce-scatter.25.cloned.1.call-done
  736.5 64.3 %all-gather.39.cloned.1.call-done = bf16[1280,1280]{0,1:T(8,128)(2,1)} async-done(((bf16[1280,160]{0,1:T(8,128)(2,1)}), bf16[1280,1280]{0,1:T(8,128)(2,1)}) %all-gather.39.cloned.1.call-update) | async-done | bytes 3276816 | tf_op jit(solution)/shard_map/all_gather | solution.py:265
  806.1 98.4 %all-gather.37.cloned.1.call-done = bf16[1280,2,1280]{2,0,1:T(8,128)(2,1)} async-done(((bf16[160,2,1280]{2,0,1:T(8,128)(2,1)}), bf16[1280,2,1280]{2,0,1:T(8,128)(2,1)}) %all-gather.37.cloned.1.call-update) | async-done | bytes 6553616 | tf_op jit(solution)/shard_map/all_gather | solution.py:264
  938.1 26.6 reduce-scatter.31.cloned.1.call-done
  1007.1 21.0 reduce-scatter.33.cloned.1.call-done
  1035.7 21.5 reduce-scatter.27.cloned.1.call-done
  1113.0 26.7 reduce-scatter.35.cloned.1.call-done
  1153.8 25.7 reduce-scatter.37.cloned.1.call-done
  1216.0 68.8 %scatter-add.75 = f32[18,34,1280]{1,2,0:T(8,128)} dynamic-update-slice(f32[18,34,1280]{1,2,0:T(8,128)} %scatter-add.74, f32[16,32,1280]{1,2,0:T(8,128)} %dynamic-slice_add_fusion.1, s32[]{:T(128)} %bitcast.85, s32[]{:T(128)} %bitcast.86, s32[]{:T(128)} %constant.649.clone.1) | dynamic-update-slice | bytes 5242884 | tf_op jit(solution)/shard_map/scatter-add | solution.py:145
  1295.0 68.8 %scatter-add.76 = f32[18,34,1280]{1,2,0:T(8,128)} dynamic-update-slice(f32[18,34,1280]{1,2,0:T(8,128)} %scatter-add.75, f32[16,32,1280]{1,2,0:T(8,128)} %add_select_fusion.1, s32[]{:T(128)} %bitcast.88, s32[]{:T(128)} %bitcast.89, s32[]{:T(128)} %constant.649.clone.1) | dynamic-update-slice | bytes 5242884 | tf_op jit(solution)/shard_map/scatter-add | solution.py:145
  1372.1 57.7 %scatter-add.79 = f32[18,34,1280]{1,2,0:T(8,128)} dynamic-update-slice(f32[18,34,1280]{1,2,0:T(8,128)} %scatter-add.76, f32[16,32,1280]{1,2,0:T(8,128)} %slice_add_fusion.11, s32[]{:T(128)} %constant.650.clone.1, s32[]{:T(128)} %constant.649.clone.1, s32[]{:T(128)} %constant.649.clone.1) | dynamic-update-slice | bytes 5242884 | tf_op jit(solution)/shard_map/scatter-add | solution.py:145
  1438.0 67.5 %scatter-add.80 = f32[18,34,1280]{1,2,0:T(8,128)} dynamic-update-slice(f32[18,34,1280]{1,2,0:T(8,128)} %scatter-add.79, f32[16,32,1280]{1,2,0:T(8,128)} %slice_add_fusion.10, s32[]{:T(128)} %constant.650.clone.1, s32[]{:T(128)} %constant.650.clone.1, s32[]{:T(128)} %constant.649.clone.1) | dynamic-update-slice | bytes 5242884 | tf_op jit(solution)/shard_map/scatter-add | solution.py:145
  1513.8 67.5 %scatter-add.81 = f32[18,34,1280]{1,2,0:T(8,128)} dynamic-update-slice(f32[18,34,1280]{1,2,0:T(8,128)} %scatter-add.80, f32[16,32,1280]{1,2,0:T(8,128)} %slice_add_fusion.9, s32[]{:T(128)} %constant.650.clone.1, s32[]{:T(128)} %constant.651.clone.1, s32[]{:T(128)} %constant.649.clone.1) | dynamic-update-slice | bytes 5242884 | tf_op jit(solution)/shard_map/scatter-add | solution.py:145
  1589.7 57.7 %scatter-add.84 = f32[18,34,1280]{1,2,0:T(8,128)} dynamic-update-slice(f32[18,34,1280]{1,2,0:T(8,128)} %scatter-add.81, f32[16,32,1280]{1,2,0:T(8,128)} %slice_add_fusion.8, s32[]{:T(128)} %constant.651.clone.1, s32[]{:T(128)} %constant.649.clone.1, s32[]{:T(128)} %constant.649.clone.1) | dynamic-update-slice | bytes 5242884 | tf_op jit(solution)/shard_map/scatter-add | solution.py:145
  1655.6 67.5 %scatter-add.85 = f32[18,34,1280]{1,2,0:T(8,128)} dynamic-update-slice(f32[18,34,1280]{1,2,0:T(8,128)} %scatter-add.84, f32[16,32,1280]{1,2,0:T(8,128)} %slice_add_fusion.7, s32[]{:T(128)} %constant.651.clone.1, s32[]{:T(128)} %constant.650.clone.1, s32[]{:T(128)} %constant.649.clone.1) | dynamic-update-slice | bytes 5242884 | tf_op jit(solution)/shard_map/scatter-add | solution.py:145
  1731.4 67.5 %scatter-add.86 = f32[18,34,1280]{1,2,0:T(8,128)} dynamic-update-slice(f32[18,34,1280]{1,2,0:T(8,128)} %scatter-add.85, f32[16,32,1280]{1,2,0:T(8,128)} %slice_add_fusion.6, s32[]{:T(128)} %constant.651.clone.1, s32[]{:T(128)} %constant.651.clone.1, s32[]{:T(128)} %constant.649.clone.1) | dynamic-update-slice | bytes 5242884 | tf_op jit(solution)/shard_map/scatter-add | solution.py:145
  1817.0 27.7 reduce-scatter.39.cloned.1.call-done
  1887.5 68.8 %scatter-add.94 = f32[18,34,1280]{1,2,0:T(8,128)} dynamic-update-slice(f32[18,34,1280]{1,2,0:T(8,128)} %scatter-add.91, f32[16,32,1280]{1,2,0:T(8,128)} %dynamic-slice_add_fusion, s32[]{:T(128)} %bitcast.85, s32[]{:T(128)} %bitcast.86, s32[]{:T(128)} %constant.649.clone.1) | dynamic-update-slice | bytes 5242884 | tf_op jit(solution)/shard_map/scatter-add | solution.py:145
  1966.5 68.8 %scatter-add.95 = f32[18,34,1280]{1,2,0:T(8,128)} dynamic-update-slice(f32[18,34,1280]{1,2,0:T(8,128)} %scatter-add.94, f32[16,32,1280]{1,2,0:T(8,128)} %add_select_fusion, s32[]{:T(128)} %bitcast.88, s32[]{:T(128)} %bitcast.89, s32[]{:T(128)} %constant.649.clone.1) | dynamic-update-slice | bytes 5242884 | tf_op jit(solution)/shard_map/scatter-add | solution.py:145
  2043.5 57.7 %scatter-add.96 = f32[18,34,1280]{1,2,0:T(8,128)} dynamic-update-slice(f32[18,34,1280]{1,2,0:T(8,128)} %scatter-add.95, f32[16,32,1280]{1,2,0:T(8,128)} %slice_add_fusion.5, s32[]{:T(128)} %constant.650.clone.1, s32[]{:T(128)} %constant.649.clone.1, s32[]{:T(128)} %constant.649.clone.1) | dynamic-update-slice | bytes 5242884 | tf_op jit(solution)/shard_map/scatter-add | solution.py:145
  2109.4 67.5 %scatter-add.99 = f32[18,34,1280]{1,2,0:T(8,128)} dynamic-update-slice(f32[18,34,1280]{1,2,0:T(8,128)} %scatter-add.96, f32[16,32,1280]{1,2,0:T(8,128)} %slice_add_fusion.4, s32[]{:T(128)} %constant.650.clone.1, s32[]{:T(128)} %constant.650.clone.1, s32[]{:T(128)} %constant.649.clone.1) | dynamic-update-slice | bytes 5242884 | tf_op jit(solution)/shard_map/scatter-add | solution.py:145
  2185.6 67.5 %scatter-add.100 = f32[18,34,1280]{1,2,0:T(8,128)} dynamic-update-slice(f32[18,34,1280]{1,2,0:T(8,128)} %scatter-add.99, f32[16,32,1280]{1,2,0:T(8,128)} %slice_add_fusion.3, s32[]{:T(128)} %constant.650.clone.1, s32[]{:T(128)} %constant.651.clone.1, s32[]{:T(128)} %constant.649.clone.1) | dynamic-update-slice | bytes 5242884 | tf_op jit(solution)/shard_map/scatter-add | solution.py:145
  2261.4 57.7 %scatter-add.101 = f32[18,34,1280]{1,2,0:T(8,128)} dynamic-update-slice(f32[18,34,1280]{1,2,0:T(8,128)} %scatter-add.100, f32[16,32,1280]{1,2,0:T(8,128)} %slice_add_fusion.2, s32[]{:T(128)} %constant.651.clone.1, s32[]{:T(128)} %constant.649.clone.1, s32[]{:T(128)} %constant.649.clone.1) | dynamic-update-slice | bytes 5242884 | tf_op jit(solution)/shard_map/scatter-add | solution.py:145
  2327.3 67.5 %scatter-add.104 = f32[18,34,1280]{1,2,0:T(8,128)} dynamic-update-slice(f32[18,34,1280]{1,2,0:T(8,128)} %scatter-add.101, f32[16,32,1280]{1,2,0:T(8,128)} %slice_add_fusion.1, s32[]{:T(128)} %constant.651.clone.1, s32[]{:T(128)} %constant.650.clone.1, s32[]{:T(128)} %constant.649.clone.1) | dynamic-update-slice | bytes 5242884 | tf_op jit(solution)/shard_map/scatter-add | solution.py:145
  2403.1 67.5 %scatter-add.105 = f32[18,34,1280]{1,2,0:T(8,128)} dynamic-update-slice(f32[18,34,1280]{1,2,0:T(8,128)} %scatter-add.104, f32[16,32,1280]{1,2,0:T(8,128)} %slice_add_fusion, s32[]{:T(128)} %constant.651.clone.1, s32[]{:T(128)} %constant.651.clone.1, s32[]{:T(128)} %constant.649.clone.1) | dynamic-update-slice | bytes 5242884 | tf_op jit(solution)/shard_map/scatter-add | solution.py:145
  2618.1 39.4 all-reduce.4
  2660.5 75.7 %reduce-scatter.61.cloned.1.call-done = f32[160,2,1280]{2,0,1:T(8,128)} async-done(((f32[1280,2,1280]{2,0,1:T(8,128)}), f32[160,2,1280]{2,0,1:T(8,128)}) %reduce-scatter.61.cloned.1.call-update) | async-done | bytes 1638416 | tf_op jit(solution)/shard_map/reduce_scatter | solution.py:514
  2740.0 66.1 %reduce-scatter.59.cloned.1.call-done = f32[320,160]{0,1:T(8,128)} async-done(((f32[320,1280]{0,1:T(8,128)}), f32[320,160]{0,1:T(8,128)}) %reduce-scatter.59.cloned.1.call-update) | async-done | bytes 204816 | tf_op jit(solution)/shard_map/reduce_scatter | solution.py:513
  2806.2 70.2 %reduce-scatter.55.cloned.1.call-done = f32[160,320]{1,0:T(8,128)} async-done(((f32[1280,320]{1,0:T(8,128)}), f32[160,320]{1,0:T(8,128)}) %reduce-scatter.55.cloned.1.call-update) | async-done | bytes 204816 | tf_op jit(solution)/shard_map/reduce_scatter | solution.py:511
  2876.4 69.7 %reduce-scatter.53.cloned.1.call-done = f32[320,160]{0,1:T(8,128)} async-done(((f32[320,1280]{0,1:T(8,128)}), f32[320,160]{0,1:T(8,128)}) %reduce-scatter.53.cloned.1.call-update) | async-done | bytes 204816 | tf_op jit(solution)/shard_map/reduce_scatter | solution.py:510
  2946.2 70.2 %reduce-scatter.65.cloned.1.call-done = f32[160,320]{1,0:T(8,128)} async-done(((f32[1280,320]{1,0:T(8,128)}), f32[160,320]{1,0:T(8,128)}) %reduce-scatter.65.cloned.1.call-update) | async-done | bytes 204816 | tf_op jit(solution)/shard_map/reduce_scatter | solution.py:516
  3016.4 124.8 %reduce-scatter.63.cloned.1.call-done = f32[1280,160]{0,1:T(8,128)} async-done(((f32[1280,1280]{0,1:T(8,128)}), f32[1280,160]{0,1:T(8,128)}) %reduce-scatter.63.cloned.1.call-update) | async-done | bytes 819216 | tf_op jit(solution)/shard_map/reduce_scatter | solution.py:515
  3141.2 106.6 %reduce-scatter.57.cloned.1.call-done = f32[256,2,320]{0,2,1:T(8,128)} async-done(((f32[2048,2,320]{0,2,1:T(8,128)}), f32[256,2,320]{0,2,1:T(8,128)}) %reduce-scatter.57.cloned.1.call-update) | async-done | bytes 655376 | tf_op jit(solution)/shard_map/reduce_scatter | solution.py:512
  3247.8 70.9 %reduce-scatter.49.cloned.1.call-done = f32[160,320]{1,0:T(8,128)} async-done(((f32[1280,320]{1,0:T(8,128)}), f32[160,320]{1,0:T(8,128)}) %reduce-scatter.49.cloned.1.call-update) | async-done | bytes 204816 | tf_op jit(solution)/shard_map/reduce_scatter | solution.py:508
  3318.8 115.0 %reduce-scatter.51.cloned.1.call-done = f32[160,3,320]{2,0,1:T(8,128)} async-done(((f32[1280,3,320]{2,0,1:T(8,128)}), f32[160,3,320]{2,0,1:T(8,128)}) %reduce-scatter.51.cloned.1.call-update) | async-done | bytes 614416 | tf_op jit(solution)/shard_map/reduce_scatter | solution.py:509
  3433.7 70.6 %reduce-scatter.47.cloned.1.call-done = f32[160,320]{1,0:T(8,128)} async-done(((f32[1280,320]{1,0:T(8,128)}), f32[160,320]{1,0:T(8,128)}) %reduce-scatter.47.cloned.1.call-update) | async-done | bytes 204816 | tf_op jit(solution)/shard_map/reduce_scatter | solution.py:507
  3504.3 301.1 %reduce-scatter.45.cloned.1.call-done = f32[3,3,160,320]{3,2,1,0:T(8,128)} async-done(((f32[3,3,1280,320]{3,2,1,0:T(8,128)}), f32[3,3,160,320]{3,2,1,0:T(8,128)}) %reduce-scatter.45.cloned.1.call-update) | async-done | bytes 1843216 | tf_op jit(solution)/shard_map/reduce_scatter | solution.py:506
  3805.4 300.9 %reduce-scatter.43.cloned.1.call-done = f32[3,3,160,320]{3,2,1,0:T(8,128)} async-done(((f32[3,3,1280,320]{3,2,1,0:T(8,128)}), f32[3,3,160,320]{3,2,1,0:T(8,128)}) %reduce-scatter.43.cloned.1.call-update) | async-done | bytes 1843216 | tf_op jit(solution)/shard_map/reduce_scatter | solution.py:505
  (835 shorter events, 737.5 us)
Async XLA Ops:
  7.2 54.6 %all-gather.17.cloned.1.call-start = ((), (), s32[]{:S(2)}) async-start(), calls=%async_computation.22 | async-start | bytes 2048000 | tf_op jit(solution)/shard_map/all_gather | solution.py:25
  8.7 5.9 collective-permute-start
  16.3 4.5 collective-permute-start.2
  21.6 154.8 %all-gather.19.cloned.1.call-start = ((), (), s32[]{:S(2)}) async-start(), calls=%async_computation.23 | async-start | bytes 9953280 | tf_op jit(solution)/shard_map/all_gather | solution.py:255
  22.3 197.8 %all-gather.21.cloned.1.call-start = ((), (), s32[]{:S(2)}) async-start(), calls=%async_computation.24 | async-start | bytes 2048000 | tf_op jit(solution)/shard_map/all_gather | solution.py:25
  195.6 4.5 collective-permute-start.5
  200.9 152.2 %all-gather.23.cloned.1.call-start = ((), (), s32[]{:S(2)}) async-start(), calls=%async_computation.25 | async-start | bytes 9953280 | tf_op jit(solution)/shard_map/all_gather | solution.py:256
  201.5 208.0 %all-gather.25.cloned.1.call-start = ((), (), s32[]{:S(2)}) async-start(), calls=%async_computation.26 | async-start | bytes 1638400 | tf_op jit(solution)/shard_map/all_gather | solution.py:25
  373.0 78.6 %all-gather.29.cloned.1.call-start = ((), (), s32[]{:S(2)}) async-start(), calls=%async_computation.28 | async-start | bytes 3317760 | tf_op jit(solution)/shard_map/all_gather | solution.py:259
  373.5 97.0 %all-gather.27.cloned.1.call-start = ((), (), s32[]{:S(2)}) async-start(), calls=%async_computation.27 | async-start | bytes 1638400 | tf_op jit(solution)/shard_map/all_gather | solution.py:25
  419.3 132.2 %reduce-scatter.23.cloned.1.call-start = ((), (), s32[]{:S(2)}) async-start(), calls=%async_computation.29 | async-start | bytes 1638400 | tf_op jit(solution)/shard_map/reduce_scatter | solution.py:29
  474.5 39.4 collective-permute-start.9
  512.9 7.1 collective-permute-start.8
  525.1 144.0 %all-gather.31.cloned.1.call-start = ((), (), s32[]{:S(2)}) async-start(), calls=%async_computation.30 | async-start | bytes 2949120 | tf_op jit(solution)/shard_map/all_gather | solution.py:262
  525.8 147.8 %all-gather.33.cloned.1.call-start = ((), (), s32[]{:S(2)}) async-start(), calls=%async_computation.31 | async-start | bytes 1638400 | tf_op jit(solution)/shard_map/all_gather | solution.py:25
  559.4 128.3 %reduce-scatter.29.cloned.1.call-start = ((), (), s32[]{:S(2)}) async-start(), calls=%async_computation.38 | async-start | bytes 1638400 | tf_op jit(solution)/shard_map/reduce_scatter | solution.py:29
  597.5 119.2 %reduce-scatter.25.cloned.1.call-start = ((), (), s32[]{:S(2)}) async-start(), calls=%async_computation.32 | async-start | bytes 1638400 | tf_op jit(solution)/shard_map/reduce_scatter | solution.py:29
  679.0 57.5 %all-gather.43.cloned.1.call-start = ((), (), s32[]{:S(2)}) async-start(), calls=%async_computation.39 | async-start | bytes 1638400 | tf_op jit(solution)/shard_map/all_gather | solution.py:25
  687.7 113.1 %all-gather.39.cloned.1.call-start = ((), (), s32[]{:S(2)}) async-start(), calls=%async_computation.35 | async-start | bytes 3686400 | tf_op jit(solution)/shard_map/all_gather | solution.py:265
  688.3 216.2 %all-gather.37.cloned.1.call-start = ((), (), s32[]{:S(2)}) async-start(), calls=%async_computation.34 | async-start | bytes 7372800 | tf_op jit(solution)/shard_map/all_gather | solution.py:264
  690.5 232.5 %all-gather.35.cloned.1.call-start = ((), (), s32[]{:S(2)}) async-start(), calls=%async_computation.33 | async-start | bytes 1638400 | tf_op jit(solution)/shard_map/all_gather | solution.py:25
  725.2 239.5 %reduce-scatter.31.cloned.1.call-start = ((), (), s32[]{:S(2)}) async-start(), calls=%async_computation.40 | async-start | bytes 1638400 | tf_op jit(solution)/shard_map/reduce_scatter | solution.py:29
  938.1 57.8 %all-gather.45.cloned.1.call-start = ((), (), s32[]{:S(2)}) async-start(), calls=%async_computation.41 | async-start | bytes 1638400 | tf_op jit(solution)/shard_map/all_gather | solution.py:25
  976.4 51.7 %reduce-scatter.33.cloned.1.call-start = ((), (), s32[]{:S(2)}) async-start(), calls=%async_computation.42 | async-start | bytes 1638400 | tf_op jit(solution)/shard_map/reduce_scatter | solution.py:29
  1001.4 55.8 %reduce-scatter.27.cloned.1.call-start = ((), (), s32[]{:S(2)}) async-start(), calls=%async_computation.36 | async-start | bytes 1638400 | tf_op jit(solution)/shard_map/reduce_scatter | solution.py:29
  1007.1 72.1 %all-gather.47.cloned.1.call-start = ((), (), s32[]{:S(2)}) async-start(), calls=%async_computation.43 | async-start | bytes 1638400 | tf_op jit(solution)/shard_map/all_gather | solution.py:25
  1060.8 78.9 %reduce-scatter.35.cloned.1.call-start = ((), (), s32[]{:S(2)}) async-start(), calls=%async_computation.44 | async-start | bytes 1638400 | tf_op jit(solution)/shard_map/reduce_scatter | solution.py:29
  1092.6 10.6 collective-permute-start.11
  1097.9 11.6 collective-permute-start.10
  1113.0 66.5 %reduce-scatter.37.cloned.1.call-start = ((), (), s32[]{:S(2)}) async-start(), calls=%async_computation.45 | async-start | bytes 1638400 | tf_op jit(solution)/shard_map/reduce_scatter | solution.py:29
  1151.7 693.0 %reduce-scatter.39.cloned.1.call-start = ((), (), s32[]{:S(2)}) async-start(), calls=%async_computation.46 | async-start | bytes 2048000 | tf_op jit(solution)/shard_map/reduce_scatter | solution.py:29
  1816.9 692.8 %all-gather.41.cloned.1.call-start = ((), (), s32[]{:S(2)}) async-start(), calls=%async_computation.37 | async-start | bytes 1638400 | tf_op jit(solution)/shard_map/all_gather | solution.py:25
  1845.6 4.4 collective-permute-start.14
  1847.1 759.9 %reduce-scatter.41.cloned.1.call-start = ((), (), s32[]{:S(2)}) async-start(), calls=%async_computation.47 | async-start | bytes 2048000 | tf_op jit(solution)/shard_map/reduce_scatter | solution.py:29
  2488.6 247.5 %reduce-scatter.61.cloned.1.call-start = ((), (), s32[]{:S(2)}) async-start(), calls=%async_computation.57 | async-start | bytes 14745600 | tf_op jit(solution)/shard_map/reduce_scatter | solution.py:514
  2499.4 306.8 %reduce-scatter.59.cloned.1.call-start = ((), (), s32[]{:S(2)}) async-start(), calls=%async_computation.56 | async-start | bytes 2211840 | tf_op jit(solution)/shard_map/reduce_scatter | solution.py:513
  2503.8 372.6 %reduce-scatter.55.cloned.1.call-start = ((), (), s32[]{:S(2)}) async-start(), calls=%async_computation.54 | async-start | bytes 2211840 | tf_op jit(solution)/shard_map/reduce_scatter | solution.py:511
  2506.1 440.1 %reduce-scatter.53.cloned.1.call-start = ((), (), s32[]{:S(2)}) async-start(), calls=%async_computation.53 | async-start | bytes 2211840 | tf_op jit(solution)/shard_map/reduce_scatter | solution.py:510
  2509.6 506.7 %reduce-scatter.65.cloned.1.call-start = ((), (), s32[]{:S(2)}) async-start(), calls=%async_computation.59 | async-start | bytes 2211840 | tf_op jit(solution)/shard_map/reduce_scatter | solution.py:516
  2513.3 627.9 %reduce-scatter.63.cloned.1.call-start = ((), (), s32[]{:S(2)}) async-start(), calls=%async_computation.58 | async-start | bytes 7372800 | tf_op jit(solution)/shard_map/reduce_scatter | solution.py:515
  2519.4 728.4 %reduce-scatter.57.cloned.1.call-start = ((), (), s32[]{:S(2)}) async-start(), calls=%async_computation.55 | async-start | bytes 5898240 | tf_op jit(solution)/shard_map/reduce_scatter | solution.py:512
  2524.6 794.1 %reduce-scatter.49.cloned.1.call-start = ((), (), s32[]{:S(2)}) async-start(), calls=%async_computation.51 | async-start | bytes 2211840 | tf_op jit(solution)/shard_map/reduce_scatter | solution.py:508
  2528.1 905.6 %reduce-scatter.51.cloned.1.call-start = ((), (), s32[]{:S(2)}) async-start(), calls=%async_computation.52 | async-start | bytes 6635520 | tf_op jit(solution)/shard_map/reduce_scatter | solution.py:509
  2534.1 970.3 %reduce-scatter.47.cloned.1.call-start = ((), (), s32[]{:S(2)}) async-start(), calls=%async_computation.50 | async-start | bytes 2211840 | tf_op jit(solution)/shard_map/reduce_scatter | solution.py:507
  2536.9 1268.5 %reduce-scatter.45.cloned.1.call-start = ((), (), s32[]{:S(2)}) async-start(), calls=%async_computation.49 | async-start | bytes 19906560 | tf_op jit(solution)/shard_map/reduce_scatter | solution.py:506
  2568.8 1537.5 %reduce-scatter.43.cloned.1.call-start = ((), (), s32[]{:S(2)}) async-start(), calls=%async_computation.48 | async-start | bytes 19906560 | tf_op jit(solution)/shard_map/reduce_scatter | solution.py:505
  2616.0 41.5 %collective-permute-start.18 = (f32[8]{0:T(128)S(1)}, f32[8]{0:T(128)S(1)}, u32[]{:S(2)}, u32[]{:S(2)}) collective-permute-start(f32[8]{0:T(128)S(1)} %reduce_sum.573), channel_id=1, source_target_pairs={{0,4},{4,0},{8,12},{12,8},{16,20},{20,16},{24,28},{28,24},{1,5},{5... | collective-permute-start | bytes 104 | tf_op jit(solution)/shard_map/ppermute | solution.py:21
  2616.9 40.7 collective-permute-start.19
  (210 other events, 6317.5 us)
Sparse Core Ops, SparseCore 0:
  21.7 20.8 all-gather.16
  44.8 131.5 all-gather.18
  201.0 19.1 all-gather.20
  222.2 130.8 all-gather.22
  373.1 17.2 all-gather.24
  392.4 59.0 all-gather.28
  453.6 16.8 all-gather.26
  525.2 26.2 reduce-scatter.22
  553.8 84.0 all-gather.30
  639.9 17.9 all-gather.32
  661.1 26.5 reduce-scatter.28
  690.1 26.5 reduce-scatter.24
  718.3 18.1 all-gather.42
  738.8 61.9 all-gather.38
  803.6 100.8 all-gather.36
  906.6 16.3 all-gather.34
  938.2 26.5 reduce-scatter.30
  976.5 19.2 all-gather.44
  1001.5 26.5 reduce-scatter.32
  1030.6 26.5 reduce-scatter.26
  1061.0 18.1 all-gather.46
  1113.1 26.5 reduce-scatter.34
  1151.8 27.7 reduce-scatter.36
  1817.0 27.6 reduce-scatter.38
  1847.2 17.9 all-gather.40
  2488.8 27.6 reduce-scatter.40
  2520.0 216.1 reduce-scatter.60
  2740.2 65.9 reduce-scatter.58
  2810.6 65.7 reduce-scatter.54
  2880.3 65.7 reduce-scatter.52
  2950.6 65.7 reduce-scatter.64
  3020.6 120.5 reduce-scatter.62
  3145.7 102.1 reduce-scatter.56
  3252.3 66.4 reduce-scatter.48
  3323.0 110.6 reduce-scatter.50
  3437.6 66.6 reduce-scatter.46
  3509.2 296.1 reduce-scatter.44
  3809.9 296.3 reduce-scatter.42
where the time goes:
time: 4150 us; the launch traced here: 4110 us
  waiting for transfers between devices  2210 us (53%)
  local copies, waits for them, and re-layouts  1200 us (29%)
  matrix products  303 us (7%)
  blocking collectives  287 us (7%)
  other arithmetic  69.6 us (2%)
    scatter-add x18, local copies, waits for them, and re-layouts, conv_backward(): spread.at[row_shift:row_shift + height, col_shift:col_shift + columns]  1060 us
    reduce_scatter x1, waiting for transfers between devices, on_device(): lax.psum_scatter(local_grads[1], 'rows', scatter_dimension=2, tiled=True)  301 us
    reduce_scatter x1, waiting for transfers between devices, on_device(): lax.psum_scatter(local_grads[0], 'rows', scatter_dimension=2, tiled=True)  301 us
    reduce_scatter x10, waiting for transfers between devices, channel_total(): lax.psum_scatter(tensor.astype(jnp.bfloat16), 'heads', scatter_dimension=...  210 us
    dot_general x18, matrix products, conv_backward(): lax.dot_general(gradient, kernel[row_shift, col_shift], CONTRACT_LAST, pr...  153 us
    reduce_scatter x1, waiting for transfers between devices, on_device(): lax.psum_scatter(local_grads[10], 'rows', scatter_dimension=1, tiled=True)  125 us
    all_gather x1, waiting for transfers between devices, on_device(): lax.all_gather(sharded[1], 'rows', axis=2, tiled=True)  120 us
    reduce_scatter x1, waiting for transfers between devices, on_device(): lax.psum_scatter(local_grads[4], 'rows', scatter_dimension=0, tiled=True)  115 us
  transfers between devices with their start and end apart: 58, of which 48 were waited for; matrix products, arithmetic and copies ran while one was open for 20% of the time, Pallas kernels for 0%

commit v1 on v0

v1 whole, which is shorter than its diff:
```python
import math

import jax
import jax.numpy as jnp
from jax import lax
from jax.experimental import pallas as pl
from jax.sharding import PartitionSpec as P
from jax.experimental.pallas import tpu as pltpu

C = 1280
DH = 64
GROUPS = 32
MEMBER = C // GROUPS
TAPS = 9
UNROLL = 8

EPS_RES = 1e-05
EPS_MID = 1e-06
EPS_LAYER = 1e-05

F32 = jnp.float32
BF16 = jnp.bfloat16


def dot(a, b, a_dim, b_dim, kind=F32):
    return lax.dot_general(
        a, b, (((a_dim,), (b_dim,)), ((), ())), preferred_element_type=F32
    ).astype(kind)


def swap(x, axis, mask):
    return lax.ppermute(x, axis, [(i, i ^ mask) for i in range(lax.axis_size(axis))])


def swap_half(x):
    return swap(x, "rows", 1)


def swap_core(x):
    return swap(x, "heads", 1)


def swap_far(x):
    return swap(x, "heads", 2)


def shift_image(x):
    n = lax.axis_size("rows")
    return lax.ppermute(x, "rows", [(i, (i + 2) % n) for i in range(n)])


def pair(own, other, place, axis):
    return jnp.where(
        place == 0,
        jnp.concatenate([own, other], axis=axis),
        jnp.concatenate([other, own], axis=axis),
    )


def pick(x, place, axis):
    return lax.dynamic_index_in_dim(x, place, axis, keepdims=False)


def part(x, place, count, axis=0):
    size = x.shape[axis] // count
    return lax.dynamic_slice_in_dim(x, place * size, size, axis)


class Place:
    def __init__(self):
        row = lax.axis_index("rows")
        head = lax.axis_index("heads")
        self.row = row
        self.half = row % 2
        self.image = row // 2
        self.images = lax.axis_size("rows") // 2
        self.core = head % 2
        self.far = head // 2
        self.head = head


def image_gather(at, chunk):
    n, size = at.images, chunk.shape[0]
    whole = jnp.zeros((n * size,) + chunk.shape[1:], chunk.dtype)

    def put(whole, chunk, step):
        start = lax.rem(at.image - step + n, n) * size
        return lax.dynamic_update_slice_in_dim(whole, chunk, start, 0)

    if n > UNROLL:

        def body(step, carry):
            whole, chunk = carry
            return put(whole, chunk, step), shift_image(chunk)

        return lax.fori_loop(0, n, body, (whole, chunk))[0]
    for step in range(n):
        whole = put(whole, chunk, step)
        if step < n - 1:
            chunk = shift_image(chunk)
    return whole


def rows_gather(at, chunk):
    n, size = at.images, chunk.shape[0]
    if n > UNROLL:
        own = image_gather(at, chunk)
        split = (n, 1) + chunk.shape
        both = pair(own.reshape(split), swap_half(own).reshape(split), at.half, 1)
        return both.reshape((2 * n * size,) + chunk.shape[1:])
    whole = jnp.zeros((2 * n * size,) + chunk.shape[1:], chunk.dtype)
    for step in range(n):
        start = lax.rem(at.image - step + n, n) * 2
        other = swap_half(chunk)
        whole = lax.dynamic_update_slice_in_dim(whole, chunk, (start + at.half) * size, 0)
        whole = lax.dynamic_update_slice_in_dim(whole, other, (start + 1 - at.half) * size, 0)
        if step < n - 1:
            chunk = shift_image(chunk)
    return whole


def image_scatter(at, blocks):
    n = at.images

    def local(step):
        return lax.dynamic_index_in_dim(
            blocks, lax.rem(at.image - 1 - step + 2 * n, n), 0, keepdims=False
        )

    def advance(step, moving):
        return shift_image(moving).astype(F32) + local(step + 1).astype(F32)

    moving = local(0)
    if n > UNROLL:
        moving = lax.fori_loop(
            0, n - 2, lambda step, value: advance(step, value).astype(blocks.dtype), moving
        )
    else:
        for step in range(n - 2):
            moving = advance(step, moving).astype(blocks.dtype)
    return advance(n - 2, moving)


def rows_scatter(at, grad):
    blocks = grad.reshape((at.images, 2, -1) + grad.shape[1:])
    other = swap_half(pick(blocks, 1 - at.half, 1))
    summed = (pick(blocks, at.half, 1).astype(F32) + other.astype(F32)).astype(BF16)
    return image_scatter(at, summed)


def rows_total(x, first=1):
    mask = first
    while mask < lax.axis_size("rows"):
        x = x + swap(x, "rows", mask)
        mask *= 2
    return x


def image_stack(at, x):
    x = x[None]
    mask = 1
    while mask < at.images:
        x = pair(x, swap(x, "rows", 2 * mask), (at.image // mask) % 2, 0)
        mask *= 2
    return x


def heads_scatter(at, grad):
    own = part(grad, at.core, 2).astype(F32)
    own = own + swap_core(part(grad, 1 - at.core, 2)).astype(F32)
    other = swap_far(part(own, 1 - at.far, 2).astype(BF16))
    return part(own, at.far, 2) + other.astype(F32)


def heads_gather(at, quarter):
    two = pair(quarter, swap_far(quarter), at.far, 0)
    return pair(two, swap_core(two), at.core, 0)


def to_tokens(at, x):
    other = swap_core(part(x, 1 - at.core, 2).astype(BF16)).astype(F32)
    x = pair(part(x, at.core, 2), other, at.core, 1)
    other = swap_far(part(x, 1 - at.far, 2).astype(BF16)).astype(F32)
    return pair(part(x, at.far, 2), other, at.far, 1)


def to_channels(at, x):
    wide = x.shape[1] // 2
    first, second = x[:, :wide], x[:, wide:]
    other = swap_far(jnp.where(at.far == 0, second, first))
    x = pair(jnp.where(at.far == 0, first, second), other, at.far, 0)
    wide = wide // 2
    first, second = x[:, :wide], x[:, wide:]
    other = swap_core(jnp.where(at.core == 0, second, first))
    return pair(jnp.where(at.core == 0, first, second), other, at.core, 0)


def channel_rows_gather(at, x):
    shape = x.shape
    x = pair(x[None], swap_far(x)[None], at.far, 0)
    x = pair(x[:, None], swap_core(x)[:, None], at.core, 1)
    return x.reshape((-1,) + shape[1:])


def channel_rows_scatter(at, x):
    blocks = x.reshape(2, 2, -1, x.shape[1])
    own = pick(blocks, at.core, 1).astype(F32)
    own = own + swap_core(pick(blocks, 1 - at.core, 1)).astype(F32)
    other = swap_far(pick(own, 1 - at.far, 0).astype(BF16))
    return pick(own, at.far, 0) + other.astype(F32)


def to_image(at, x):
    blocks = x.reshape(2, -1, x.shape[1])
    return pair(pick(blocks, at.half, 0), swap_half(pick(blocks, 1 - at.half, 0)), at.half, 1)


def from_image(at, x):
    return pair(
        part(x, at.half, 2, 1), swap_half(part(x, 1 - at.half, 2, 1)), at.half, 0
    )


def plane_gather(at, x):
    width, tokens = x.shape
    left, right = x[:, : tokens // 2], x[:, tokens // 2 :]
    left = pair(left[None], swap_half(left)[None], at.half, 0)
    right = pair(right[None], swap_far(right)[None], at.far, 0)
    left = pair(left[None], swap_far(left)[None], at.far, 0)
    right = pair(right[:, None], swap_half(right)[:, None], at.half, 1)
    x = jnp.concatenate([left, right], axis=3)
    x = pair(x[:, None], swap_core(x)[:, None], at.core, 1)
    return x.reshape(8 * width, tokens)


def plane_scatter(at, x):
    tokens = x.shape[1]
    blocks = x.reshape(2, 2, 2, -1, tokens)
    own = pick(blocks, at.core, 1).astype(F32)
    own = own + swap_core(pick(blocks, 1 - at.core, 1)).astype(F32)
    left, right = own[..., : tokens // 2], own[..., tokens // 2 :]
    left = pick(left, at.half, 1) + swap_half(pick(left, 1 - at.half, 1).astype(BF16)).astype(F32)
    right = pick(right, at.far, 0) + swap_far(pick(right, 1 - at.far, 0).astype(BF16)).astype(F32)
    left = pick(left, at.far, 0) + swap_far(pick(left, 1 - at.far, 0).astype(BF16)).astype(F32)
    right = pick(right, at.half, 0) + swap_half(pick(right, 1 - at.half, 0).astype(BF16)).astype(
        F32
    )
    return jnp.concatenate([left, right], axis=1)


def group_forward(inputs, gain, shift, epsilon):
    grouped = inputs.reshape(-1, MEMBER, inputs.shape[1])
    center = jnp.mean(grouped, axis=(1, 2), keepdims=True)
    inverse = lax.rsqrt(jnp.mean(jnp.square(grouped - center), axis=(1, 2), keepdims=True) + epsilon)
    normed = ((grouped - center) * inverse).reshape(inputs.shape)
    return normed * gain[:, None] + shift[:, None], (normed, inverse)


def group_backward(gradient, gain, stored):
    normed, inverse = stored
    shape = gradient.shape
    scaled = (gradient * gain[:, None]).reshape(-1, MEMBER, shape[1])
    flat = normed.reshape(scaled.shape)
    first = jnp.mean(scaled, axis=(1, 2), keepdims=True)
    second = jnp.mean(scaled * flat, axis=(1, 2), keepdims=True)
    back = (inverse * (scaled - first - flat * second)).reshape(shape)
    return back, [jnp.sum(gradient * normed, axis=1), jnp.sum(gradient, axis=1)]


def layer_forward(inputs, params):
    center = jnp.mean(inputs, axis=1, keepdims=True)
    inverse = lax.rsqrt(jnp.mean(jnp.square(inputs - center), axis=1, keepdims=True) + EPS_LAYER)
    normed = (inputs - center) * inverse
    return (normed * params[0] + params[1]).astype(BF16), (normed, inverse)


def layer_backward(gradient, params, stored):
    normed, inverse = stored
    scaled = gradient * params[0]
    first = jnp.mean(scaled, axis=1, keepdims=True)
    second = jnp.mean(scaled * normed, axis=1, keepdims=True)
    back = inverse * (scaled - first - normed * second)
    return back, [jnp.sum(gradient * normed, axis=0), jnp.sum(gradient, axis=0)]


def silu_slope(inputs):
    sigma = jax.nn.sigmoid(inputs)
    return sigma * (1.0 + inputs * (1.0 - sigma))


def tap_mask(shape, tap, columns):
    place = lax.broadcasted_iota(jnp.int32, shape, 1)
    line, column = place // columns, place % columns
    keep = None
    for value, step, count in (
        (line, tap // 3 - 1, shape[1] // columns),
        (column, tap % 3 - 1, columns),
    ):
        if step != 0:
            inside = value >= 1 if step < 0 else value <= count - 2
            keep = inside if keep is None else jnp.logical_and(keep, inside)
    return keep


def tap_offset(tap, columns):
    return (tap // 3 - 1) * columns + tap % 3 - 1


def tap_sum_kernel(columns, taps_ref, sum_ref):
    tokens = taps_ref.shape[2]
    total = taps_ref[4]
    for tap in range(TAPS):
        if tap != 4:
            moved = pltpu.roll(taps_ref[tap], -tap_offset(tap, columns) % tokens, 1)
            total = total + jnp.where(tap_mask(moved.shape, tap, columns), moved, 0.0)
    sum_ref[...] = total


def tap_sum(taps, columns):
    tokens = taps.shape[1]
    width = taps.shape[0] // TAPS
    block = 32
    return pl.pallas_call(
        lambda *refs: tap_sum_kernel(columns, *refs),
        grid=(width // block,),
        in_specs=[pl.BlockSpec((TAPS, block, tokens), lambda i: (0, i, 0))],
        out_specs=pl.BlockSpec((block, tokens), lambda i: (i, 0)),
        out_shape=jax.ShapeDtypeStruct((width, tokens), F32),
        compiler_params=pltpu.CompilerParams(vmem_limit_bytes=16 * 2**20),
        name="tap_sum",
    )(taps.reshape(TAPS, width, tokens))


def tap_spread_kernel(columns, grad_ref, taps_ref):
    tokens = grad_ref.shape[1]
    grad = grad_ref[...].astype(F32)
    for tap in range(TAPS):
        if tap == 4:
            taps_ref[tap] = grad_ref[...]
            continue
        moved = pltpu.roll(grad, tap_offset(tap, columns) % tokens, 1)
        keep = tap_mask(moved.shape, TAPS - 1 - tap, columns)
        taps_ref[tap] = jnp.where(keep, moved, 0.0).astype(taps_ref.dtype)


def tap_spread(grad, columns):
    width, tokens = grad.shape
    block = 32
    return pl.pallas_call(
        lambda *refs: tap_spread_kernel(columns, *refs),
        grid=(width // block,),
        in_specs=[pl.BlockSpec((block, tokens), lambda i: (i, 0))],
        out_specs=pl.BlockSpec((TAPS, block, tokens), lambda i: (0, i, 0)),
        out_shape=jax.ShapeDtypeStruct((TAPS, width, tokens), BF16),
        compiler_params=pltpu.CompilerParams(vmem_limit_bytes=16 * 2**20),
        name="tap_spread",
    )(grad).reshape(TAPS * width, tokens)


def conv_weights(at, kernel):
    inputs, outputs = kernel.shape[2:]
    halves = kernel.reshape(TAPS, inputs, 2, outputs // 2).transpose(2, 1, 0, 3)
    halves = halves.reshape(2, inputs, -1)
    other = swap_half(pick(halves, 1 - at.half, 0))
    return image_gather(at, pair(pick(halves, at.half, 0), other, at.half, 0))


def conv_weights_back(at, grad, inputs):
    total = image_scatter(at, grad.reshape(at.images, 2 * inputs, -1))
    other = swap_half(part(total, 1 - at.half, 2).astype(BF16)).astype(F32)
    own = part(total, at.half, 2).reshape(inputs, TAPS, -1)
    grad = pair(own, other.reshape(inputs, TAPS, -1), at.half, 2)
    return grad.transpose(1, 0, 2).reshape(3, 3, inputs, -1)


def by_heads(x):
    return x.reshape(x.shape[0], -1, DH)


def attend(queries, blocks):
    q_heads = by_heads(queries)
    scores = [
        jnp.einsum("qhd,khd->hqk", q_heads, by_heads(keys), preferred_element_type=F32)
        * (1.0 / math.sqrt(DH))
        for keys, values in blocks
    ]
    peak = scores[0].max(axis=-1, keepdims=True)
    for one in scores[1:]:
        peak = jnp.maximum(peak, one.max(axis=-1, keepdims=True))
    raised = [jnp.exp(one - peak) for one in scores]
    total = sum(one.sum(axis=-1, keepdims=True) for one in raised)
    joined = sum(
        jnp.einsum(
            "hqk,khd->qhd",
            (one / total).astype(BF16),
            by_heads(values),
            preferred_element_type=F32,
        )
        for one, (keys, values) in zip(raised, blocks)
    )
    return joined.reshape(queries.shape).astype(BF16), peak + jnp.log(total)


def attend_back(grad_out, queries, blocks, log_total):
    scaling = 1.0 / math.sqrt(DH)
    q_heads, g_heads = by_heads(queries), by_heads(grad_out)
    probs, slopes = [], []
    for keys, values in blocks:
        scores = jnp.einsum("qhd,khd->hqk", q_heads, by_heads(keys), preferred_element_type=F32)
        probs.append(jnp.exp(scores * scaling - log_total))
        slopes.append(
            jnp.einsum("qhd,khd->hqk", g_heads, by_heads(values), preferred_element_type=F32)
        )
    center = sum(
        jnp.sum(one * slope, axis=-1, keepdims=True) for one, slope in zip(probs, slopes)
    )
    grad_query, grad_blocks = 0.0, []
    for one, slope, (keys, values) in zip(probs, slopes, blocks):
        grad_scores = (one * (slope - center)).astype(BF16)
        grad_query = grad_query + jnp.einsum(
            "hqk,khd->qhd", grad_scores, by_heads(keys), preferred_element_type=F32
        )
        grad_keys = scaling * jnp.einsum(
            "hqk,qhd->khd", grad_scores, q_heads, preferred_element_type=F32
        )
        grad_values = jnp.einsum(
            "hqk,qhd->khd", one.astype(BF16), g_heads, preferred_element_type=F32
        )
        grad_blocks.append(
            jnp.concatenate(
                [grad_keys.reshape(keys.shape), grad_values.reshape(values.shape)], axis=1
            )
        )
    return (grad_query * scaling).reshape(queries.shape).astype(BF16), grad_blocks


def on_device(
    latents,
    text,
    step_count,
    time_index,
    conv1_w,
    conv2_w,
    time_w,
    proj_in_w,
    qkv_w,
    self_out_w,
    cross_q_w,
    cross_kv_w,
    cross_out_w,
    ff_in_w,
    ff_out_w,
    proj_out_w,
    gn_params,
    ln_params,
    biases,
    ff_bias,
    cotangent,
):
    at = Place()
    columns = latents.shape[2]
    width = latents.shape[3]
    tokens = latents.shape[1] * columns
    half = width // 2
    inputs = time_w.shape[0]
    hidden = ff_in_w.shape[2]

    conv_one = conv_weights(at, conv1_w)
    conv_two = conv_weights(at, conv2_w)
    w_first = rows_gather(
        at,
        jnp.concatenate([qkv_w[:, 1], qkv_w[:, 2], qkv_w[:, 0], proj_in_w], axis=1),
    )
    w_kvq, w_in = w_first[:, : 3 * width], w_first[:, 3 * width :]
    w_second = rows_gather(
        at, jnp.concatenate([self_out_w.T, cross_q_w, cross_out_w.T, proj_out_w], axis=1)
    )
    w_self, w_query, w_cross, w_out = (
        w_second[:, i * width : (i + 1) * width] for i in range(4)
    )
    w_value = rows_gather(at, ff_in_w[:, 0])
    w_gate = rows_gather(at, ff_in_w[:, 1])
    w_narrow = rows_gather(at, ff_out_w.T)

    own_params = jnp.concatenate([ln_params.reshape(6, width), biases[4:7]], axis=0)
    wide = pair(own_params, swap_core(own_params), at.core, 1)
    wide = pair(wide, swap_far(wide), at.far, 1)
    ln_wide, bias_self, bias_cross, bias_narrow = wide[:6].reshape(3, 2, C), wide[6], wide[7], wide[8]
    gn_own = part(gn_params, at.half, 2, 2)
    bias_own = part(biases, at.half, 2, 1)

    images = step_count.shape[0]
    moment = (999 - 1000 * time_index // step_count).astype(F32)
    half_width = C // 2
    channel = at.row * inputs + jnp.arange(inputs)
    frequency = jnp.exp(-math.log(10000.0) * (channel % half_width).astype(F32) / half_width)
    angles = moment[:, None] * frequency[None, :]
    embedding = jnp.where(channel[None, :] < half_width, jnp.cos(angles), jnp.sin(angles))
    temb_low = jax.nn.silu(embedding).astype(BF16)
    shift_all = rows_total(jnp.dot(temb_low, time_w, preferred_element_type=F32))
    shift_time = lax.dynamic_index_in_dim(shift_all, at.image, 0, keepdims=False)
    shift_time = part(shift_time, at.half, 2) + bias_own[1]

    text_own = part(text, at.row, lax.axis_size("rows"), 2)
    pair_w = cross_kv_w.reshape(cross_kv_w.shape[0], -1)
    kv_part = jnp.einsum("isc,cd->isd", text_own, pair_w, preferred_element_type=F32)
    kv_part = (kv_part + swap_half(kv_part.astype(BF16)).astype(F32)).astype(BF16)
    cross_kv = image_scatter(at, kv_part).astype(BF16)
    cross_keys, cross_values = cross_kv[:, :width], cross_kv[:, width:]

    source = to_image(at, latents.reshape(tokens, width).T).astype(F32)
    cot_rows = cotangent.reshape(tokens, width)
    cot_image = to_image(at, cot_rows.T).astype(F32)
    norm_one, stored_one = group_forward(source, gn_own[0, 0], gn_own[0, 1], EPS_RES)
    act_one = plane_gather(at, jax.nn.silu(norm_one).astype(BF16))
    hidden_two = tap_sum(dot(conv_one, act_one, 0, 0), columns)
    hidden_two = hidden_two + (bias_own[0] + shift_time)[:, None]
    norm_two, stored_two = group_forward(hidden_two, gn_own[1, 0], gn_own[1, 1], EPS_RES)
    act_two = plane_gather(at, jax.nn.silu(norm_two).astype(BF16))
    resid = source + tap_sum(dot(conv_two, act_two, 0, 0), columns) + bias_own[2][:, None]
    norm_three, stored_three = group_forward(resid, gn_own[2, 0], gn_own[2, 1], EPS_MID)
    gin = channel_rows_gather(at, from_image(at, norm_three.astype(BF16)))
    resid_own = from_image(at, resid)

    stream_zero = to_tokens(at, dot(gin, w_in, 0, 0) + biases[3])
    low_one, stored_ln_one = layer_forward(stream_zero, ln_wide[0])
    n_one = heads_gather(at, low_one)
    kv_own = dot(n_one, w_kvq[:, : 2 * width], 1, 0, BF16)
    kv_other = swap_half(kv_own)
    queries = dot(n_one, w_kvq[:, 2 * width :], 1, 0, BF16)
    self_blocks = [(kv[:, :width], kv[:, width:]) for kv in (kv_own, kv_other)]
    attended, log_self = attend(queries, self_blocks)
    stream_one = stream_zero + heads_scatter(at, dot(attended, w_self, 1, 1, BF16)) + bias_self

    low_two, stored_ln_two = layer_forward(stream_one, ln_wide[1])
    n_two = heads_gather(at, low_two)
    cross_query = dot(n_two, w_query, 1, 0, BF16)
    cross_blocks = [(cross_keys, cross_values)]
    cross_att, log_cross = attend(cross_query, cross_blocks)
    stream_two = stream_one + heads_scatter(at, dot(cross_att, w_cross, 1, 1, BF16)) + bias_cross

    low_three, stored_ln_three = layer_forward(stream_two, ln_wide[2])
    n_three = heads_gather(at, low_three)
    value_in = dot(n_three, w_value, 1, 0) + ff_bias[0]
    gate_in = dot(n_three, w_gate, 1, 0) + ff_bias[1]
    cdf = 0.5 * (1.0 + lax.erf(gate_in / math.sqrt(2.0)))
    gelu = gate_in * cdf
    mixed = (value_in * gelu).astype(BF16)
    stream_three = stream_two + heads_scatter(at, dot(mixed, w_narrow, 1, 1, BF16)) + bias_narrow
    three = heads_gather(at, stream_three.astype(BF16))
    result = resid_own + (dot(w_out, three, 0, 1) + biases[7][:, None])
    output = result.astype(BF16).T.reshape(latents.shape)

    out_grad = dot(three, cot_rows, 0, 0, BF16)
    bias_seven = jnp.sum(cot_rows.astype(F32), axis=0)
    grad_three = heads_scatter(at, dot(cot_rows, w_out, 1, 1, BF16))
    low_ff = grad_three.astype(BF16)
    grad_ff = heads_gather(at, low_ff)
    narrow_grad = dot(grad_ff, mixed, 0, 0, BF16)
    grad_mixed = dot(grad_ff, w_narrow, 1, 0, BF16).astype(F32)
    pdf = jnp.exp(-0.5 * gate_in * gate_in) / math.sqrt(2.0 * math.pi)
    grad_value = (grad_mixed * gelu).astype(BF16)
    grad_gate = (grad_mixed * value_in * (cdf + gate_in * pdf)).astype(BF16)
    ffbias_grad = jnp.stack(
        [jnp.sum(grad_value.astype(F32), axis=0), jnp.sum(grad_gate.astype(F32), axis=0)]
    )
    value_grad = dot(n_three, grad_value, 0, 0, BF16)
    gate_grad = dot(n_three, grad_gate, 0, 0, BF16)
    grad_ln = heads_scatter(
        at, (dot(grad_value, w_value, 1, 1) + dot(grad_gate, w_gate, 1, 1)).astype(BF16)
    )
    back, ln_grad_three = layer_backward(grad_ln, ln_wide[2], stored_ln_three)
    grad_two = grad_three + back

    low_cross = grad_two.astype(BF16)
    grad_cross = heads_gather(at, low_cross)
    cross_grad = dot(grad_cross, cross_att, 0, 0, BF16)
    grad_cross_att = dot(grad_cross, w_cross, 1, 0, BF16)
    grad_cq, (grad_ckv,) = attend_back(grad_cross_att, cross_query, cross_blocks, log_cross)
    query_grad = dot(n_two, grad_cq, 0, 0, BF16)
    grad_ckv = (grad_ckv + swap_half(grad_ckv.astype(BF16)).astype(F32)).astype(BF16)
    grad_ckv = image_gather(at, grad_ckv[None])
    pair_grad = jnp.einsum("isc,isd->cd", text_own, grad_ckv, preferred_element_type=F32)
    grad_ln = heads_scatter(at, dot(grad_cq, w_query, 1, 1, BF16))
    back, ln_grad_two = layer_backward(grad_ln, ln_wide[1], stored_ln_two)
    grad_one = grad_two + back

    low_self = grad_one.astype(BF16)
    grad_self = heads_gather(at, low_self)
    self_grad = dot(grad_self, attended, 0, 0, BF16)
    grad_attended = dot(grad_self, w_self, 1, 0, BF16)
    grad_q, (grad_kv, grad_kv_other) = attend_back(grad_attended, queries, self_blocks, log_self)
    grad_kv = (grad_kv + swap_half(grad_kv_other.astype(BF16)).astype(F32)).astype(BF16)
    grad_kvq = jnp.concatenate([grad_kv, grad_q], axis=1)
    kvq_grad = dot(n_one, grad_kvq, 0, 0, BF16)
    grad_ln = heads_scatter(at, dot(grad_kvq, w_kvq, 1, 1, BF16))
    back, ln_grad_one = layer_backward(grad_ln, ln_wide[0], stored_ln_one)
    grad_zero = to_channels(at, (grad_one + back).astype(BF16))
    in_grad = dot(gin, grad_zero, 1, 0, BF16)
    bias_three = jnp.sum(grad_zero.astype(F32), axis=0)
    grad_gin = channel_rows_scatter(at, dot(w_in, grad_zero, 1, 1, BF16))

    own_half = pick(grad_gin.reshape(2, half, tokens), at.half, 0)
    other_half = pick(grad_gin.reshape(2, half, tokens), 1 - at.half, 0)
    grad_gin = pair(own_half, swap_half(other_half.astype(BF16)).astype(F32), at.half, 1)
    back, gn_grad_three = group_backward(grad_gin, gn_own[2, 0], stored_three)
    grad_resid = cot_image + back
    grad_c_two = grad_resid.astype(BF16)
    bias_two = jnp.sum(grad_c_two.astype(F32), axis=1)
    spread_two = tap_spread(grad_c_two, columns)
    grad_act = plane_scatter(at, dot(conv_two, spread_two, 1, 0, BF16))
    conv_two_grad = dot(act_two, spread_two, 1, 1, BF16)
    grad_hidden, gn_grad_two = group_backward(
        grad_act * silu_slope(norm_two), gn_own[1, 0], stored_two
    )
    image_sum = jnp.sum(grad_hidden, axis=1)
    grad_c_one = grad_hidden.astype(BF16)
    bias_zero = jnp.sum(grad_c_one.astype(F32), axis=1)
    spread_one = tap_spread(grad_c_one, columns)
    grad_act = plane_scatter(at, dot(conv_one, spread_one, 1, 0, BF16))
    conv_one_grad = dot(act_one, spread_one, 1, 1, BF16)
    back, gn_grad_one = group_backward(
        grad_act * silu_slope(norm_one), gn_own[0, 0], stored_one
    )
    latents_grad = from_image(at, grad_resid + back).T.reshape(latents.shape)

    second = rows_scatter(
        at, jnp.concatenate([self_grad, query_grad, cross_grad, out_grad], axis=1)
    )
    narrow = rows_scatter(at, narrow_grad)
    value = rows_scatter(at, value_grad)
    gate = rows_scatter(at, gate_grad)
    first = rows_scatter(at, jnp.concatenate([kvq_grad, in_grad], axis=1))
    conv_two_out = conv_weights_back(at, conv_two_grad, inputs)
    conv_one_out = conv_weights_back(at, conv_one_grad, inputs)

    token_sums = jnp.stack(
        ln_grad_one
        + ln_grad_two
        + ln_grad_three
        + [jnp.sum(low.astype(F32), axis=0) for low in (low_self, low_cross, low_ff)]
    )
    wide_half = C // 2
    keep = jnp.where(at.far == 0, token_sums[:, :wide_half], token_sums[:, wide_half:])
    send = jnp.where(at.far == 0, token_sums[:, wide_half:], token_sums[:, :wide_half])
    keep = keep + swap_far(send)
    own = jnp.where(at.core == 0, keep[:, :width], keep[:, width:])
    send = jnp.where(at.core == 0, keep[:, width:], keep[:, :width])
    own = own + swap_core(send)
    own = jnp.concatenate(
        [own, bias_three[None], bias_seven[None], ffbias_grad.reshape(-1, width)], axis=0
    )
    own = rows_total(own)
    ln_total = own[:6].reshape(3, 2, width)
    ffbias_total = own[11:].reshape(2, hidden)
    image_sums = jnp.stack(
        gn_grad_one + gn_grad_two + gn_grad_three + [bias_zero, image_sum, bias_two]
    )
    image_sums = image_stack(at, image_sums)
    image_sums = pair(image_sums, swap_half(image_sums), at.half, 2)
    totals = jnp.sum(image_sums, axis=0)
    gn_total = totals[:6].reshape(3, 2, width)
    bias_total = jnp.concatenate([totals[6:9], own[9:10], own[6:9], own[10:11]], axis=0)
    time_grad = lax.dot_general(
        temb_low.astype(F32),
        image_sums[:, 7],
        (((0,), (0,)), ((), ())),
        precision=lax.Precision.HIGHEST,
        preferred_element_type=F32,
    )

    cut = [i * width for i in range(5)]
    return (
        output,
        latents_grad,
        conv_one_out,
        conv_two_out,
        time_grad,
        first[:, cut[3] : cut[4]],
        jnp.stack([first[:, cut[2] : cut[3]], first[:, : cut[1]], first[:, cut[1] : cut[2]]], axis=1),
        second[:, : cut[1]].T,
        second[:, cut[1] : cut[2]],
        pair_grad.reshape(cross_kv_w.shape),
        second[:, cut[2] : cut[3]].T,
        jnp.stack([value, gate], axis=1),
        narrow.T,
        second[:, cut[3] : cut[4]],
        gn_total,
        ln_total,
        bias_total,
        ffbias_total,
    )


def solution(mesh):
    return jax.shard_map(
        on_device,
        mesh=mesh,
        in_specs=(
            P("rows", None, None, "heads"),
            P(),
            P(),
            P(),
            P(None, None, "rows", "heads"),
            P(None, None, "rows", "heads"),
            P("rows", "heads"),
            P("rows", "heads"),
            P("rows", None, "heads"),
            P("heads", "rows"),
            P("rows", "heads"),
            P("rows", None, "heads"),
            P("heads", "rows"),
            P("rows", None, "heads"),
            P("heads", "rows"),
            P("rows", "heads"),
            P(None, None, "heads"),
            P(None, None, "heads"),
            P(None, "heads"),
            P(None, "heads"),
            P("rows", None, None, "heads"),
        ),
        out_specs=(
            P("rows", None, None, "heads"),
            P("rows", None, None, "heads"),
            P(None, None, "rows", "heads"),
            P(None, None, "rows", "heads"),
            P("rows", "heads"),
            P("rows", "heads"),
            P("rows", None, "heads"),
            P("heads", "rows"),
            P("rows", "heads"),
            P("rows", None, "heads"),
            P("heads", "rows"),
            P("rows", None, "heads"),
            P("heads", "rows"),
            P("rows", "heads"),
            P(None, None, "heads"),
            P(None, None, "heads"),
            P(None, "heads"),
            P(None, "heads"),
        ),
        check_vma=False,
    )
```

time: 4150 us -> 1210 us (0.29)
  waiting for transfers between devices: 2210 us -> 508 us
  local copies, waits for them, and re-layouts: 1200 us -> 310 us
  blocking collectives: 287 us -> 0 us
  matrix products: 303 us -> 125 us
  starting transfers between devices: 25.8 us -> 142 us
    reduce_scatter x22 -> x0, waiting for transfers between devices: 1650 us -> none  [the longest x1 301 us: on_device(): lax.psum_scatter(local_grads[1], 'rows', scatter_dimension=2, tiled=True)]
    scatter-add x22 -> x0, local copies, waits for them, and re-layouts: 1070 us -> none  [the longest x18 1060 us: conv_backward(): spread.at[row_shift:row_shift + height, col_shift:col_shift + columns]]
    all_gather x16 -> x0, waiting for transfers between devices: 520 us -> none  [the longest x1 120 us: on_device(): lax.all_gather(sharded[1], 'rows', axis=2, tiled=True)]
    ppermute x20 -> x156, waiting for transfers between devices: 30.5 us -> 508 us  [the longest x108 295 us: swap(): lax.ppermute(x, axis, [(i, i ^ mask) for i in range(lax.axis_size(axis))])]
    all_gather x6 -> x0, blocking collectives: 211 us -> none  [the longest x1 36.9 us: on_device(): lax.all_gather(sharded[5], 'rows', axis=1, tiled=True)]
    dot_general x93 -> x56, matrix products: 303 us -> 125 us  [the longest x34 99.3 us: dot(): lax.dot_general(a, b, (((a_dim,), (b_dim,)), ((), ())), preferred_element...]
    dynamic_update_slice x0 -> x51, local copies, waits for them, and re-layouts: none -> 137 us  [the longest x11 92.2 us: put(): return lax.dynamic_update_slice_in_dim(whole, chunk, start, 0)]
    ppermute x20 -> x156, starting transfers between devices: 23.3 us -> 142 us  [the longest x108 101 us: swap(): lax.ppermute(x, axis, [(i, i ^ mask) for i in range(lax.axis_size(axis))])]
  transfers between devices with their start and end apart: 58 -> 156, of which waited for: 48 -> 65; matrix products, arithmetic and copies ran while one was open for 20% -> 42% of each run, Pallas kernels for 0% -> 1%
where the time goes in v1:
time: 1210 us; the launch traced here: 1200 us
  waiting for transfers between devices  508 us (42%)
  local copies, waits for them, and re-layouts  310 us (26%)
  starting transfers between devices  142 us (12%)
  matrix products  125 us (10%)
  other arithmetic  100 us (8%)
    ppermute x108, waiting for transfers between devices, swap(): lax.ppermute(x, axis, [(i, i ^ mask) for i in range(lax.axis_size(axis))])  295 us
    ppermute x48, waiting for transfers between devices, shift_image(): return lax.ppermute(x, 'rows', [(i, (i + 2) % n) for i in range(n)])  212 us
    ppermute x108, starting transfers between devices, swap(): lax.ppermute(x, axis, [(i, i ^ mask) for i in range(lax.axis_size(axis))])  101 us
    dot_general x34, matrix products, dot(): lax.dot_general(a, b, (((a_dim,), (b_dim,)), ((), ())), preferred_element...  99.3 us
    dynamic_update_slice x11, local copies, waits for them, and re-layouts, put(): return lax.dynamic_update_slice_in_dim(whole, chunk, start, 0)  92.2 us
    ppermute x48, starting transfers between devices, shift_image(): return lax.ppermute(x, 'rows', [(i, (i + 2) % n) for i in range(n)])  41.1 us
    unnamed x377, local copies, waits for them, and re-layouts  29.1 us
    dynamic_update_slice x20, local copies, waits for them, and re-layouts, rows_gather(): lax.dynamic_update_slice_in_dim(whole, chunk, (start + at.half) * size, 0)  26.4 us
  transfers between devices with their start and end apart: 156, of which 65 were waited for; matrix products, arithmetic and copies ran while one was open for 42% of the time, Pallas kernels for 1%

profile of v1, /device:TPU:0, one launch (start us, length us, event | category | flops | bytes accessed | tf_op | source)
XLA Modules:
  0.0 1196.2 jit_solution(2188132224310273435)
XLA Ops:
  97.3 8.5 collective-permute-done.59
  107.1 6.7 collective-permute-done.5
  117.7 10.5 collective-permute-done.60
  131.8 6.0 collective-permute-done.33
  165.2 7.6 collective-permute-done.7
  179.0 11.1 dynamic_update_slice.160
  190.1 10.2 collective-permute-done.50
  203.1 11.6 dynamic_update_slice.161
  220.8 11.0 dynamic_update_slice.162
  233.9 12.4 %dynamic_update_slice.163 = bf16[1280,1440]{0,1:T(8,128)(2,1)} dynamic-update-slice(bf16[1280,1440]{0,1:T(8,128)(2,1)} %dynamic_update_slice.162, bf16[320,1440]{0,1:T(8,128)(2,1)S(1)} %copy.371, s32[]{:T(128)S(6)} %select_n.754, s32[]{:T(128)} %constant.374.clone.1) | dynamic-update-slice | bytes 1843204 | tf_op jit(solution)/shard_map/dynamic_update_slice | solution.py:88
  246.3 6.9 fusion.204.refs_0_
  267.5 7.1 collective-permute-done.20
  284.2 11.1 dynamic_update_slice.156
  314.5 18.2 %collective-permute-done.36 = bf16[160,1280]{1,0:T(8,128)(2,1)S(1)} collective-permute-done((bf16[160,1280]{1,0:T(8,128)(2,1)}, bf16[160,1280]{1,0:T(8,128)(2,1)S(1)}, u32[]{:S(2)}, u32[]{:S(2)}) %collective-permute-start.36) | collective-permute-done | bytes 409632 | tf_op jit(solution)/shard_map/ppermute | solution.py:49
  336.9 11.6 dynamic_update_slice.157
  350.8 11.0 dynamic_update_slice.158
  366.0 12.4 %dynamic_update_slice.159 = bf16[1280,1440]{0,1:T(8,128)(2,1)} dynamic-update-slice(bf16[1280,1440]{0,1:T(8,128)(2,1)} %dynamic_update_slice.158, bf16[320,1440]{0,1:T(8,128)(2,1)S(1)} %copy.364, s32[]{:T(128)S(6)} %select_n.754, s32[]{:T(128)} %constant.374.clone.1) | dynamic-update-slice | bytes 1843204 | tf_op jit(solution)/shard_map/dynamic_update_slice | solution.py:88
  411.2 12.2 %collective-permute-done.39 = bf16[160,1280]{1,0:T(8,128)(2,1)S(1)} collective-permute-done((bf16[160,1280]{1,0:T(8,128)(2,1)S(1)}, bf16[160,1280]{1,0:T(8,128)(2,1)S(1)}, u32[]{:S(2)}, u32[]{:S(2)}) %collective-permute-start.39) | collective-permute-done | bytes 409632 | tf_op jit(solution)/shard_map/ppermute | solution.py:32
  479.1 6.0 collective-permute-done.46
  510.6 5.7 collective-permute-done.48
  543.9 7.3 collective-permute-done.65
  552.0 8.2 collective-permute-done.56
  576.2 5.8 convert_reduce_fusion.1
  607.6 8.3 collective-permute-done.90
  646.4 24.2 %collective-permute-done.139 = bf16[4,160,1280]{2,1,0:T(8,128)(2,1)} collective-permute-done((bf16[4,160,1280]{2,1,0:T(8,128)(2,1)}, bf16[4,160,1280]{2,1,0:T(8,128)(2,1)}, u32[]{:S(2)}, u32[]{:S(2)}) %collective-permute-start.139) | collective-permute-done | bytes 1638432 | tf_op jit(solution)/shard_map/ppermute | solution.py:32
  673.3 38.8 %collective-permute-done.143 = bf16[4,160,1280]{2,1,0:T(8,128)(2,1)S(1)} collective-permute-done((bf16[4,160,1280]{2,1,0:T(8,128)(2,1)}, bf16[4,160,1280]{2,1,0:T(8,128)(2,1)S(1)}, u32[]{:S(2)}, u32[]{:S(2)}) %collective-permute-start.143) | collective-permute-done | bytes 1638432 | tf_op jit(solution)/shard_map/ppermute | solution.py:32
  745.1 17.3 %collective-permute-done.136 = bf16[1,77,640]{2,1,0:T(8,128)(2,1)S(1)} collective-permute-done((bf16[1,77,640]{2,1,0:T(8,128)(2,1)S(1)}, bf16[1,77,640]{2,1,0:T(8,128)(2,1)S(1)}, u32[]{:S(2)}, u32[]{:S(2)}) %collective-permute-start.136) | collective-permute-done | bytes 98592 | tf_op jit(solution)/shard_map/ppermute | solution.py:49
  762.5 6.4 collective-permute-done.137
  769.0 6.4 collective-permute-done.138
  779.0 10.6 collective-permute-done.145
  791.9 15.2 %collective-permute-done.142 = bf16[160,1280]{1,0:T(8,128)(2,1)S(1)} collective-permute-done((bf16[160,1280]{1,0:T(8,128)(2,1)S(1)}, bf16[160,1280]{1,0:T(8,128)(2,1)S(1)}, u32[]{:S(2)}, u32[]{:S(2)}) %collective-permute-start.142) | collective-permute-done | bytes 409632 | tf_op jit(solution)/shard_map/ppermute | solution.py:49
  817.1 5.7 copy.420
  845.9 32.8 %collective-permute-done.97 = bf16[512,640]{0,1:T(8,128)(2,1)S(1)} collective-permute-done((bf16[512,640]{0,1:T(8,128)(2,1)S(1)}, bf16[512,640]{0,1:T(8,128)(2,1)S(1)}, u32[]{:S(2)}, u32[]{:S(2)}) %collective-permute-start.97) | collective-permute-done | bytes 655392 | tf_op jit(solution)/shard_map/ppermute | solution.py:32
  892.1 5.7 collective-permute-done.99
  914.2 5.6 copy.419
  931.9 7.5 collective-permute-done.133
  942.5 22.1 %collective-permute-done.104 = bf16[160,512]{1,0:T(8,128)(2,1)S(1)} collective-permute-done((bf16[160,512]{1,0:T(8,128)(2,1)S(1)}, bf16[160,512]{1,0:T(8,128)(2,1)S(1)}, u32[]{:S(2)}, u32[]{:S(2)}) %collective-permute-start.104) | collective-permute-done | bytes 163872 | tf_op jit(solution)/shard_map/ppermute | solution.py:32
  969.4 5.5 convolution_convert_fusion
  974.9 6.2 copy.416
  983.5 6.7 convolution_convert_fusion.6
  996.6 19.7 %collective-permute-done.128 = bf16[160,1280]{1,0:T(8,128)(2,1)S(1)} collective-permute-done((bf16[160,1280]{1,0:T(8,128)(2,1)S(1)}, bf16[160,1280]{1,0:T(8,128)(2,1)S(1)}, u32[]{:S(2)}, u32[]{:S(2)}) %collective-permute-start.128) | collective-permute-done | bytes 409632 | tf_op jit(solution)/shard_map/ppermute | solution.py:49
  1022.8 7.9 collective-permute-done.129
  1033.5 24.8 %collective-permute-done.130 = bf16[160,1280]{1,0:T(8,128)(2,1)S(1)} collective-permute-done((bf16[160,1280]{1,0:T(8,128)(2,1)S(1)}, bf16[160,1280]{1,0:T(8,128)(2,1)S(1)}, u32[]{:S(2)}, u32[]{:S(2)}) %collective-permute-start.130) | collective-permute-done | bytes 409632 | tf_op jit(solution)/shard_map/ppermute | solution.py:49
  1072.1 5.5 convolution_convert_fusion.1
  1077.6 6.2 copy.413
  1085.2 13.4 %collective-permute-done.122 = bf16[320,1440]{1,0:T(8,128)(2,1)S(1)} collective-permute-done((bf16[320,1440]{1,0:T(8,128)(2,1)S(1)}, bf16[320,1440]{1,0:T(8,128)(2,1)S(1)}, u32[]{:S(2)}, u32[]{:S(2)}) %collective-permute-start.122) | collective-permute-done | bytes 921632 | tf_op jit(solution)/shard_map/ppermute | solution.py:49
  1104.7 13.4 %collective-permute-done.116 = bf16[320,1440]{1,0:T(8,128)(2,1)S(1)} collective-permute-done((bf16[320,1440]{1,0:T(8,128)(2,1)S(1)}, bf16[320,1440]{1,0:T(8,128)(2,1)S(1)}, u32[]{:S(2)}, u32[]{:S(2)}) %collective-permute-start.116) | collective-permute-done | bytes 921632 | tf_op jit(solution)/shard_map/ppermute | solution.py:49
  1159.4 11.9 collective-permute-done.118
  (1129 shorter events, 644.2 us)
Async XLA Ops:
  2.9 57.0 %collective-permute-start.14 = (f32[4,320]{1,0:T(4,128)S(1)}, f32[4,320]{1,0:T(4,128)}, u32[]{:S(2)}, u32[]{:S(2)}) collective-permute-start(f32[4,320]{1,0:T(4,128)S(1)} %fusion.154), channel_id=1, source_target_pairs={{0,4},{4,0},{8,12},{12,8},{16,20},{20,16},{24,28},{28,24},{1,5},{5... | collective-permute-start | bytes 15368 | tf_op jit(solution)/shard_map/ppermute | solution.py:32
  7.3 64.2 %collective-permute-start.42 = (f32[9,320]{1,0:T(8,128)S(1)}, f32[9,320]{1,0:T(8,128)S(1)}, u32[]{:S(2)}, u32[]{:S(2)}) collective-permute-start(f32[9,320]{1,0:T(8,128)S(1)} %pad_maximum_fusion.12), channel_id=1, source_target_pairs={{0,1},{1,0},{2,3},{3,2},{4,5},{5,4},{6,7},{7,6},{8,9},{9,8},{10,11... | collective-permute-start | bytes 34568 | tf_op jit(solution)/shard_map/ppermute | solution.py:32
  9.2 68.0 %collective-permute-start = (bf16[160,512]{1,0:T(8,128)(2,1)}, bf16[160,512]{1,0:T(8,128)(2,1)S(1)}, u32[]{:S(2)}, u32[]{:S(2)}) collective-permute-start(bf16[160,512]{1,0:T(8,128)(2,1)} %get-tuple-element.270), channel_id=1, source_target_pairs={{0,4},{4,0},{8,12},{12,8},{16,20},{20,16},{24,28},{28,24},{1,5},{5... | collective-permute-start | bytes 491528 | tf_op jit(solution)/shard_map/ppermute | solution.py:32
  11.3 144.0 %collective-permute-start.24 = (bf16[160,1280]{1,0:T(8,128)(2,1)}, bf16[160,1280]{1,0:T(8,128)(2,1)}, u32[]{:S(2)}, u32[]{:S(2)}) collective-permute-start(bf16[160,1280]{1,0:T(8,128)(2,1)} %concatenate.558), channel_id=1, source_target_pairs={{0,8},{4,12},{8,16},{12,20},{16,24},{20,28},{24,0},{28,4},{1,9},{5... | collective-permute-start | bytes 1228808 | tf_op jit(solution)/shard_map/ppermute | solution.py:49
  14.4 134.9 %collective-permute-start.34 = (bf16[160,1280]{1,0:T(8,128)(2,1)}, bf16[160,1280]{1,0:T(8,128)(2,1)}, u32[]{:S(2)}, u32[]{:S(2)}) collective-permute-start(bf16[160,1280]{1,0:T(8,128)(2,1)} %concatenate.573), channel_id=1, source_target_pairs={{0,8},{4,12},{8,16},{12,20},{16,24},{20,28},{24,0},{28,4},{1,9},{5... | collective-permute-start | bytes 1228808 | tf_op jit(solution)/shard_map/ppermute | solution.py:49
  70.0 44.5 %collective-permute-start.73 = (bf16[160,1280]{1,0:T(8,128)(2,1)}, bf16[160,1280]{1,0:T(8,128)(2,1)}, u32[]{:S(2)}, u32[]{:S(2)}) collective-permute-start(bf16[160,1280]{1,0:T(8,128)(2,1)} %bitcast.595), channel_id=1, source_target_pairs={{0,4},{4,0},{8,12},{12,8},{16,20},{20,16},{24,28},{28,24},{1,5},{5... | collective-permute-start | bytes 1228808 | tf_op jit(solution)/shard_map/ppermute | solution.py:32
  114.5 31.2 %collective-permute-start.6 = (bf16[320,1440]{1,0:T(8,128)(2,1)S(1)}, bf16[320,1440]{1,0:T(8,128)(2,1)S(1)}, u32[]{:S(2)}, u32[]{:S(2)}) collective-permute-start(bf16[320,1440]{1,0:T(8,128)(2,1)S(1)} %maximum_select_fusion.13), channel_id=1, source_target_pairs={{0,8},{4,12},{8,16},{12,20},{16,24},{20,28},{24,0},{28,4},{1,9},{5... | collective-permute-start | bytes 2764808 | tf_op jit(solution)/shard_map/ppermute | solution.py:49
  149.2 65.5 %collective-permute-start.13 = (bf16[2,2,160,1024]{3,2,0,1:T(8,128)(2,1)}, bf16[2,2,160,1024]{3,2,0,1:T(8,128)(2,1)}, u32[]{:S(2)}, u32[]{:S(2)}) collective-permute-start(bf16[2,2,160,1024]{3,2,0,1:T(8,128)(2,1)} %get-tuple-element.227), channel_id=1, source_target_pairs={{0,1},{1,0},{2,3},{3,2},{4,5},{5,4},{6,7},{7,6},{8,9},{9,8},{10,11... | collective-permute-start | bytes 3932168 | tf_op jit(solution)/shard_map/ppermute | solution.py:32
  154.6 123.6 %collective-permute-start.67 = (bf16[160,1280]{1,0:T(8,128)(2,1)}, bf16[160,1280]{1,0:T(8,128)(2,1)}, u32[]{:S(2)}, u32[]{:S(2)}) collective-permute-start(bf16[160,1280]{1,0:T(8,128)(2,1)} %get-tuple-element.203), channel_id=1, source_target_pairs={{0,8},{4,12},{8,16},{12,20},{16,24},{20,28},{24,0},{28,4},{1,9},{5... | collective-permute-start | bytes 1228808 | tf_op jit(solution)/shard_map/ppermute | solution.py:49
  162.8 803.0 %collective-permute-start.84 = (bf16[160,512]{1,0:T(8,128)(2,1)}, bf16[160,512]{1,0:T(8,128)(2,1)}, u32[]{:S(2)}, u32[]{:S(2)}) collective-permute-start(bf16[160,512]{1,0:T(8,128)(2,1)} %get-tuple-element.250), channel_id=1, source_target_pairs={{0,4},{4,0},{8,12},{12,8},{16,20},{20,16},{24,28},{28,24},{1,5},{5... | collective-permute-start | bytes 491528 | tf_op jit(solution)/shard_map/ppermute | solution.py:32
  172.8 59.0 %collective-permute-start.8 = (bf16[320,1440]{1,0:T(8,128)(2,1)}, bf16[320,1440]{1,0:T(8,128)(2,1)}, u32[]{:S(2)}, u32[]{:S(2)}) collective-permute-start(bf16[320,1440]{1,0:T(8,128)(2,1)} %collective-permute-done.7), channel_id=1, source_target_pairs={{0,8},{4,12},{8,16},{12,20},{16,24},{20,28},{24,0},{28,4},{1,9},{5... | collective-permute-start | bytes 2764808 | tf_op jit(solution)/shard_map/ppermute | solution.py:49
  200.3 60.6 %collective-permute-start.2 = (bf16[320,1440]{1,0:T(8,128)(2,1)}, bf16[320,1440]{1,0:T(8,128)(2,1)}, u32[]{:S(2)}, u32[]{:S(2)}) collective-permute-start(bf16[320,1440]{1,0:T(8,128)(2,1)} %maximum_select_fusion.12), channel_id=1, source_target_pairs={{0,8},{4,12},{8,16},{12,20},{16,24},{20,28},{24,0},{28,4},{1,9},{5... | collective-permute-start | bytes 2764808 | tf_op jit(solution)/shard_map/ppermute | solution.py:49
  214.8 43.9 %collective-permute-start.51 = (bf16[77,640]{1,0:T(8,128)(2,1)}, bf16[77,640]{1,0:T(8,128)(2,1)S(1)}, u32[]{:S(2)}, u32[]{:S(2)}) collective-permute-start(bf16[77,640]{1,0:T(8,128)(2,1)} %fusion.133), channel_id=1, source_target_pairs={{0,8},{4,12},{8,16},{12,20},{16,24},{20,28},{24,0},{28,4},{1,9},{5... | collective-permute-start | bytes 295688 | tf_op jit(solution)/shard_map/ppermute | solution.py:49
  260.8 35.5 %collective-permute-start.3 = (bf16[320,1440]{1,0:T(8,128)(2,1)}, bf16[320,1440]{1,0:T(8,128)(2,1)}, u32[]{:S(2)}, u32[]{:S(2)}) collective-permute-start(bf16[320,1440]{1,0:T(8,128)(2,1)} %collective-permute-done.2), channel_id=1, source_target_pairs={{0,8},{4,12},{8,16},{12,20},{16,24},{20,28},{24,0},{28,4},{1,9},{5... | collective-permute-start | bytes 2764808 | tf_op jit(solution)/shard_map/ppermute | solution.py:49
  274.6 37.5 %collective-permute-start.35 = (bf16[160,1280]{1,0:T(8,128)(2,1)}, bf16[160,1280]{1,0:T(8,128)(2,1)}, u32[]{:S(2)}, u32[]{:S(2)}) collective-permute-start(bf16[160,1280]{1,0:T(8,128)(2,1)} %collective-permute-done.34), channel_id=1, source_target_pairs={{0,4},{4,0},{8,12},{12,8},{16,20},{20,16},{24,28},{28,24},{1,5},{5... | collective-permute-start | bytes 1228808 | tf_op jit(solution)/shard_map/ppermute | solution.py:32
  278.2 100.3 %collective-permute-start.21 = (bf16[2,2,160,1024]{3,2,0,1:T(8,128)(2,1)}, bf16[2,2,160,1024]{3,2,0,1:T(8,128)(2,1)}, u32[]{:S(2)}, u32[]{:S(2)}) collective-permute-start(bf16[2,2,160,1024]{3,2,0,1:T(8,128)(2,1)} %get-tuple-element.225), channel_id=1, source_target_pairs={{0,1},{1,0},{2,3},{3,2},{4,5},{5,4},{6,7},{7,6},{8,9},{9,8},{10,11... | collective-permute-start | bytes 3932168 | tf_op jit(solution)/shard_map/ppermute | solution.py:32
  296.3 65.4 %collective-permute-start.4 = (bf16[320,1440]{1,0:T(8,128)(2,1)}, bf16[320,1440]{1,0:T(8,128)(2,1)}, u32[]{:S(2)}, u32[]{:S(2)}) collective-permute-start(bf16[320,1440]{1,0:T(8,128)(2,1)} %collective-permute-done.3), channel_id=1, source_target_pairs={{0,8},{4,12},{8,16},{12,20},{16,24},{20,28},{24,0},{28,4},{1,9},{5... | collective-permute-start | bytes 2764808 | tf_op jit(solution)/shard_map/ppermute | solution.py:49
  312.1 119.8 %collective-permute-start.26 = (bf16[160,1280]{1,0:T(8,128)(2,1)}, bf16[160,1280]{1,0:T(8,128)(2,1)}, u32[]{:S(2)}, u32[]{:S(2)}) collective-permute-start(bf16[160,1280]{1,0:T(8,128)(2,1)} %collective-permute-done.24), channel_id=1, source_target_pairs={{0,8},{4,12},{8,16},{12,20},{16,24},{20,28},{24,0},{28,4},{1,9},{5... | collective-permute-start | bytes 1228808 | tf_op jit(solution)/shard_map/ppermute | solution.py:49
  332.7 66.2 %collective-permute-start.75 = (bf16[160,1280]{1,0:T(8,128)(2,1)}, bf16[160,1280]{1,0:T(8,128)(2,1)}, u32[]{:S(2)}, u32[]{:S(2)}) collective-permute-start(bf16[160,1280]{1,0:T(8,128)(2,1)} %copy-done.87), channel_id=1, source_target_pairs={{0,4},{4,0},{8,12},{12,8},{16,20},{20,16},{24,28},{28,24},{1,5},{5... | collective-permute-start | bytes 1228808 | tf_op jit(solution)/shard_map/ppermute | solution.py:32
  361.8 30.0 %collective-permute-start.62 = (bf16[160,1280]{1,0:T(8,128)(2,1)S(1)}, bf16[160,1280]{1,0:T(8,128)(2,1)}, u32[]{:S(2)}, u32[]{:S(2)}) collective-permute-start(bf16[160,1280]{1,0:T(8,128)(2,1)S(1)} %copy-done.90), channel_id=1, source_target_pairs={{0,8},{4,12},{8,16},{12,20},{16,24},{20,28},{24,0},{28,4},{1,9},{5... | collective-permute-start | bytes 1228808 | tf_op jit(solution)/shard_map/ppermute | solution.py:49
  425.5 74.5 %collective-permute-start.69 = (bf16[160,1280]{1,0:T(8,128)(2,1)}, bf16[160,1280]{1,0:T(8,128)(2,1)}, u32[]{:S(2)}, u32[]{:S(2)}) collective-permute-start(bf16[160,1280]{1,0:T(8,128)(2,1)} %collective-permute-done.67), channel_id=1, source_target_pairs={{0,8},{4,12},{8,16},{12,20},{16,24},{20,28},{24,0},{28,4},{1,9},{5... | collective-permute-start | bytes 1228808 | tf_op jit(solution)/shard_map/ppermute | solution.py:49
  450.7 69.1 %collective-permute-start.78 = (bf16[160,1280]{1,0:T(8,128)(2,1)}, bf16[160,1280]{1,0:T(8,128)(2,1)}, u32[]{:S(2)}, u32[]{:S(2)}) collective-permute-start(bf16[160,1280]{1,0:T(8,128)(2,1)} %collective-permute-done.76), channel_id=1, source_target_pairs={{0,8},{4,12},{8,16},{12,20},{16,24},{20,28},{24,0},{28,4},{1,9},{5... | collective-permute-start | bytes 1228808 | tf_op jit(solution)/shard_map/ppermute | solution.py:49
  465.1 38.6 %collective-permute-start.64 = (bf16[160,1280]{1,0:T(8,128)(2,1)}, bf16[160,1280]{1,0:T(8,128)(2,1)}, u32[]{:S(2)}, u32[]{:S(2)}) collective-permute-start(bf16[160,1280]{1,0:T(8,128)(2,1)} %collective-permute-done.62), channel_id=1, source_target_pairs={{0,8},{4,12},{8,16},{12,20},{16,24},{20,28},{24,0},{28,4},{1,9},{5... | collective-permute-start | bytes 1228808 | tf_op jit(solution)/shard_map/ppermute | solution.py:49
  503.7 35.0 %collective-permute-start.71 = (bf16[160,1280]{1,0:T(8,128)(2,1)}, bf16[160,1280]{1,0:T(8,128)(2,1)S(1)}, u32[]{:S(2)}, u32[]{:S(2)}) collective-permute-start(bf16[160,1280]{1,0:T(8,128)(2,1)} %collective-permute-done.69), channel_id=1, source_target_pairs={{0,8},{4,12},{8,16},{12,20},{16,24},{20,28},{24,0},{28,4},{1,9},{5... | collective-permute-start | bytes 1228808 | tf_op jit(solution)/shard_map/ppermute | solution.py:49
  527.4 34.0 %collective-permute-start.79 = (bf16[160,1280]{1,0:T(8,128)(2,1)}, bf16[160,1280]{1,0:T(8,128)(2,1)S(1)}, u32[]{:S(2)}, u32[]{:S(2)}) collective-permute-start(bf16[160,1280]{1,0:T(8,128)(2,1)} %collective-permute-done.78), channel_id=1, source_target_pairs={{0,4},{4,0},{8,12},{12,8},{16,20},{20,16},{24,28},{28,24},{1,5},{5... | collective-permute-start | bytes 1228808 | tf_op jit(solution)/shard_map/ppermute | solution.py:32
  596.5 46.3 %collective-permute-start.147 = (bf16[4,160,1280]{2,1,0:T(8,128)(2,1)}, bf16[4,160,1280]{2,1,0:T(8,128)(2,1)}, u32[]{:S(2)}, u32[]{:S(2)}) collective-permute-start(bf16[4,160,1280]{2,1,0:T(8,128)(2,1)} %dynamic-slice_bitcast_fusion), channel_id=1, source_target_pairs={{0,4},{4,0},{8,12},{12,8},{16,20},{20,16},{24,28},{28,24},{1,5},{5... | collective-permute-start | bytes 4915208 | tf_op jit(solution)/shard_map/ppermute | solution.py:32
  601.9 68.6 %collective-permute-start.139 = (bf16[4,160,1280]{2,1,0:T(8,128)(2,1)}, bf16[4,160,1280]{2,1,0:T(8,128)(2,1)}, u32[]{:S(2)}, u32[]{:S(2)}) collective-permute-start(bf16[4,160,1280]{2,1,0:T(8,128)(2,1)} %dynamic-slice_bitcast_fusion.2), channel_id=1, source_target_pairs={{0,4},{4,0},{8,12},{12,8},{16,20},{20,16},{24,28},{28,24},{1,5},{5... | collective-permute-start | bytes 4915208 | tf_op jit(solution)/shard_map/ppermute | solution.py:32
  634.9 86.8 %collective-permute-start.22 = (f32[160,512]{1,0:T(8,128)}, f32[160,512]{1,0:T(8,128)S(1)}, u32[]{:S(2)}, u32[]{:S(2)}) collective-permute-start(f32[160,512]{1,0:T(8,128)} %get-tuple-element.246), channel_id=1, source_target_pairs={{0,4},{4,0},{8,12},{12,8},{16,20},{20,16},{24,28},{28,24},{1,5},{5... | collective-permute-start | bytes 983048 | tf_op jit(solution)/shard_map/ppermute | solution.py:32
  640.0 72.1 %collective-permute-start.143 = (bf16[4,160,1280]{2,1,0:T(8,128)(2,1)}, bf16[4,160,1280]{2,1,0:T(8,128)(2,1)S(1)}, u32[]{:S(2)}, u32[]{:S(2)}) collective-permute-start(bf16[4,160,1280]{2,1,0:T(8,128)(2,1)} %dynamic-slice_bitcast_fusion.1), channel_id=1, source_target_pairs={{0,4},{4,0},{8,12},{12,8},{16,20},{20,16},{24,28},{28,24},{1,5},{5... | collective-permute-start | bytes 4915208 | tf_op jit(solution)/shard_map/ppermute | solution.py:32
  642.8 81.0 %collective-permute-start.83 = (bf16[256,1280]{0,1:T(8,128)(2,1)S(1)}, bf16[256,1280]{0,1:T(8,128)(2,1)S(1)}, u32[]{:S(2)}, u32[]{:S(2)}) collective-permute-start(bf16[256,1280]{0,1:T(8,128)(2,1)S(1)} %maximum_select_fusion.26), channel_id=1, source_target_pairs={{0,1},{1,0},{2,3},{3,2},{4,5},{5,4},{6,7},{7,6},{8,9},{9,8},{10,11... | collective-permute-start | bytes 1966088 | tf_op jit(solution)/shard_map/ppermute | solution.py:32
  670.5 43.1 %collective-permute-start.92 = (bf16[256,1280]{0,1:T(8,128)(2,1)S(1)}, bf16[256,1280]{0,1:T(8,128)(2,1)S(1)}, u32[]{:S(2)}, u32[]{:S(2)}) collective-permute-start(bf16[256,1280]{0,1:T(8,128)(2,1)S(1)} %maximum_select_fusion.28), channel_id=1, source_target_pairs={{0,1},{1,0},{2,3},{3,2},{4,5},{5,4},{6,7},{7,6},{8,9},{9,8},{10,11... | collective-permute-start | bytes 1966088 | tf_op jit(solution)/shard_map/ppermute | solution.py:32
  735.3 43.1 %collective-permute-start.93 = (bf16[256,1280]{0,1:T(8,128)(2,1)S(1)}, bf16[256,1280]{0,1:T(8,128)(2,1)S(1)}, u32[]{:S(2)}, u32[]{:S(2)}) collective-permute-start(bf16[256,1280]{0,1:T(8,128)(2,1)S(1)} %constant_dynamic-slice_fusion.10), channel_id=1, source_target_pairs={{0,1},{1,0},{2,3},{3,2},{4,5},{5,4},{6,7},{7,6},{8,9},{9,8},{10,11... | collective-permute-start | bytes 1966088 | tf_op jit(solution)/shard_map/ppermute | solution.py:32
  737.2 39.4 %collective-permute-start.149 = (bf16[160,1280]{1,0:T(8,128)(2,1)S(1)}, bf16[160,1280]{1,0:T(8,128)(2,1)S(1)}, u32[]{:S(2)}, u32[]{:S(2)}) collective-permute-start(bf16[160,1280]{1,0:T(8,128)(2,1)S(1)} %fusion.69), channel_id=1, source_target_pairs={{0,8},{4,12},{8,16},{12,20},{16,24},{20,28},{24,0},{28,4},{1,9},{5... | collective-permute-start | bytes 1228808 | tf_op jit(solution)/shard_map/ppermute | solution.py:49
  738.8 38.8 %collective-permute-start.141 = (bf16[160,1280]{1,0:T(8,128)(2,1)S(1)}, bf16[160,1280]{1,0:T(8,128)(2,1)S(1)}, u32[]{:S(2)}, u32[]{:S(2)}) collective-permute-start(bf16[160,1280]{1,0:T(8,128)(2,1)S(1)} %fusion.75), channel_id=1, source_target_pairs={{0,8},{4,12},{8,16},{12,20},{16,24},{20,28},{24,0},{28,4},{1,9},{5... | collective-permute-start | bytes 1228808 | tf_op jit(solution)/shard_map/ppermute | solution.py:49
  777.5 104.8 %collective-permute-start.150 = (bf16[160,1280]{1,0:T(8,128)(2,1)}, bf16[160,1280]{1,0:T(8,128)(2,1)}, u32[]{:S(2)}, u32[]{:S(2)}) collective-permute-start(bf16[160,1280]{1,0:T(8,128)(2,1)} %fusion.68), channel_id=1, source_target_pairs={{0,8},{4,12},{8,16},{12,20},{16,24},{20,28},{24,0},{28,4},{1,9},{5... | collective-permute-start | bytes 1228808 | tf_op jit(solution)/shard_map/ppermute | solution.py:49
  777.7 29.5 %collective-permute-start.142 = (bf16[160,1280]{1,0:T(8,128)(2,1)S(1)}, bf16[160,1280]{1,0:T(8,128)(2,1)S(1)}, u32[]{:S(2)}, u32[]{:S(2)}) collective-permute-start(bf16[160,1280]{1,0:T(8,128)(2,1)S(1)} %fusion.74), channel_id=1, source_target_pairs={{0,8},{4,12},{8,16},{12,20},{16,24},{20,28},{24,0},{28,4},{1,9},{5... | collective-permute-start | bytes 1228808 | tf_op jit(solution)/shard_map/ppermute | solution.py:49
  830.2 58.0 %collective-permute-start.131 = (bf16[4,160,1280]{2,1,0:T(8,128)(2,1)}, bf16[4,160,1280]{2,1,0:T(8,128)(2,1)}, u32[]{:S(2)}, u32[]{:S(2)}) collective-permute-start(bf16[4,160,1280]{2,1,0:T(8,128)(2,1)} %dynamic-slice_bitcast_fusion.3), channel_id=1, source_target_pairs={{0,4},{4,0},{8,12},{12,8},{16,20},{20,16},{24,28},{28,24},{1,5},{5... | collective-permute-start | bytes 4915208 | tf_op jit(solution)/shard_map/ppermute | solution.py:32
  843.0 35.7 %collective-permute-start.97 = (bf16[512,640]{0,1:T(8,128)(2,1)S(1)}, bf16[512,640]{0,1:T(8,128)(2,1)S(1)}, u32[]{:S(2)}, u32[]{:S(2)}) collective-permute-start(bf16[512,640]{0,1:T(8,128)(2,1)S(1)} %pad_maximum_fusion.7), channel_id=1, source_target_pairs={{0,4},{4,0},{8,12},{12,8},{16,20},{20,16},{24,28},{28,24},{1,5},{5... | collective-permute-start | bytes 1966088 | tf_op jit(solution)/shard_map/ppermute | solution.py:32
  891.9 33.6 %collective-permute-start.132 = (bf16[160,1280]{1,0:T(8,128)(2,1)}, bf16[160,1280]{1,0:T(8,128)(2,1)}, u32[]{:S(2)}, u32[]{:S(2)}) collective-permute-start(bf16[160,1280]{1,0:T(8,128)(2,1)} %dynamic-slice_bitcast_fusion.14), channel_id=1, source_target_pairs={{0,8},{4,12},{8,16},{12,20},{16,24},{20,28},{24,0},{28,4},{1,9},{5... | collective-permute-start | bytes 1228808 | tf_op jit(solution)/shard_map/ppermute | solution.py:49
  922.7 67.7 %collective-permute-start.127 = (bf16[4,160,1280]{2,1,0:T(8,128)(2,1)}, bf16[4,160,1280]{2,1,0:T(8,128)(2,1)}, u32[]{:S(2)}, u32[]{:S(2)}) collective-permute-start(bf16[4,160,1280]{2,1,0:T(8,128)(2,1)} %dynamic-slice_bitcast_fusion.4), channel_id=1, source_target_pairs={{0,4},{4,0},{8,12},{12,8},{16,20},{20,16},{24,28},{28,24},{1,5},{5... | collective-permute-start | bytes 4915208 | tf_op jit(solution)/shard_map/ppermute | solution.py:32
  941.3 53.2 %collective-permute-start.134 = (bf16[160,1280]{1,0:T(8,128)(2,1)}, bf16[160,1280]{1,0:T(8,128)(2,1)S(1)}, u32[]{:S(2)}, u32[]{:S(2)}) collective-permute-start(bf16[160,1280]{1,0:T(8,128)(2,1)} %fusion.76), channel_id=1, source_target_pairs={{0,8},{4,12},{8,16},{12,20},{16,24},{20,28},{24,0},{28,4},{1,9},{5... | collective-permute-start | bytes 1228808 | tf_op jit(solution)/shard_map/ppermute | solution.py:49
  982.4 34.1 %collective-permute-start.120 = (bf16[320,1440]{1,0:T(8,128)(2,1)S(1)}, bf16[320,1440]{1,0:T(8,128)(2,1)S(1)}, u32[]{:S(2)}, u32[]{:S(2)}) collective-permute-start(bf16[320,1440]{1,0:T(8,128)(2,1)S(1)} %dynamic-slice_bitcast_fusion.7), channel_id=1, source_target_pairs={{0,8},{4,12},{8,16},{12,20},{16,24},{20,28},{24,0},{28,4},{1,9},{5... | collective-permute-start | bytes 2764808 | tf_op jit(solution)/shard_map/ppermute | solution.py:49
  990.3 29.2 %collective-permute-start.105 = (bf16[2,2,160,1024]{3,2,1,0:T(8,128)(2,1)S(1)}, bf16[2,2,160,1024]{3,2,1,0:T(8,128)(2,1)S(1)}, u32[]{:S(2)}, u32[]{:S(2)}) collective-permute-start(bf16[2,2,160,1024]{3,2,1,0:T(8,128)(2,1)S(1)} %dynamic-slice_bitcast_fusion.6), channel_id=1, source_target_pairs={{0,1},{1,0},{2,3},{3,2},{4,5},{5,4},{6,7},{7,6},{8,9},{9,8},{10,11... | collective-permute-start | bytes 3932168 | tf_op jit(solution)/shard_map/ppermute | solution.py:32
  1018.0 51.6 %collective-permute-start.121 = (bf16[320,1440]{1,0:T(8,128)(2,1)S(1)}, bf16[320,1440]{1,0:T(8,128)(2,1)S(1)}, u32[]{:S(2)}, u32[]{:S(2)}) collective-permute-start(bf16[320,1440]{1,0:T(8,128)(2,1)S(1)} %fusion.29), channel_id=1, source_target_pairs={{0,8},{4,12},{8,16},{12,20},{16,24},{20,28},{24,0},{28,4},{1,9},{5... | collective-permute-start | bytes 2764808 | tf_op jit(solution)/shard_map/ppermute | solution.py:49
  1031.0 29.2 %collective-permute-start.109 = (bf16[160,512]{1,0:T(8,128)(2,1)S(1)}, bf16[160,512]{1,0:T(8,128)(2,1)S(1)}, u32[]{:S(2)}, u32[]{:S(2)}) collective-permute-start(bf16[160,512]{1,0:T(8,128)(2,1)S(1)} %fusion.136), channel_id=1, source_target_pairs={{0,4},{4,0},{8,12},{12,8},{16,20},{20,16},{24,28},{28,24},{1,5},{5... | collective-permute-start | bytes 491528 | tf_op jit(solution)/shard_map/ppermute | solution.py:32
  1032.1 28.1 %collective-permute-start.107 = (bf16[160,512]{1,0:T(8,128)(2,1)S(1)}, bf16[160,512]{1,0:T(8,128)(2,1)S(1)}, u32[]{:S(2)}, u32[]{:S(2)}) collective-permute-start(bf16[160,512]{1,0:T(8,128)(2,1)S(1)} %fusion.135), channel_id=1, source_target_pairs={{0,2},{1,3},{2,0},{3,1},{4,6},{5,7},{6,4},{7,5},{8,10},{9,11},{10,... | collective-permute-start | bytes 491528 | tf_op jit(solution)/shard_map/ppermute | solution.py:32
  1069.5 31.6 %collective-permute-start.110 = (bf16[2,2,160,1024]{3,2,1,0:T(8,128)(2,1)}, bf16[2,2,160,1024]{3,2,1,0:T(8,128)(2,1)}, u32[]{:S(2)}, u32[]{:S(2)}) collective-permute-start(bf16[2,2,160,1024]{3,2,1,0:T(8,128)(2,1)} %dynamic-slice_bitcast_fusion.5), channel_id=1, source_target_pairs={{0,1},{1,0},{2,3},{3,2},{4,5},{5,4},{6,7},{7,6},{8,9},{9,8},{10,11... | collective-permute-start | bytes 3932168 | tf_op jit(solution)/shard_map/ppermute | solution.py:32
  1085.1 33.0 %collective-permute-start.116 = (bf16[320,1440]{1,0:T(8,128)(2,1)S(1)}, bf16[320,1440]{1,0:T(8,128)(2,1)S(1)}, u32[]{:S(2)}, u32[]{:S(2)}) collective-permute-start(bf16[320,1440]{1,0:T(8,128)(2,1)S(1)} %dynamic-slice_bitcast_fusion.8), channel_id=1, source_target_pairs={{0,8},{4,12},{8,16},{12,20},{16,24},{20,28},{24,0},{28,4},{1,9},{5... | collective-permute-start | bytes 2764808 | tf_op jit(solution)/shard_map/ppermute | solution.py:49
  (295 other events, 4754.4 us)

commit v2 on v1

--- a/solution.py
+++ b/solution.py
@@ -4,6 +4,7 @@
 import jax.numpy as jnp
 from jax import lax
 from jax.experimental import pallas as pl
+from jax.experimental.layout import Layout, with_layout_constraint
 from jax.sharding import PartitionSpec as P
 from jax.experimental.pallas import tpu as pltpu
 
@@ -28,6 +29,10 @@
     ).astype(kind)
 
 
+def row_major(x):
+    return with_layout_constraint(x, Layout(tuple(range(x.ndim))))
+
+
 def swap(x, axis, mask):
     return lax.ppermute(x, axis, [(i, i ^ mask) for i in range(lax.axis_size(axis))])
 
@@ -44,9 +49,9 @@
     return swap(x, "heads", 2)
 
 
-def shift_image(x):
+def shift_image(x, images=1):
     n = lax.axis_size("rows")
-    return lax.ppermute(x, "rows", [(i, (i + 2) % n) for i in range(n)])
+    return lax.ppermute(x, "rows", [(i, (i + 2 * images) % n) for i in range(n)])
 
 
 def pair(own, other, place, axis):
@@ -101,22 +106,37 @@
     return whole
 
 
-def rows_gather(at, chunk):
-    n, size = at.images, chunk.shape[0]
+def rows_gather(chunk):
+    return lax.all_gather(chunk, "rows", axis=0, tiled=True)
+
+
+def rows_scatter(grad):
+    return lax.psum_scatter(grad, "rows", scatter_dimension=0, tiled=True).astype(F32)
+
+
+def small_gather(at, x):
+    n = at.images
     if n > UNROLL:
-        own = image_gather(at, chunk)
-        split = (n, 1) + chunk.shape
-        both = pair(own.reshape(split), swap_half(own).reshape(split), at.half, 1)
-        return both.reshape((2 * n * size,) + chunk.shape[1:])
-    whole = jnp.zeros((2 * n * size,) + chunk.shape[1:], chunk.dtype)
+        return image_gather(at, x[None])
+    whole = jnp.zeros((n,) + x.shape, x.dtype)
     for step in range(n):
-        start = lax.rem(at.image - step + n, n) * 2
-        other = swap_half(chunk)
-        whole = lax.dynamic_update_slice_in_dim(whole, chunk, (start + at.half) * size, 0)
-        whole = lax.dynamic_update_slice_in_dim(whole, other, (start + 1 - at.half) * size, 0)
-        if step < n - 1:
-            chunk = shift_image(chunk)
+        other = shift_image(x, step) if step else x
+        start = lax.rem(at.image - step + n, n)
+        whole = lax.dynamic_update_index_in_dim(whole, other, start, 0)
     return whole
+
+
+def small_scatter(at, blocks):
+    n = at.images
+    if n > UNROLL:
+        return image_scatter(at, blocks)
+    total = lax.dynamic_index_in_dim(blocks, at.image, 0, keepdims=False).astype(F32)
+    for step in range(1, n):
+        block = lax.dynamic_index_in_dim(
+            blocks, lax.rem(at.image + step, n), 0, keepdims=False
+        )
+        total = total + shift_image(block, step).astype(F32)
+    return total
 
 
 def image_scatter(at, blocks):
@@ -141,11 +161,38 @@
     return advance(n - 2, moving)
 
 
-def rows_scatter(at, grad):
-    blocks = grad.reshape((at.images, 2, -1) + grad.shape[1:])
-    other = swap_half(pick(blocks, 1 - at.half, 1))
-    summed = (pick(blocks, at.half, 1).astype(F32) + other.astype(F32)).astype(BF16)
-    return image_scatter(at, summed)
+def image_spread(at, chunk):
+    if at.images != 4:
+        return image_gather(at, chunk)
+    size = chunk.shape[0]
+    up, down = shift_image(chunk, 1), shift_image(chunk, 3)
+    far = (shift_image(up[: size // 2], 1), shift_image(down[size // 2 :], 3))
+    whole = jnp.concatenate([chunk] * 4, axis=0)
+    for move, block in ((3, up), (1, down), (2, jnp.concatenate(far, axis=0))):
+        start = lax.rem(at.image + move, 4) * size
+        whole = lax.dynamic_update_slice_in_dim(whole, block, start, 0)
+    return whole
+
+
+def add_low(a, b):
+    return (a.astype(F32) + b.astype(F32)).astype(BF16)
+
+
+def image_total(at, blocks):
+    if at.images != 4:
+        return image_scatter(at, blocks)
+
+    def local(move):
+        place = lax.rem(at.image + move, 4)
+        return lax.dynamic_index_in_dim(blocks, place, 0, keepdims=False)
+
+    size = blocks.shape[1] // 2
+    far, up, down = local(2), local(1), local(3)
+    first, second = shift_image(far[:size], 1), shift_image(far[size:], 3)
+    up = jnp.concatenate([add_low(up[:size], first), up[size:]], axis=0)
+    down = jnp.concatenate([down[:size], add_low(down[size:], second)], axis=0)
+    up, down = shift_image(up, 1), shift_image(down, 3)
+    return local(0).astype(F32) + up.astype(F32) + down.astype(F32)
 
 
 def rows_total(x, first=1):
@@ -306,29 +353,39 @@
     return (tap // 3 - 1) * columns + tap % 3 - 1
 
 
-def tap_sum_kernel(columns, taps_ref, sum_ref):
-    tokens = taps_ref.shape[2]
-    total = taps_ref[4]
-    for tap in range(TAPS):
-        if tap != 4:
-            moved = pltpu.roll(taps_ref[tap], -tap_offset(tap, columns) % tokens, 1)
-            total = total + jnp.where(tap_mask(moved.shape, tap, columns), moved, 0.0)
-    sum_ref[...] = total
-
-
-def tap_sum(taps, columns):
-    tokens = taps.shape[1]
-    width = taps.shape[0] // TAPS
-    block = 32
+def conv_kernel(columns, weights_ref, acts_ref, sum_ref, taps_ref):
+    width, tokens = sum_ref.shape
+    acts = acts_ref[...]
+    for start in range(0, TAPS * width, 256):
+        cut = slice(start, min(start + 256, TAPS * width))
+        taps_ref[cut, :] = lax.dot_general(
+            weights_ref[:, cut], acts, (((0,), (0,)), ((), ())), preferred_element_type=F32
+        )
+    for start in range(0, width, 32):
+        total = taps_ref[4 * width + start : 4 * width + start + 32, :]
+        for tap in range(TAPS):
+            if tap != 4:
+                taps = taps_ref[tap * width + start : tap * width + start + 32, :]
+                moved = pltpu.roll(taps, -tap_offset(tap, columns) % tokens, 1)
+                total = total + jnp.where(tap_mask(moved.shape, tap, columns), moved, 0.0)
+        sum_ref[start : start + 32, :] = total
+
+
+def conv_forward(weights, acts, columns):
+    tokens = acts.shape[1]
+    width = weights.shape[1] // TAPS
     return pl.pallas_call(
-        lambda *refs: tap_sum_kernel(columns, *refs),
-        grid=(width // block,),
-        in_specs=[pl.BlockSpec((TAPS, block, tokens), lambda i: (0, i, 0))],
-        out_specs=pl.BlockSpec((block, tokens), lambda i: (i, 0)),
+        lambda *refs: conv_kernel(columns, *refs),
+        in_specs=[pl.BlockSpec(memory_space=pltpu.VMEM)] * 2,
+        out_specs=pl.BlockSpec(memory_space=pltpu.VMEM),
         out_shape=jax.ShapeDtypeStruct((width, tokens), F32),
-        compiler_params=pltpu.CompilerParams(vmem_limit_bytes=16 * 2**20),
-        name="tap_sum",
-    )(taps.reshape(TAPS, width, tokens))
+        scratch_shapes=[pltpu.VMEM((TAPS * width, tokens), F32)],
+        compiler_params=pltpu.CompilerParams(vmem_limit_bytes=40 * 2**20),
+        cost_estimate=pl.CostEstimate(
+            flops=2 * weights.size * tokens, bytes_accessed=2 * weights.size, transcendentals=0
+        ),
+        name="conv_forward",
+    )(weights, acts)
 
 
 def tap_spread_kernel(columns, grad_ref, taps_ref):
@@ -357,20 +414,65 @@
     )(grad).reshape(TAPS * width, tokens)
 
 
-def conv_weights(at, kernel):
-    inputs, outputs = kernel.shape[2:]
-    halves = kernel.reshape(TAPS, inputs, 2, outputs // 2).transpose(2, 1, 0, 3)
-    halves = halves.reshape(2, inputs, -1)
+def pack_kernel(kernel_ref, halves_ref):
+    half = kernel_ref.shape[2] // 2
+    taps = [kernel_ref[tap].astype(F32) for tap in range(TAPS)]
+    for side in range(2):
+        row = jnp.concatenate([tap[:, side * half : (side + 1) * half] for tap in taps], axis=1)
+        halves_ref[side] = row.astype(halves_ref.dtype)
+
+
+def pack(kernel):
+    taps, inputs, outputs = kernel.shape
+    block = 32 if inputs % 32 == 0 else inputs
+    return pl.pallas_call(
+        pack_kernel,
+        grid=(inputs // block,),
+        in_specs=[pl.BlockSpec((taps, block, outputs), lambda i: (0, i, 0))],
+        out_specs=pl.BlockSpec((2, block, taps * outputs // 2), lambda i: (0, i, 0)),
+        out_shape=jax.ShapeDtypeStruct((2, inputs, taps * outputs // 2), kernel.dtype),
+        compiler_params=pltpu.CompilerParams(vmem_limit_bytes=16 * 2**20),
+        name="conv_pack",
+    )(kernel)
+
+
+def unpack_kernel(side_ref, own_ref, other_ref, kernel_ref):
+    half = kernel_ref.shape[2] // 2
+    first = side_ref[0] == 0
+    own, other = own_ref[...], other_ref[...].astype(F32)
+    low, high = jnp.where(first, own, other), jnp.where(first, other, own)
+    for tap in range(TAPS):
+        cut = slice(tap * half, (tap + 1) * half)
+        kernel_ref[tap] = jnp.concatenate([low[:, cut], high[:, cut]], axis=1)
+
+
+def unpack(side, own, other):
+    inputs, width = own.shape
+    outputs = 2 * width // TAPS
+    block = 32 if inputs % 32 == 0 else inputs
+    rows = pl.BlockSpec((block, width), lambda i: (i, 0))
+    return pl.pallas_call(
+        unpack_kernel,
+        grid=(inputs // block,),
+        in_specs=[pl.BlockSpec(memory_space=pltpu.SMEM), rows, rows],
+        out_specs=pl.BlockSpec((TAPS, block, outputs), lambda i: (0, i, 0)),
+        out_shape=jax.ShapeDtypeStruct((TAPS, inputs, outputs), F32),
+        compiler_params=pltpu.CompilerParams(vmem_limit_bytes=16 * 2**20),
+        name="conv_unpack",
+    )(side.astype(jnp.int32)[None], own, other)
+
+
+def conv_chunk(at, kernel):
+    halves = pack(kernel.reshape((TAPS,) + kernel.shape[2:]))
     other = swap_half(pick(halves, 1 - at.half, 0))
-    return image_gather(at, pair(pick(halves, at.half, 0), other, at.half, 0))
+    return row_major(pair(pick(halves, at.half, 0), other, at.half, 0))
 
 
 def conv_weights_back(at, grad, inputs):
-    total = image_scatter(at, grad.reshape(at.images, 2 * inputs, -1))
-    other = swap_half(part(total, 1 - at.half, 2).astype(BF16)).astype(F32)
-    own = part(total, at.half, 2).reshape(inputs, TAPS, -1)
-    grad = pair(own, other.reshape(inputs, TAPS, -1), at.half, 2)
-    return grad.transpose(1, 0, 2).reshape(3, 3, inputs, -1)
+    total = image_total(at, grad.reshape(at.images, 2 * inputs, -1))
+    other = swap_half(part(total, 1 - at.half, 2).astype(BF16))
+    grad = unpack(at.half, part(total, at.half, 2), other)
+    return grad.reshape((3, 3) + grad.shape[1:])
 
 
 def by_heads(x):
@@ -465,23 +567,6 @@
     inputs = time_w.shape[0]
     hidden = ff_in_w.shape[2]
 
-    conv_one = conv_weights(at, conv1_w)
-    conv_two = conv_weights(at, conv2_w)
-    w_first = rows_gather(
-        at,
-        jnp.concatenate([qkv_w[:, 1], qkv_w[:, 2], qkv_w[:, 0], proj_in_w], axis=1),
-    )
-    w_kvq, w_in = w_first[:, : 3 * width], w_first[:, 3 * width :]
-    w_second = rows_gather(
-        at, jnp.concatenate([self_out_w.T, cross_q_w, cross_out_w.T, proj_out_w], axis=1)
-    )
-    w_self, w_query, w_cross, w_out = (
-        w_second[:, i * width : (i + 1) * width] for i in range(4)
-    )
-    w_value = rows_gather(at, ff_in_w[:, 0])
-    w_gate = rows_gather(at, ff_in_w[:, 1])
-    w_narrow = rows_gather(at, ff_out_w.T)
-
     own_params = jnp.concatenate([ln_params.reshape(6, width), biases[4:7]], axis=0)
     wide = pair(own_params, swap_core(own_params), at.core, 1)
     wide = pair(wide, swap_far(wide), at.far, 1)
@@ -504,27 +589,55 @@
     text_own = part(text, at.row, lax.axis_size("rows"), 2)
     pair_w = cross_kv_w.reshape(cross_kv_w.shape[0], -1)
     kv_part = jnp.einsum("isc,cd->isd", text_own, pair_w, preferred_element_type=F32)
-    kv_part = (kv_part + swap_half(kv_part.astype(BF16)).astype(F32)).astype(BF16)
-    cross_kv = image_scatter(at, kv_part).astype(BF16)
+    kv_image = small_scatter(at, kv_part.astype(BF16))
+
+    source = to_image(at, latents.reshape(tokens, width).T).astype(F32)
+    norm_one, stored_one = group_forward(source, gn_own[0, 0], gn_own[0, 1], EPS_RES)
+
+    chunk_one = conv_chunk(at, conv1_w)
+    chunk_two = conv_chunk(at, conv2_w)
+    square = jnp.concatenate(
+        [
+            qkv_w[:, 1],
+            qkv_w[:, 2],
+            qkv_w[:, 0],
+            proj_in_w,
+            self_out_w.T,
+            cross_q_w,
+            cross_out_w.T,
+            proj_out_w,
+        ],
+        axis=1,
+    )
+    wide = jnp.concatenate([ff_in_w[:, 0], ff_in_w[:, 1], ff_out_w.T], axis=1)
+    cross_kv = (kv_image + swap_half(kv_image.astype(BF16)).astype(F32)).astype(BF16)
     cross_keys, cross_values = cross_kv[:, :width], cross_kv[:, width:]
-
-    source = to_image(at, latents.reshape(tokens, width).T).astype(F32)
+    conv_one = row_major(image_spread(at, chunk_one))
+    conv_two = row_major(image_spread(at, chunk_two))
+    low_one = jax.nn.silu(norm_one).astype(BF16)
+    w_square = rows_gather(square)
+    w_kvq, w_rest = w_square[:, : 3 * width], w_square[:, 3 * width :]
+    w_in, w_self, w_query, w_cross, w_out = (
+        w_rest[:, i * width : (i + 1) * width] for i in range(5)
+    )
+    w_wide = rows_gather(wide)
+    w_value, w_gate, w_narrow = (w_wide[:, i * hidden : (i + 1) * hidden] for i in range(3))
+
     cot_rows = cotangent.reshape(tokens, width)
     cot_image = to_image(at, cot_rows.T).astype(F32)
-    norm_one, stored_one = group_forward(source, gn_own[0, 0], gn_own[0, 1], EPS_RES)
-    act_one = plane_gather(at, jax.nn.silu(norm_one).astype(BF16))
-    hidden_two = tap_sum(dot(conv_one, act_one, 0, 0), columns)
+    act_one = plane_gather(at, low_one)
+    hidden_two = conv_forward(conv_one, act_one, columns)
     hidden_two = hidden_two + (bias_own[0] + shift_time)[:, None]
     norm_two, stored_two = group_forward(hidden_two, gn_own[1, 0], gn_own[1, 1], EPS_RES)
     act_two = plane_gather(at, jax.nn.silu(norm_two).astype(BF16))
-    resid = source + tap_sum(dot(conv_two, act_two, 0, 0), columns) + bias_own[2][:, None]
+    resid = source + conv_forward(conv_two, act_two, columns) + bias_own[2][:, None]
     norm_three, stored_three = group_forward(resid, gn_own[2, 0], gn_own[2, 1], EPS_MID)
     gin = channel_rows_gather(at, from_image(at, norm_three.astype(BF16)))
     resid_own = from_image(at, resid)
 
     stream_zero = to_tokens(at, dot(gin, w_in, 0, 0) + biases[3])
-    low_one, stored_ln_one = layer_forward(stream_zero, ln_wide[0])
-    n_one = heads_gather(at, low_one)
+    ln_low_one, stored_ln_one = layer_forward(stream_zero, ln_wide[0])
+    n_one = heads_gather(at, ln_low_one)
     kv_own = dot(n_one, w_kvq[:, : 2 * width], 1, 0, BF16)
     kv_other = swap_half(kv_own)
     queries = dot(n_one, w_kvq[:, 2 * width :], 1, 0, BF16)
@@ -556,7 +669,7 @@
     grad_three = heads_scatter(at, dot(cot_rows, w_out, 1, 1, BF16))
     low_ff = grad_three.astype(BF16)
     grad_ff = heads_gather(at, low_ff)
-    narrow_grad = dot(grad_ff, mixed, 0, 0, BF16)
+    narrow_grad = row_major(dot(grad_ff, mixed, 0, 0, BF16))
     grad_mixed = dot(grad_ff, w_narrow, 1, 0, BF16).astype(F32)
     pdf = jnp.exp(-0.5 * gate_in * gate_in) / math.sqrt(2.0 * math.pi)
     grad_value = (grad_mixed * gelu).astype(BF16)
@@ -564,10 +677,11 @@
     ffbias_grad = jnp.stack(
         [jnp.sum(grad_value.astype(F32), axis=0), jnp.sum(grad_gate.astype(F32), axis=0)]
     )
-    value_grad = dot(n_three, grad_value, 0, 0, BF16)
-    gate_grad = dot(n_three, grad_gate, 0, 0, BF16)
     grad_ln = heads_scatter(
         at, (dot(grad_value, w_value, 1, 1) + dot(grad_gate, w_gate, 1, 1)).astype(BF16)
+    )
+    wide_grad = row_major(
+        dot(n_three, jnp.concatenate([grad_value, grad_gate], axis=1), 0, 0, BF16)
     )
     back, ln_grad_three = layer_backward(grad_ln, ln_wide[2], stored_ln_three)
     grad_two = grad_three + back
@@ -579,7 +693,7 @@
     grad_cq, (grad_ckv,) = attend_back(grad_cross_att, cross_query, cross_blocks, log_cross)
     query_grad = dot(n_two, grad_cq, 0, 0, BF16)
     grad_ckv = (grad_ckv + swap_half(grad_ckv.astype(BF16)).astype(F32)).astype(BF16)
-    grad_ckv = image_gather(at, grad_ckv[None])
+    grad_ckv = small_gather(at, grad_ckv)
     pair_grad = jnp.einsum("isc,isd->cd", text_own, grad_ckv, preferred_element_type=F32)
     grad_ln = heads_scatter(at, dot(grad_cq, w_query, 1, 1, BF16))
     back, ln_grad_two = layer_backward(grad_ln, ln_wide[1], stored_ln_two)
@@ -609,7 +723,7 @@
     bias_two = jnp.sum(grad_c_two.astype(F32), axis=1)
     spread_two = tap_spread(grad_c_two, columns)
     grad_act = plane_scatter(at, dot(conv_two, spread_two, 1, 0, BF16))
-    conv_two_grad = dot(act_two, spread_two, 1, 1, BF16)
+    conv_two_grad = row_major(dot(act_two, spread_two, 1, 1, BF16))
     grad_hidden, gn_grad_two = group_backward(
         grad_act * silu_slope(norm_two), gn_own[1, 0], stored_two
     )
@@ -618,19 +732,23 @@
     bias_zero = jnp.sum(grad_c_one.astype(F32), axis=1)
     spread_one = tap_spread(grad_c_one, columns)
     grad_act = plane_scatter(at, dot(conv_one, spread_one, 1, 0, BF16))
-    conv_one_grad = dot(act_one, spread_one, 1, 1, BF16)
+    conv_one_grad = row_major(dot(act_one, spread_one, 1, 1, BF16))
     back, gn_grad_one = group_backward(
         grad_act * silu_slope(norm_one), gn_own[0, 0], stored_one
     )
     latents_grad = from_image(at, grad_resid + back).T.reshape(latents.shape)
 
-    second = rows_scatter(
-        at, jnp.concatenate([self_grad, query_grad, cross_grad, out_grad], axis=1)
-    )
-    narrow = rows_scatter(at, narrow_grad)
-    value = rows_scatter(at, value_grad)
-    gate = rows_scatter(at, gate_grad)
-    first = rows_scatter(at, jnp.concatenate([kvq_grad, in_grad], axis=1))
+    narrow = rows_scatter(narrow_grad)
+    wide_out = rows_scatter(wide_grad)
+    value, gate = wide_out[:, :hidden], wide_out[:, hidden:]
+    rest_out = rows_scatter(
+        row_major(
+            jnp.concatenate(
+                [kvq_grad, in_grad, self_grad, query_grad, cross_grad, out_grad], axis=1
+            )
+        )
+    )
+    rest = [rest_out[:, i * width : (i + 1) * width] for i in range(8)]
     conv_two_out = conv_weights_back(at, conv_two_grad, inputs)
     conv_one_out = conv_weights_back(at, conv_one_grad, inputs)
 
@@ -669,22 +787,21 @@
         preferred_element_type=F32,
     )
 
-    cut = [i * width for i in range(5)]
     return (
         output,
         latents_grad,
         conv_one_out,
         conv_two_out,
         time_grad,
-        first[:, cut[3] : cut[4]],
-        jnp.stack([first[:, cut[2] : cut[3]], first[:, : cut[1]], first[:, cut[1] : cut[2]]], axis=1),
-        second[:, : cut[1]].T,
-        second[:, cut[1] : cut[2]],
+        rest[3],
+        jnp.stack([rest[2], rest[0], rest[1]], axis=1),
+        rest[4].T,
+        rest[5],
         pair_grad.reshape(cross_kv_w.shape),
-        second[:, cut[2] : cut[3]].T,
+        rest[6].T,
         jnp.stack([value, gate], axis=1),
         narrow.T,
-        second[:, cut[3] : cut[4]],
+        rest[7],
         gn_total,
         ln_total,
         bias_total,

time: 1210 us -> 942 us (0.78)
  local copies, waits for them, and re-layouts: 310 us -> 98.6 us
  waiting for transfers between devices: 508 us -> 434 us
  between operations: 4.98 us -> 17.4 us
    dynamic_update_slice x51 -> x7, local copies, waits for them, and re-layouts: 137 us -> 0.41 us  [the longest x4 0.36 us: image_spread(): whole = lax.dynamic_update_slice_in_dim(whole, block, start, 0)]
    ppermute x108 -> x83, waiting for transfers between devices: 295 us -> 160 us  [swap(): lax.ppermute(x, axis, [(i, i ^ mask) for i in range(lax.axis_size(axis))])]
    ppermute x48 -> x22, waiting for transfers between devices: 212 us -> 271 us  [shift_image(): lax.ppermute(x, 'rows', [(i, (i + 2 * images) % n) for i in range(n)])]
    convert_element_type x24 -> x7, other arithmetic: 29.8 us -> 6.5 us  [the longest x2 2.76 us: rows_scatter(): lax.psum_scatter(grad, 'rows', scatter_dimension=0, tiled=True).astype(F32)]
    ppermute x108 -> x83, starting transfers between devices: 101 us -> 81.9 us  [swap(): lax.ppermute(x, axis, [(i, i ^ mask) for i in range(lax.axis_size(axis))])]
    reshape x6 -> x0, local copies, waits for them, and re-layouts: 19 us -> none  [the longest x4 15.3 us: conv_weights(): halves = kernel.reshape(TAPS, inputs, 2, outputs // 2).transpose(2, 1, 0, 3)]
    ppermute x48 -> x22, starting transfers between devices: 41.1 us -> 56.8 us  [shift_image(): lax.ppermute(x, 'rows', [(i, (i + 2 * images) % n) for i in range(n)])]
    ppermute x6 -> x0, local copies, waits for them, and re-layouts: 13.2 us -> none  [shift_image(): return lax.ppermute(x, 'rows', [(i, (i + 2) % n) for i in range(n)])]
  transfers between devices with their start and end apart: 156 -> 110, of which waited for: 65 -> 56; matrix products, arithmetic and copies ran while one was open for 42% -> 30% of each run, Pallas kernels for 1% -> 2%
where the time goes in v2:
time: 942 us; the launch traced here: 931 us
  waiting for transfers between devices  434 us (46%)
  starting transfers between devices  140 us (15%)
  matrix products  135 us (14%)
  local copies, waits for them, and re-layouts  98.6 us (10%)
  other arithmetic  88.1 us (9%)
  Pallas kernels  18.6 us (2%)
  between operations  17.4 us (2%)
    ppermute x22, waiting for transfers between devices, shift_image(): lax.ppermute(x, 'rows', [(i, (i + 2 * images) % n) for i in range(n)])  271 us
    ppermute x83, waiting for transfers between devices, swap(): lax.ppermute(x, axis, [(i, i ^ mask) for i in range(lax.axis_size(axis))])  160 us
    dot_general x31, matrix products, dot(): lax.dot_general(a, b, (((a_dim,), (b_dim,)), ((), ())), preferred_element...  110 us
    ppermute x83, starting transfers between devices, swap(): lax.ppermute(x, axis, [(i, i ^ mask) for i in range(lax.axis_size(axis))])  81.9 us
    ppermute x22, starting transfers between devices, shift_image(): lax.ppermute(x, 'rows', [(i, (i + 2 * images) % n) for i in range(n)])  56.8 us
    unnamed x345, local copies, waits for them, and re-layouts  19.5 us
  transfers between devices with their start and end apart: 110, of which 56 were waited for; matrix products, arithmetic and copies ran while one was open for 30% of the time, Pallas kernels for 2%

profile of v2, /device:TPU:0, one launch (start us, length us, event | category | flops | bytes accessed | tf_op | source)
XLA Modules:
  0.0 931.0 jit_solution(7002867597841846854)
XLA Ops:
  63.5 22.1 %collective-permute-done.7 = bf16[320,1440]{1,0:T(8,128)(2,1)S(1)} collective-permute-done((bf16[320,1440]{1,0:T(8,128)(2,1)S(1)}, bf16[320,1440]{1,0:T(8,128)(2,1)S(1)}, u32[]{:S(2)}, u32[]{:S(2)}) %collective-permute-start.7) | collective-permute-done | bytes 921632 | tf_op jit(solution)/shard_map/ppermute | solution.py:54
  85.7 11.2 %collective-permute-start.9 = (bf16[160,1440]{1,0:T(8,128)(2,1)S(1)}, bf16[160,1440]{1,0:T(8,128)(2,1)S(1)}, u32[]{:S(2)}, u32[]{:S(2)}) collective-permute-start(bf16[160,1440]{1,0:T(8,128)(2,1)S(1)} %slice.458), channel_id=1, source_target_pairs={{0,8},{4,12},{8,16},{12,20},{16,24},{20,28},{24,0},{28,4},{1,9},{5... | collective-permute-start | bytes 1382408 | tf_op jit(solution)/shard_map/ppermute | solution.py:54
  96.9 33.1 %collective-permute-done.8 = bf16[320,1440]{1,0:T(8,128)(2,1)S(1)} collective-permute-done((bf16[320,1440]{1,0:T(8,128)(2,1)S(1)}, bf16[320,1440]{1,0:T(8,128)(2,1)S(1)}, u32[]{:S(2)}, u32[]{:S(2)}) %collective-permute-start.8) | collective-permute-done | bytes 921632 | tf_op jit(solution)/shard_map/ppermute | solution.py:54
  130.3 10.0 %collective-permute-done.9 = bf16[160,1440]{1,0:T(8,128)(2,1)S(1)} collective-permute-done((bf16[160,1440]{1,0:T(8,128)(2,1)S(1)}, bf16[160,1440]{1,0:T(8,128)(2,1)S(1)}, u32[]{:S(2)}, u32[]{:S(2)}) %collective-permute-start.9) | collective-permute-done | bytes 460832 | tf_op jit(solution)/shard_map/ppermute | solution.py:54
  140.2 27.7 %collective-permute-done.10 = bf16[160,1440]{1,0:T(8,128)(2,1)S(1)} collective-permute-done((bf16[160,1440]{1,0:T(8,128)(2,1)S(1)}, bf16[160,1440]{1,0:T(8,128)(2,1)S(1)}, u32[]{:S(2)}, u32[]{:S(2)}) %collective-permute-start.10) | collective-permute-done | bytes 460832 | tf_op jit(solution)/shard_map/ppermute | solution.py:54
  187.3 5.4 collective-permute-done.22
  195.0 13.1 %collective-permute-done.2 = bf16[320,1440]{1,0:T(8,128)(2,1)S(1)} collective-permute-done((bf16[320,1440]{1,0:T(8,128)(2,1)S(1)}, bf16[320,1440]{1,0:T(8,128)(2,1)S(1)}, u32[]{:S(2)}, u32[]{:S(2)}) %collective-permute-start.2) | collective-permute-done | bytes 921632 | tf_op jit(solution)/shard_map/ppermute | solution.py:54
  208.1 11.8 %collective-permute-start.4 = (bf16[160,1440]{1,0:T(8,128)(2,1)S(1)}, bf16[160,1440]{1,0:T(8,128)(2,1)S(1)}, u32[]{:S(2)}, u32[]{:S(2)}) collective-permute-start(bf16[160,1440]{1,0:T(8,128)(2,1)S(1)} %slice.456), channel_id=1, source_target_pairs={{0,8},{4,12},{8,16},{12,20},{16,24},{20,28},{24,0},{28,4},{1,9},{5... | collective-permute-start | bytes 1382408 | tf_op jit(solution)/shard_map/ppermute | solution.py:54
  219.9 8.2 collective-permute-done.3
  230.4 8.9 collective-permute-done.4
  239.3 5.9 collective-permute-done.5
  247.2 4.3 conv_forward.3
  255.2 4.8 collective-permute-done.25
  261.9 5.7 collective-permute-done.26
  285.7 7.4 collective-permute-done.32
  347.7 10.3 %collective-permute-done.38 = bf16[77,640]{1,0:T(8,128)(2,1)S(1)} collective-permute-done((bf16[77,640]{1,0:T(8,128)(2,1)S(1)}, bf16[77,640]{1,0:T(8,128)(2,1)S(1)}, u32[]{:S(2)}, u32[]{:S(2)}) %collective-permute-start.38) | collective-permute-done | bytes 98592 | tf_op jit(solution)/shard_map/ppermute | solution.py:54
  381.8 7.0 collective-permute-done.53
  390.6 5.2 collective-permute-done.44
  404.8 4.7 collective-permute-done.45
  415.9 4.8 convolution_convert_fusion.12
  425.3 8.0 convert_reduce_fusion
  434.3 5.3 convolution_convert_fusion.3
  439.7 4.3 fusion.9
  456.1 7.4 collective-permute-done.57
  464.8 4.9 collective-permute-done.48
  484.9 7.9 convolution_convert_fusion
  515.0 4.4 collective-permute-done.61
  547.2 4.7 multiply_convert_fusion
  558.5 21.1 %collective-permute-done.64 = bf16[512,640]{0,1:T(8,128)(2,1)S(1)} collective-permute-done((bf16[512,640]{0,1:T(8,128)(2,1)S(1)}, bf16[512,640]{0,1:T(8,128)(2,1)S(1)}, u32[]{:S(2)}, u32[]{:S(2)}) %collective-permute-start.64) | collective-permute-done | bytes 655392 | tf_op jit(solution)/shard_map/ppermute | solution.py:37
  596.9 5.5 collective-permute-done.98
  606.5 6.6 collective-permute-done.66
  632.3 4.4 convolution_convert_fusion.6
  636.7 4.4 copy.230
  651.5 11.8 %concatenate.660 = bf16[1280,2560]{1,0:T(8,128)(2,1)} concatenate(bf16[1280,960]{1,0:T(8,128)(2,1)} %copy.230, bf16[1280,320]{1,0:T(8,128)(2,1)} %copy.231, bf16[1280,320]{1,0:T(8,128)(2,1)} %copy.232, bf16[1280,320]{1,0:T(8,128)(2,1)} %copy.233, bf16[1280,320]{1,0:T(8,128)(2,1)} %copy.234, bf16[1280,320]{1,0:T(8,128)(2,1)S(1)} %copy-done.27), dimensions={1} | concatenate | bytes 13107200 | tf_op jit(solution)/shard_map/concatenate | solution.py:746
  667.9 8.8 collective-permute-done.71
  682.9 4.4 convolution_convert_fusion.5
  687.3 4.5 convolution_convert_fusion.1
  701.2 20.9 %collective-permute-done.88 = bf16[160,1440]{1,0:T(8,128)(2,1)} collective-permute-done((bf16[160,1440]{1,0:T(8,128)(2,1)}, bf16[160,1440]{1,0:T(8,128)(2,1)}, u32[]{:S(2)}, u32[]{:S(2)}) %collective-permute-start.88) | collective-permute-done | bytes 460832 | tf_op jit(solution)/shard_map/ppermute | solution.py:54
  722.0 19.0 %collective-permute-done.90 = bf16[160,1440]{1,0:T(8,128)(2,1)} collective-permute-done((bf16[160,1440]{1,0:T(8,128)(2,1)}, bf16[160,1440]{1,0:T(8,128)(2,1)}, u32[]{:S(2)}, u32[]{:S(2)}) %collective-permute-start.90) | collective-permute-done | bytes 460832 | tf_op jit(solution)/shard_map/ppermute | solution.py:54
  756.5 7.3 collective-permute-done.73
  773.6 4.4 convolution_convert_fusion.4
  779.8 4.5 convolution_convert_fusion.2
  789.3 9.7 %collective-permute-done.89 = bf16[320,1440]{1,0:T(8,128)(2,1)S(1)} collective-permute-done((bf16[320,1440]{1,0:T(8,128)(2,1)}, bf16[320,1440]{1,0:T(8,128)(2,1)S(1)}, u32[]{:S(2)}, u32[]{:S(2)}) %collective-permute-start.89) | collective-permute-done | bytes 921632 | tf_op jit(solution)/shard_map/ppermute | solution.py:54
  800.8 19.2 %collective-permute-done.83 = bf16[160,1440]{1,0:T(8,128)(2,1)S(1)} collective-permute-done((bf16[160,1440]{1,0:T(8,128)(2,1)S(1)}, bf16[160,1440]{1,0:T(8,128)(2,1)S(1)}, u32[]{:S(2)}, u32[]{:S(2)}) %collective-permute-start.83) | collective-permute-done | bytes 460832 | tf_op jit(solution)/shard_map/ppermute | solution.py:54
  820.1 13.4 %collective-permute-done.85 = bf16[160,1440]{1,0:T(8,128)(2,1)S(1)} collective-permute-done((bf16[160,1440]{1,0:T(8,128)(2,1)S(1)}, bf16[160,1440]{1,0:T(8,128)(2,1)S(1)}, u32[]{:S(2)}, u32[]{:S(2)}) %collective-permute-start.85) | collective-permute-done | bytes 460832 | tf_op jit(solution)/shard_map/ppermute | solution.py:54
  841.7 18.6 %collective-permute-done.86 = bf16[320,1440]{1,0:T(8,128)(2,1)S(1)} collective-permute-done((bf16[320,1440]{1,0:T(8,128)(2,1)S(1)}, bf16[320,1440]{1,0:T(8,128)(2,1)S(1)}, u32[]{:S(2)}, u32[]{:S(2)}) %collective-permute-start.86) | collective-permute-done | bytes 921632 | tf_op jit(solution)/shard_map/ppermute | solution.py:54
  860.3 20.0 %collective-permute-done.84 = bf16[320,1440]{1,0:T(8,128)(2,1)S(1)} collective-permute-done((bf16[320,1440]{1,0:T(8,128)(2,1)S(1)}, bf16[320,1440]{1,0:T(8,128)(2,1)S(1)}, u32[]{:S(2)}, u32[]{:S(2)}) %collective-permute-start.84) | collective-permute-done | bytes 921632 | tf_op jit(solution)/shard_map/ppermute | solution.py:54
  886.3 9.0 collective-permute-done.81
  (921 shorter events, 437.7 us)
Async XLA Ops:
  7.2 265.0 %all-gather.3.cloned.1.call-start = ((), (), s32[]{:S(2)}) async-start(), calls=%async_computation.3 | async-start | bytes 7372800 | tf_op jit(solution)/shard_map/all_gather | solution.py:110
  14.3 15.2 %collective-permute-start = (bf16[160,512]{1,0:T(8,128)(2,1)}, bf16[160,512]{1,0:T(8,128)(2,1)}, u32[]{:S(2)}, u32[]{:S(2)}) collective-permute-start(bf16[160,512]{1,0:T(8,128)(2,1)} %get-tuple-element.246), channel_id=1, source_target_pairs={{0,4},{4,0},{8,12},{12,8},{16,20},{20,16},{24,28},{28,24},{1,5},{5... | collective-permute-start | bytes 491528 | tf_op jit(solution)/shard_map/ppermute | solution.py:37
  17.5 398.4 %all-gather.5.cloned.1.call-start = ((), (), s32[]{:S(2)}) async-start(), calls=%async_computation.4 | async-start | bytes 11059200 | tf_op jit(solution)/shard_map/all_gather | solution.py:110
  19.5 32.7 %collective-permute-start.6 = (bf16[160,1440]{1,0:T(8,128)(2,1)}, bf16[160,1440]{1,0:T(8,128)(2,1)}, u32[]{:S(2)}, u32[]{:S(2)}) collective-permute-start(bf16[160,1440]{1,0:T(8,128)(2,1)} %get-tuple-element.203), channel_id=1, source_target_pairs={{0,4},{4,0},{8,12},{12,8},{16,20},{20,16},{24,28},{28,24},{1,5},{5... | collective-permute-start | bytes 1382408 | tf_op jit(solution)/shard_map/ppermute | solution.py:37
  37.2 142.8 %collective-permute-start.1 = (bf16[160,1440]{1,0:T(8,128)(2,1)}, bf16[160,1440]{1,0:T(8,128)(2,1)}, u32[]{:S(2)}, u32[]{:S(2)}) collective-permute-start(bf16[160,1440]{1,0:T(8,128)(2,1)} %get-tuple-element.205), channel_id=1, source_target_pairs={{0,4},{4,0},{8,12},{12,8},{16,20},{20,16},{24,28},{28,24},{1,5},{5... | collective-permute-start | bytes 1382408 | tf_op jit(solution)/shard_map/ppermute | solution.py:37
  46.8 15.5 %collective-permute-start.12 = (bf16[2,160,512]{2,1,0:T(8,128)(2,1)S(1)}, bf16[2,160,512]{2,1,0:T(8,128)(2,1)S(1)}, u32[]{:S(2)}, u32[]{:S(2)}) collective-permute-start(bf16[2,160,512]{2,1,0:T(8,128)(2,1)S(1)} %maximum_select_fusion.34), channel_id=1, source_target_pairs={{0,2},{1,3},{2,0},{3,1},{4,6},{5,7},{6,4},{7,5},{8,10},{9,11},{10,... | collective-permute-start | bytes 983048 | tf_op jit(solution)/shard_map/ppermute | solution.py:37
  53.7 32.0 %collective-permute-start.7 = (bf16[320,1440]{1,0:T(8,128)(2,1)S(1)}, bf16[320,1440]{1,0:T(8,128)(2,1)S(1)}, u32[]{:S(2)}, u32[]{:S(2)}) collective-permute-start(bf16[320,1440]{1,0:T(8,128)(2,1)S(1)} %maximum_select_fusion.11), channel_id=1, source_target_pairs={{0,8},{4,12},{8,16},{12,20},{16,24},{20,28},{24,0},{28,4},{1,9},{5... | collective-permute-start | bytes 2764808 | tf_op jit(solution)/shard_map/ppermute | solution.py:54
  55.2 74.8 %collective-permute-start.8 = (bf16[320,1440]{1,0:T(8,128)(2,1)S(1)}, bf16[320,1440]{1,0:T(8,128)(2,1)S(1)}, u32[]{:S(2)}, u32[]{:S(2)}) collective-permute-start(bf16[320,1440]{1,0:T(8,128)(2,1)S(1)} %maximum_select_fusion.11), channel_id=1, source_target_pairs={{0,24},{4,28},{8,0},{12,4},{16,8},{20,12},{24,16},{28,20},{1,25},{... | collective-permute-start | bytes 2764808 | tf_op jit(solution)/shard_map/ppermute | solution.py:54
  62.7 105.4 %collective-permute-start.15 = (bf16[2,2,160,1024]{3,2,0,1:T(8,128)(2,1)S(1)}, bf16[2,2,160,1024]{3,2,0,1:T(8,128)(2,1)S(1)}, u32[]{:S(2)}, u32[]{:S(2)}) collective-permute-start(bf16[2,2,160,1024]{3,2,0,1:T(8,128)(2,1)S(1)} %get-tuple-element.201), channel_id=1, source_target_pairs={{0,1},{1,0},{2,3},{3,2},{4,5},{5,4},{6,7},{7,6},{8,9},{9,8},{10,11... | collective-permute-start | bytes 3932168 | tf_op jit(solution)/shard_map/ppermute | solution.py:37
  85.7 54.5 %collective-permute-start.9 = (bf16[160,1440]{1,0:T(8,128)(2,1)S(1)}, bf16[160,1440]{1,0:T(8,128)(2,1)S(1)}, u32[]{:S(2)}, u32[]{:S(2)}) collective-permute-start(bf16[160,1440]{1,0:T(8,128)(2,1)S(1)} %slice.458), channel_id=1, source_target_pairs={{0,8},{4,12},{8,16},{12,20},{16,24},{20,28},{24,0},{28,4},{1,9},{5... | collective-permute-start | bytes 1382408 | tf_op jit(solution)/shard_map/ppermute | solution.py:54
  130.0 38.0 %collective-permute-start.10 = (bf16[160,1440]{1,0:T(8,128)(2,1)S(1)}, bf16[160,1440]{1,0:T(8,128)(2,1)S(1)}, u32[]{:S(2)}, u32[]{:S(2)}) collective-permute-start(bf16[160,1440]{1,0:T(8,128)(2,1)S(1)} %slice.459), channel_id=1, source_target_pairs={{0,24},{4,28},{8,0},{12,4},{16,8},{20,12},{24,16},{28,20},{1,25},{... | collective-permute-start | bytes 1382408 | tf_op jit(solution)/shard_map/ppermute | solution.py:54
  181.5 26.5 %collective-permute-start.2 = (bf16[320,1440]{1,0:T(8,128)(2,1)S(1)}, bf16[320,1440]{1,0:T(8,128)(2,1)S(1)}, u32[]{:S(2)}, u32[]{:S(2)}) collective-permute-start(bf16[320,1440]{1,0:T(8,128)(2,1)S(1)} %maximum_select_fusion.10), channel_id=1, source_target_pairs={{0,8},{4,12},{8,16},{12,20},{16,24},{20,28},{24,0},{28,4},{1,9},{5... | collective-permute-start | bytes 2764808 | tf_op jit(solution)/shard_map/ppermute | solution.py:54
  184.0 44.1 %collective-permute-start.3 = (bf16[320,1440]{1,0:T(8,128)(2,1)S(1)}, bf16[320,1440]{1,0:T(8,128)(2,1)S(1)}, u32[]{:S(2)}, u32[]{:S(2)}) collective-permute-start(bf16[320,1440]{1,0:T(8,128)(2,1)S(1)} %maximum_select_fusion.10), channel_id=1, source_target_pairs={{0,24},{4,28},{8,0},{12,4},{16,8},{20,12},{24,16},{28,20},{1,25},{... | collective-permute-start | bytes 2764808 | tf_op jit(solution)/shard_map/ppermute | solution.py:54
  194.1 51.2 %collective-permute-start.23 = (bf16[2,2,160,1024]{3,2,0,1:T(8,128)(2,1)S(1)}, bf16[2,2,160,1024]{3,2,0,1:T(8,128)(2,1)S(1)}, u32[]{:S(2)}, u32[]{:S(2)}) collective-permute-start(bf16[2,2,160,1024]{3,2,0,1:T(8,128)(2,1)S(1)} %get-tuple-element.199), channel_id=1, source_target_pairs={{0,1},{1,0},{2,3},{3,2},{4,5},{5,4},{6,7},{7,6},{8,9},{9,8},{10,11... | collective-permute-start | bytes 3932168 | tf_op jit(solution)/shard_map/ppermute | solution.py:37
  208.1 31.2 %collective-permute-start.4 = (bf16[160,1440]{1,0:T(8,128)(2,1)S(1)}, bf16[160,1440]{1,0:T(8,128)(2,1)S(1)}, u32[]{:S(2)}, u32[]{:S(2)}) collective-permute-start(bf16[160,1440]{1,0:T(8,128)(2,1)S(1)} %slice.456), channel_id=1, source_target_pairs={{0,8},{4,12},{8,16},{12,20},{16,24},{20,28},{24,0},{28,4},{1,9},{5... | collective-permute-start | bytes 1382408 | tf_op jit(solution)/shard_map/ppermute | solution.py:54
  228.1 17.1 %collective-permute-start.5 = (bf16[160,1440]{1,0:T(8,128)(2,1)S(1)}, bf16[160,1440]{1,0:T(8,128)(2,1)S(1)}, u32[]{:S(2)}, u32[]{:S(2)}) collective-permute-start(bf16[160,1440]{1,0:T(8,128)(2,1)S(1)} %slice.457), channel_id=1, source_target_pairs={{0,24},{4,28},{8,0},{12,4},{16,8},{20,12},{24,16},{28,20},{1,25},{... | collective-permute-start | bytes 1382408 | tf_op jit(solution)/shard_map/ppermute | solution.py:54
  268.9 430.2 %reduce-scatter.8.cloned.1.call-start = ((), (), s32[]{:S(2)}) async-start(), calls=%async_computation.7 | async-start | bytes 3686400 | tf_op jit(solution)/shard_map/reduce_scatter | solution.py:114
  299.4 17.2 %collective-permute-start.34 = (bf16[512,640]{1,0:T(8,128)(2,1)}, bf16[512,640]{1,0:T(8,128)(2,1)}, u32[]{:S(2)}, u32[]{:S(2)}) collective-permute-start(bf16[512,640]{1,0:T(8,128)(2,1)} %fusion.37), channel_id=1, source_target_pairs={{0,4},{4,0},{8,12},{12,8},{16,20},{20,16},{24,28},{28,24},{1,5},{5... | collective-permute-start | bytes 1966088 | tf_op jit(solution)/shard_map/ppermute | solution.py:37
  338.9 19.1 %collective-permute-start.38 = (bf16[77,640]{1,0:T(8,128)(2,1)S(1)}, bf16[77,640]{1,0:T(8,128)(2,1)S(1)}, u32[]{:S(2)}, u32[]{:S(2)}) collective-permute-start(bf16[77,640]{1,0:T(8,128)(2,1)S(1)} %get-tuple-element.222), channel_id=1, source_target_pairs={{0,16},{4,20},{8,24},{12,28},{16,0},{20,4},{24,8},{28,12},{1,17},{... | collective-permute-start | bytes 295688 | tf_op jit(solution)/shard_map/ppermute | solution.py:54
  340.4 19.6 %collective-permute-start.36 = (bf16[128,1280]{0,1:T(8,128)(2,1)S(1)}, bf16[128,1280]{0,1:T(8,128)(2,1)S(1)}, u32[]{:S(2)}, u32[]{:S(2)}) collective-permute-start(bf16[128,1280]{0,1:T(8,128)(2,1)S(1)} %dynamic-slice_convert_fusion.13), channel_id=1, source_target_pairs={{0,2},{1,3},{2,0},{3,1},{4,6},{5,7},{6,4},{7,5},{8,10},{9,11},{10,... | collective-permute-start | bytes 983048 | tf_op jit(solution)/shard_map/ppermute | solution.py:37
  380.3 15.5 %collective-permute-start.44 = (bf16[128,1280]{0,1:T(8,128)(2,1)S(1)}, bf16[128,1280]{0,1:T(8,128)(2,1)S(1)}, u32[]{:S(2)}, u32[]{:S(2)}) collective-permute-start(bf16[128,1280]{0,1:T(8,128)(2,1)S(1)} %dynamic-slice_convert_fusion.12), channel_id=1, source_target_pairs={{0,2},{1,3},{2,0},{3,1},{4,6},{5,7},{6,4},{7,5},{8,10},{9,11},{10,... | collective-permute-start | bytes 983048 | tf_op jit(solution)/shard_map/ppermute | solution.py:37
  439.7 477.0 %reduce-scatter.6.cloned.1.call-start = ((), (), s32[]{:S(2)}) async-start(), calls=%async_computation.6 | async-start | bytes 7372800 | tf_op jit(solution)/shard_map/reduce_scatter | solution.py:114
  454.7 15.0 %collective-permute-start.48 = (bf16[128,1280]{0,1:T(8,128)(2,1)S(1)}, bf16[128,1280]{0,1:T(8,128)(2,1)S(1)}, u32[]{:S(2)}, u32[]{:S(2)}) collective-permute-start(bf16[128,1280]{0,1:T(8,128)(2,1)S(1)} %dynamic-slice_convert_fusion.11), channel_id=1, source_target_pairs={{0,2},{1,3},{2,0},{3,1},{4,6},{5,7},{6,4},{7,5},{8,10},{9,11},{10,... | collective-permute-start | bytes 983048 | tf_op jit(solution)/shard_map/ppermute | solution.py:37
  474.0 205.2 %collective-permute-start.51 = (bf16[160,512]{1,0:T(8,128)(2,1)}, bf16[160,512]{1,0:T(8,128)(2,1)}, u32[]{:S(2)}, u32[]{:S(2)}) collective-permute-start(bf16[160,512]{1,0:T(8,128)(2,1)} %get-tuple-element.226), channel_id=1, source_target_pairs={{0,4},{4,0},{8,12},{12,8},{16,20},{20,16},{24,28},{28,24},{1,5},{5... | collective-permute-start | bytes 491528 | tf_op jit(solution)/shard_map/ppermute | solution.py:37
  480.3 44.1 %collective-permute-start.24 = (f32[160,512]{1,0:T(8,128)}, f32[160,512]{1,0:T(8,128)}, u32[]{:S(2)}, u32[]{:S(2)}) collective-permute-start(f32[160,512]{1,0:T(8,128)} %get-tuple-element.218), channel_id=1, source_target_pairs={{0,4},{4,0},{8,12},{12,8},{16,20},{20,16},{24,28},{28,24},{1,5},{5... | collective-permute-start | bytes 983048 | tf_op jit(solution)/shard_map/ppermute | solution.py:37
  501.7 418.9 %reduce-scatter.4.cloned.1.call-start = ((), (), s32[]{:S(2)}) async-start(), calls=%async_computation.5 | async-start | bytes 7372800 | tf_op jit(solution)/shard_map/reduce_scatter | solution.py:114
  506.3 18.1 %collective-permute-start.50 = (bf16[256,1280]{0,1:T(8,128)(2,1)}, bf16[256,1280]{0,1:T(8,128)(2,1)}, u32[]{:S(2)}, u32[]{:S(2)}) collective-permute-start(bf16[256,1280]{0,1:T(8,128)(2,1)} %maximum_select_fusion.24), channel_id=1, source_target_pairs={{0,1},{1,0},{2,3},{3,2},{4,5},{5,4},{6,7},{7,6},{8,9},{9,8},{10,11... | collective-permute-start | bytes 1966088 | tf_op jit(solution)/shard_map/ppermute | solution.py:37
  513.5 25.6 %collective-permute-start.96 = (bf16[77,640]{1,0:T(8,128)(2,1)S(1)}, bf16[77,640]{1,0:T(8,128)(2,1)S(1)}, u32[]{:S(2)}, u32[]{:S(2)}) collective-permute-start(bf16[77,640]{1,0:T(8,128)(2,1)S(1)} %fusion.128), channel_id=1, source_target_pairs={{0,4},{4,0},{8,12},{12,8},{16,20},{20,16},{24,28},{28,24},{1,5},{5... | collective-permute-start | bytes 295688 | tf_op jit(solution)/shard_map/ppermute | solution.py:37
  539.9 57.0 %collective-permute-start.97 = (bf16[77,640]{1,0:T(8,128)(2,1)}, bf16[77,640]{1,0:T(8,128)(2,1)S(1)}, u32[]{:S(2)}, u32[]{:S(2)}) collective-permute-start(bf16[77,640]{1,0:T(8,128)(2,1)} %get-tuple-element.145), channel_id=1, source_target_pairs={{0,8},{4,12},{8,16},{12,20},{16,24},{20,28},{24,0},{28,4},{1,9},{5... | collective-permute-start | bytes 295688 | tf_op jit(solution)/shard_map/ppermute | solution.py:54
  553.9 25.7 %collective-permute-start.64 = (bf16[512,640]{0,1:T(8,128)(2,1)S(1)}, bf16[512,640]{0,1:T(8,128)(2,1)S(1)}, u32[]{:S(2)}, u32[]{:S(2)}) collective-permute-start(bf16[512,640]{0,1:T(8,128)(2,1)S(1)} %pad_maximum_fusion.12), channel_id=1, source_target_pairs={{0,4},{4,0},{8,12},{12,8},{16,20},{20,16},{24,28},{28,24},{1,5},{5... | collective-permute-start | bytes 1966088 | tf_op jit(solution)/shard_map/ppermute | solution.py:37
  583.3 19.1 %collective-permute-start.65 = (bf16[256,1280]{0,1:T(8,128)(2,1)}, bf16[256,1280]{0,1:T(8,128)(2,1)}, u32[]{:S(2)}, u32[]{:S(2)}) collective-permute-start(bf16[256,1280]{0,1:T(8,128)(2,1)} %constant_dynamic-slice_fusion.10), channel_id=1, source_target_pairs={{0,1},{1,0},{2,3},{3,2},{4,5},{5,4},{6,7},{7,6},{8,9},{9,8},{10,11... | collective-permute-start | bytes 1966088 | tf_op jit(solution)/shard_map/ppermute | solution.py:37
  628.1 16.4 %collective-permute-start.69 = (bf16[2,320,512]{2,1,0:T(8,128)(2,1)}, bf16[2,320,512]{2,1,0:T(8,128)(2,1)}, u32[]{:S(2)}, u32[]{:S(2)}) collective-permute-start(bf16[2,320,512]{2,1,0:T(8,128)(2,1)} %dynamic-slice_bitcast_fusion.2), channel_id=1, source_target_pairs={{0,1},{1,0},{2,3},{3,2},{4,5},{5,4},{6,7},{7,6},{8,9},{9,8},{10,11... | collective-permute-start | bytes 1966088 | tf_op jit(solution)/shard_map/ppermute | solution.py:37
  641.1 22.2 %collective-permute-start.104 = (f32[19,320]{1,0:T(8,128)S(1)}, f32[19,320]{1,0:T(8,128)S(1)}, u32[]{:S(2)}, u32[]{:S(2)}) collective-permute-start(f32[19,320]{1,0:T(8,128)S(1)} %add.890), channel_id=1, source_target_pairs={{0,16},{4,20},{8,24},{12,28},{16,0},{20,4},{24,8},{28,12},{1,17},{... | collective-permute-start | bytes 72968 | tf_op jit(solution)/shard_map/ppermute | solution.py:37
  646.1 19.8 %collective-permute-start.70 = (bf16[320,512]{1,0:T(8,128)(2,1)S(1)}, bf16[320,512]{1,0:T(8,128)(2,1)}, u32[]{:S(2)}, u32[]{:S(2)}) collective-permute-start(bf16[320,512]{1,0:T(8,128)(2,1)S(1)} %fusion.112), channel_id=1, source_target_pairs={{0,2},{1,3},{2,0},{3,1},{4,6},{5,7},{6,4},{7,5},{8,10},{9,11},{10,... | collective-permute-start | bytes 983048 | tf_op jit(solution)/shard_map/ppermute | solution.py:37
  693.1 51.8 %collective-permute-start.72 = (bf16[2,2,160,1024]{3,2,1,0:T(8,128)(2,1)}, bf16[2,2,160,1024]{3,2,1,0:T(8,128)(2,1)}, u32[]{:S(2)}, u32[]{:S(2)}) collective-permute-start(bf16[2,2,160,1024]{3,2,1,0:T(8,128)(2,1)} %dynamic-slice_bitcast_fusion.1), channel_id=1, source_target_pairs={{0,1},{1,0},{2,3},{3,2},{4,5},{5,4},{6,7},{7,6},{8,9},{9,8},{10,11... | collective-permute-start | bytes 3932168 | tf_op jit(solution)/shard_map/ppermute | solution.py:37
  695.3 26.7 %collective-permute-start.88 = (bf16[160,1440]{1,0:T(8,128)(2,1)}, bf16[160,1440]{1,0:T(8,128)(2,1)}, u32[]{:S(2)}, u32[]{:S(2)}) collective-permute-start(bf16[160,1440]{1,0:T(8,128)(2,1)} %get-tuple-element.175), channel_id=1, source_target_pairs={{0,8},{4,12},{8,16},{12,20},{16,24},{20,28},{24,0},{28,4},{1,9},{5... | collective-permute-start | bytes 1382408 | tf_op jit(solution)/shard_map/ppermute | solution.py:54
  695.3 45.7 %collective-permute-start.90 = (bf16[160,1440]{1,0:T(8,128)(2,1)}, bf16[160,1440]{1,0:T(8,128)(2,1)}, u32[]{:S(2)}, u32[]{:S(2)}) collective-permute-start(bf16[160,1440]{1,0:T(8,128)(2,1)} %get-tuple-element.177), channel_id=1, source_target_pairs={{0,24},{4,28},{8,0},{12,4},{16,8},{20,12},{24,16},{28,20},{1,25},{... | collective-permute-start | bytes 1382408 | tf_op jit(solution)/shard_map/ppermute | solution.py:54
  743.8 45.5 %collective-permute-start.91 = (bf16[320,1440]{1,0:T(8,128)(2,1)}, bf16[320,1440]{1,0:T(8,128)(2,1)}, u32[]{:S(2)}, u32[]{:S(2)}) collective-permute-start(bf16[320,1440]{1,0:T(8,128)(2,1)} %pad_maximum_fusion.10), channel_id=1, source_target_pairs={{0,24},{4,28},{8,0},{12,4},{16,8},{20,12},{24,16},{28,20},{1,25},{... | collective-permute-start | bytes 2764808 | tf_op jit(solution)/shard_map/ppermute | solution.py:54
  748.4 50.7 %collective-permute-start.89 = (bf16[320,1440]{1,0:T(8,128)(2,1)}, bf16[320,1440]{1,0:T(8,128)(2,1)S(1)}, u32[]{:S(2)}, u32[]{:S(2)}) collective-permute-start(bf16[320,1440]{1,0:T(8,128)(2,1)} %pad_maximum_fusion.9), channel_id=1, source_target_pairs={{0,8},{4,12},{8,16},{12,20},{16,24},{20,28},{24,0},{28,4},{1,9},{5... | collective-permute-start | bytes 2764808 | tf_op jit(solution)/shard_map/ppermute | solution.py:54
  778.1 61.3 %collective-permute-start.77 = (bf16[2,2,160,1024]{3,2,1,0:T(8,128)(2,1)S(1)}, bf16[2,2,160,1024]{3,2,1,0:T(8,128)(2,1)S(1)}, u32[]{:S(2)}, u32[]{:S(2)}) collective-permute-start(bf16[2,2,160,1024]{3,2,1,0:T(8,128)(2,1)S(1)} %dynamic-slice_bitcast_fusion), channel_id=1, source_target_pairs={{0,1},{1,0},{2,3},{3,2},{4,5},{5,4},{6,7},{7,6},{8,9},{9,8},{10,11... | collective-permute-start | bytes 3932168 | tf_op jit(solution)/shard_map/ppermute | solution.py:37
  784.4 35.6 %collective-permute-start.83 = (bf16[160,1440]{1,0:T(8,128)(2,1)S(1)}, bf16[160,1440]{1,0:T(8,128)(2,1)S(1)}, u32[]{:S(2)}, u32[]{:S(2)}) collective-permute-start(bf16[160,1440]{1,0:T(8,128)(2,1)S(1)} %get-tuple-element.181), channel_id=1, source_target_pairs={{0,8},{4,12},{8,16},{12,20},{16,24},{20,28},{24,0},{28,4},{1,9},{5... | collective-permute-start | bytes 1382408 | tf_op jit(solution)/shard_map/ppermute | solution.py:54
  786.7 46.8 %collective-permute-start.85 = (bf16[160,1440]{1,0:T(8,128)(2,1)S(1)}, bf16[160,1440]{1,0:T(8,128)(2,1)S(1)}, u32[]{:S(2)}, u32[]{:S(2)}) collective-permute-start(bf16[160,1440]{1,0:T(8,128)(2,1)S(1)} %get-tuple-element.183), channel_id=1, source_target_pairs={{0,24},{4,28},{8,0},{12,4},{16,8},{20,12},{24,16},{28,20},{1,25},{... | collective-permute-start | bytes 1382408 | tf_op jit(solution)/shard_map/ppermute | solution.py:54
  833.8 26.4 %collective-permute-start.86 = (bf16[320,1440]{1,0:T(8,128)(2,1)S(1)}, bf16[320,1440]{1,0:T(8,128)(2,1)S(1)}, u32[]{:S(2)}, u32[]{:S(2)}) collective-permute-start(bf16[320,1440]{1,0:T(8,128)(2,1)S(1)} %pad_maximum_fusion.8), channel_id=1, source_target_pairs={{0,24},{4,28},{8,0},{12,4},{16,8},{20,12},{24,16},{28,20},{1,25},{... | collective-permute-start | bytes 2764808 | tf_op jit(solution)/shard_map/ppermute | solution.py:54
  838.1 42.1 %collective-permute-start.84 = (bf16[320,1440]{1,0:T(8,128)(2,1)S(1)}, bf16[320,1440]{1,0:T(8,128)(2,1)S(1)}, u32[]{:S(2)}, u32[]{:S(2)}) collective-permute-start(bf16[320,1440]{1,0:T(8,128)(2,1)S(1)} %pad_maximum_fusion.7), channel_id=1, source_target_pairs={{0,8},{4,12},{8,16},{12,20},{16,24},{20,28},{24,0},{28,4},{1,9},{5... | collective-permute-start | bytes 2764808 | tf_op jit(solution)/shard_map/ppermute | solution.py:54
  838.5 43.5 %collective-permute-start.92 = (bf16[160,1440]{1,0:T(8,128)(2,1)S(1)}, bf16[160,1440]{1,0:T(8,128)(2,1)S(1)}, u32[]{:S(2)}, u32[]{:S(2)}) collective-permute-start(bf16[160,1440]{1,0:T(8,128)(2,1)S(1)} %dynamic-slice_convert_fusion), channel_id=1, source_target_pairs={{0,4},{4,0},{8,12},{12,8},{16,20},{20,16},{24,28},{28,24},{1,5},{5... | collective-permute-start | bytes 1382408 | tf_op jit(solution)/shard_map/ppermute | solution.py:37
  840.4 44.5 %collective-permute-start.80 = (bf16[2,160,512]{2,1,0:T(8,128)(2,1)S(1)}, bf16[2,160,512]{2,1,0:T(8,128)(2,1)S(1)}, u32[]{:S(2)}, u32[]{:S(2)}) collective-permute-start(bf16[2,160,512]{2,1,0:T(8,128)(2,1)S(1)} %fusion.116), channel_id=1, source_target_pairs={{0,2},{1,3},{2,0},{3,1},{4,6},{5,7},{6,4},{7,5},{8,10},{9,11},{10,... | collective-permute-start | bytes 983048 | tf_op jit(solution)/shard_map/ppermute | solution.py:37
  840.5 45.6 %collective-permute-start.78 = (bf16[2,160,512]{2,1,0:T(8,128)(2,1)S(1)}, bf16[2,160,512]{2,1,0:T(8,128)(2,1)S(1)}, u32[]{:S(2)}, u32[]{:S(2)}) collective-permute-start(bf16[2,160,512]{2,1,0:T(8,128)(2,1)S(1)} %fusion.115), channel_id=1, source_target_pairs={{0,4},{4,0},{8,12},{12,8},{16,20},{20,16},{24,28},{28,24},{1,5},{5... | collective-permute-start | bytes 983048 | tf_op jit(solution)/shard_map/ppermute | solution.py:37
  880.7 31.9 %collective-permute-start.87 = (bf16[160,1440]{1,0:T(8,128)(2,1)S(1)}, bf16[160,1440]{1,0:T(8,128)(2,1)S(1)}, u32[]{:S(2)}, u32[]{:S(2)}) collective-permute-start(bf16[160,1440]{1,0:T(8,128)(2,1)S(1)} %dynamic-slice_convert_fusion.1), channel_id=1, source_target_pairs={{0,4},{4,0},{8,12},{12,8},{16,20},{20,16},{24,28},{28,24},{1,5},{5... | collective-permute-start | bytes 1382408 | tf_op jit(solution)/shard_map/ppermute | solution.py:37
  (233 other events, 2723.4 us)
Sparse Core Ops, SparseCore 0:
  17.6 160.3 all-gather.2
  269.1 146.7 all-gather.4
  439.8 80.1 reduce-scatter.7
  523.9 121.9 reduce-scatter.5
  663.5 173.9 reduce-scatter.3

commit v3 on v2

--- a/solution.py
+++ b/solution.py
@@ -31,6 +31,10 @@
 
 def row_major(x):
     return with_layout_constraint(x, Layout(tuple(range(x.ndim))))
+
+
+def together(*values):
+    return lax.optimization_barrier(values)
 
 
 def swap(x, axis, mask):
@@ -178,9 +182,9 @@
     return (a.astype(F32) + b.astype(F32)).astype(BF16)
 
 
-def image_total(at, blocks):
+def image_total(at, blocks, gate=None):
     if at.images != 4:
-        return image_scatter(at, blocks)
+        return image_scatter(at, blocks), gate
 
     def local(move):
         place = lax.rem(at.image + move, 4)
@@ -189,10 +193,12 @@
     size = blocks.shape[1] // 2
     far, up, down = local(2), local(1), local(3)
     first, second = shift_image(far[:size], 1), shift_image(far[size:], 3)
+    if gate is not None:
+        first, second, gate = together(first, second, gate)
     up = jnp.concatenate([add_low(up[:size], first), up[size:]], axis=0)
     down = jnp.concatenate([down[:size], add_low(down[size:], second)], axis=0)
     up, down = shift_image(up, 1), shift_image(down, 3)
-    return local(0).astype(F32) + up.astype(F32) + down.astype(F32)
+    return local(0).astype(F32) + up.astype(F32) + down.astype(F32), gate
 
 
 def rows_total(x, first=1):
@@ -468,8 +474,7 @@
     return row_major(pair(pick(halves, at.half, 0), other, at.half, 0))
 
 
-def conv_weights_back(at, grad, inputs):
-    total = image_total(at, grad.reshape(at.images, 2 * inputs, -1))
+def conv_weights_back(at, total):
     other = swap_half(part(total, 1 - at.half, 2).astype(BF16))
     grad = unpack(at.half, part(total, at.half, 2), other)
     return grad.reshape((3, 3) + grad.shape[1:])
@@ -612,7 +617,6 @@
     wide = jnp.concatenate([ff_in_w[:, 0], ff_in_w[:, 1], ff_out_w.T], axis=1)
     cross_kv = (kv_image + swap_half(kv_image.astype(BF16)).astype(F32)).astype(BF16)
     cross_keys, cross_values = cross_kv[:, :width], cross_kv[:, width:]
-    conv_one = row_major(image_spread(at, chunk_one))
     conv_two = row_major(image_spread(at, chunk_two))
     low_one = jax.nn.silu(norm_one).astype(BF16)
     w_square = rows_gather(square)
@@ -625,6 +629,8 @@
 
     cot_rows = cotangent.reshape(tokens, width)
     cot_image = to_image(at, cot_rows.T).astype(F32)
+    low_one, chunk_one = together(low_one, chunk_one)
+    conv_one = row_major(image_spread(at, chunk_one))
     act_one = plane_gather(at, low_one)
     hidden_two = conv_forward(conv_one, act_one, columns)
     hidden_two = hidden_two + (bias_own[0] + shift_time)[:, None]
@@ -637,11 +643,12 @@
 
     stream_zero = to_tokens(at, dot(gin, w_in, 0, 0) + biases[3])
     ln_low_one, stored_ln_one = layer_forward(stream_zero, ln_wide[0])
-    n_one = heads_gather(at, ln_low_one)
-    kv_own = dot(n_one, w_kvq[:, : 2 * width], 1, 0, BF16)
-    kv_other = swap_half(kv_own)
-    queries = dot(n_one, w_kvq[:, 2 * width :], 1, 0, BF16)
-    self_blocks = [(kv[:, :width], kv[:, width:]) for kv in (kv_own, kv_other)]
+    n_one_x = heads_gather(at, ln_low_one)
+    n_one, resid_own, cross_keys, cross_values = together(n_one_x, resid_own, cross_keys, cross_values)
+    keys, values, queries = (
+        dot(n_one, w_kvq[:, i * width : (i + 1) * width], 1, 0, BF16) for i in range(3)
+    )
+    self_blocks = [(keys, values), (swap_half(keys), swap_half(values))]
     attended, log_self = attend(queries, self_blocks)
     stream_one = stream_zero + heads_scatter(at, dot(attended, w_self, 1, 1, BF16)) + bias_self
 
@@ -724,6 +731,7 @@
     spread_two = tap_spread(grad_c_two, columns)
     grad_act = plane_scatter(at, dot(conv_two, spread_two, 1, 0, BF16))
     conv_two_grad = row_major(dot(act_two, spread_two, 1, 1, BF16))
+    total_two, grad_act = image_total(at, conv_two_grad.reshape(at.images, 2 * inputs, -1), grad_act)
     grad_hidden, gn_grad_two = group_backward(
         grad_act * silu_slope(norm_two), gn_own[1, 0], stored_two
     )
@@ -733,6 +741,7 @@
     spread_one = tap_spread(grad_c_one, columns)
     grad_act = plane_scatter(at, dot(conv_one, spread_one, 1, 0, BF16))
     conv_one_grad = row_major(dot(act_one, spread_one, 1, 1, BF16))
+    total_one, grad_act = image_total(at, conv_one_grad.reshape(at.images, 2 * inputs, -1), grad_act)
     back, gn_grad_one = group_backward(
         grad_act * silu_slope(norm_one), gn_own[0, 0], stored_one
     )
@@ -749,8 +758,8 @@
         )
     )
     rest = [rest_out[:, i * width : (i + 1) * width] for i in range(8)]
-    conv_two_out = conv_weights_back(at, conv_two_grad, inputs)
-    conv_one_out = conv_weights_back(at, conv_one_grad, inputs)
+    conv_two_out = conv_weights_back(at, total_two)
+    conv_one_out = conv_weights_back(at, total_one)
 
     token_sums = jnp.stack(
         ln_grad_one

time: 942 us -> 932 us (0.989)
  starting transfers between devices: 140 us -> 175 us
  waiting for transfers between devices: 434 us -> 405 us
  matrix products: 135 us -> 125 us
    ppermute x22, waiting for transfers between devices: 271 us -> 172 us  [shift_image(): lax.ppermute(x, 'rows', [(i, (i + 2 * images) % n) for i in range(n)])]
    ppermute x83 -> x84, waiting for transfers between devices: 160 us -> 223 us  [swap(): lax.ppermute(x, axis, [(i, i ^ mask) for i in range(lax.axis_size(axis))])]
    ppermute x22, starting transfers between devices: 56.8 us -> 88.6 us  [shift_image(): lax.ppermute(x, 'rows', [(i, (i + 2 * images) % n) for i in range(n)])]
    dot_general x31 -> x32, matrix products: 110 us -> 104 us  [dot(): lax.dot_general(a, b, (((a_dim,), (b_dim,)), ((), ())), preferred_element...]
    unnamed x345 -> x339, local copies, waits for them, and re-layouts: 19.5 us -> 14.6 us
    ppermute x83 -> x84, starting transfers between devices: 81.9 us -> 85.5 us  [swap(): lax.ppermute(x, axis, [(i, i ^ mask) for i in range(lax.axis_size(axis))])]
  transfers between devices with their start and end apart: 110 -> 111, of which waited for: 56 -> 53; matrix products, arithmetic and copies ran while one was open for 30% -> 29% of each run, Pallas kernels for 2% -> 2%
where the time goes in v3:
time: 932 us; the launch traced here: 920 us
  waiting for transfers between devices  405 us (43%)
  starting transfers between devices  175 us (19%)
  matrix products  125 us (13%)
  local copies, waits for them, and re-layouts  90.8 us (10%)
  other arithmetic  87 us (9%)
  Pallas kernels  19.2 us (2%)
  between operations  17.6 us (2%)
    ppermute x84, waiting for transfers between devices, swap(): lax.ppermute(x, axis, [(i, i ^ mask) for i in range(lax.axis_size(axis))])  223 us
    ppermute x22, waiting for transfers between devices, shift_image(): lax.ppermute(x, 'rows', [(i, (i + 2 * images) % n) for i in range(n)])  172 us
    dot_general x32, matrix products, dot(): lax.dot_general(a, b, (((a_dim,), (b_dim,)), ((), ())), preferred_element...  104 us
    ppermute x22, starting transfers between devices, shift_image(): lax.ppermute(x, 'rows', [(i, (i + 2 * images) % n) for i in range(n)])  88.6 us
    ppermute x84, starting transfers between devices, swap(): lax.ppermute(x, axis, [(i, i ^ mask) for i in range(lax.axis_size(axis))])  85.5 us
  transfers between devices with their start and end apart: 111, of which 53 were waited for; matrix products, arithmetic and copies ran while one was open for 29% of the time, Pallas kernels for 2%

profile of v3, /device:TPU:0, one launch (start us, length us, event | category | flops | bytes accessed | tf_op | source)
XLA Modules:
  0.0 920.1 jit_solution(12193246722889534448)
XLA Ops:
  52.4 5.9 collective-permute-done.11
  68.6 14.7 %collective-permute-done.8 = bf16[320,1440]{1,0:T(8,128)(2,1)S(1)} collective-permute-done((bf16[320,1440]{1,0:T(8,128)(2,1)S(1)}, bf16[320,1440]{1,0:T(8,128)(2,1)S(1)}, u32[]{:S(2)}, u32[]{:S(2)}) %collective-permute-start.8) | collective-permute-done | bytes 921632 | tf_op jit(solution)/shard_map/ppermute | solution.py:58
  83.3 4.3 collective-permute-start.10
  87.7 32.4 %collective-permute-done.7 = bf16[320,1440]{1,0:T(8,128)(2,1)S(1)} collective-permute-done((bf16[320,1440]{1,0:T(8,128)(2,1)S(1)}, bf16[320,1440]{1,0:T(8,128)(2,1)S(1)}, u32[]{:S(2)}, u32[]{:S(2)}) %collective-permute-start.7) | collective-permute-done | bytes 921632 | tf_op jit(solution)/shard_map/ppermute | solution.py:58
  120.1 19.3 %collective-permute-start.9 = (bf16[160,1440]{1,0:T(8,128)(2,1)S(1)}, bf16[160,1440]{1,0:T(8,128)(2,1)S(1)}, u32[]{:S(2)}, u32[]{:S(2)}) collective-permute-start(bf16[160,1440]{1,0:T(8,128)(2,1)S(1)} %slice.447), channel_id=1, source_target_pairs={{0,8},{4,12},{8,16},{12,20},{16,24},{20,28},{24,0},{28,4},{1,9},{5... | collective-permute-start | bytes 1382408 | tf_op jit(solution)/shard_map/ppermute | solution.py:58
  139.6 23.4 %collective-permute-done.9 = bf16[160,1440]{1,0:T(8,128)(2,1)S(1)} collective-permute-done((bf16[160,1440]{1,0:T(8,128)(2,1)S(1)}, bf16[160,1440]{1,0:T(8,128)(2,1)S(1)}, u32[]{:S(2)}, u32[]{:S(2)}) %collective-permute-start.9) | collective-permute-done | bytes 460832 | tf_op jit(solution)/shard_map/ppermute | solution.py:58
  165.0 4.3 conv_forward.2
  174.7 10.9 %collective-permute-start.2 = (bf16[320,1440]{1,0:T(8,128)(2,1)S(1)}, bf16[320,1440]{1,0:T(8,128)(2,1)S(1)}, u32[]{:S(2)}, u32[]{:S(2)}) collective-permute-start(bf16[320,1440]{1,0:T(8,128)(2,1)S(1)} %maximum_select_fusion.10), channel_id=1, source_target_pairs={{0,8},{4,12},{8,16},{12,20},{16,24},{20,28},{24,0},{28,4},{1,9},{5... | collective-permute-start | bytes 2764808 | tf_op jit(solution)/shard_map/ppermute | solution.py:58
  191.0 5.1 collective-permute-done.22
  199.0 11.6 %collective-permute-done.2 = bf16[320,1440]{1,0:T(8,128)(2,1)S(1)} collective-permute-done((bf16[320,1440]{1,0:T(8,128)(2,1)S(1)}, bf16[320,1440]{1,0:T(8,128)(2,1)S(1)}, u32[]{:S(2)}, u32[]{:S(2)}) %collective-permute-start.2) | collective-permute-done | bytes 921632 | tf_op jit(solution)/shard_map/ppermute | solution.py:58
  210.6 21.0 %collective-permute-start.4 = (bf16[160,1440]{1,0:T(8,128)(2,1)S(1)}, bf16[160,1440]{1,0:T(8,128)(2,1)S(1)}, u32[]{:S(2)}, u32[]{:S(2)}) collective-permute-start(bf16[160,1440]{1,0:T(8,128)(2,1)S(1)} %slice.445), channel_id=1, source_target_pairs={{0,8},{4,12},{8,16},{12,20},{16,24},{20,28},{24,0},{28,4},{1,9},{5... | collective-permute-start | bytes 1382408 | tf_op jit(solution)/shard_map/ppermute | solution.py:58
  233.5 11.3 %collective-permute-done.4 = bf16[160,1440]{1,0:T(8,128)(2,1)S(1)} collective-permute-done((bf16[160,1440]{1,0:T(8,128)(2,1)S(1)}, bf16[160,1440]{1,0:T(8,128)(2,1)S(1)}, u32[]{:S(2)}, u32[]{:S(2)}) %collective-permute-start.4) | collective-permute-done | bytes 460832 | tf_op jit(solution)/shard_map/ppermute | solution.py:58
  244.8 5.6 collective-permute-done.5
  252.5 4.3 conv_forward.3
  268.0 6.9 collective-permute-done.25
  297.0 5.5 collective-permute-done.31
  305.8 7.2 collective-permute-done.33
  319.8 12.1 %collective-permute-done.38 = bf16[512,320]{0,1:T(8,128)(2,1)S(1)} collective-permute-done((bf16[512,320]{0,1:T(8,128)(2,1)S(1)}, bf16[512,320]{0,1:T(8,128)(2,1)S(1)}, u32[]{:S(2)}, u32[]{:S(2)}) %collective-permute-start.38) | collective-permute-done | bytes 327712 | tf_op jit(solution)/shard_map/ppermute | solution.py:41
  342.9 8.2 collective-permute-done.41
  353.6 7.4 collective-permute-done.42
  377.5 8.0 collective-permute-done.54
  387.4 5.1 collective-permute-done.45
  395.1 4.5 collective-permute-done.55
  399.9 6.3 collective-permute-done.46
  407.3 10.4 %all-gather.5.cloned.1.call-done = bf16[1280,3840]{1,0:T(8,128)(2,1)} async-done(((bf16[160,3840]{1,0:T(8,128)(2,1)}), bf16[1280,3840]{1,0:T(8,128)(2,1)}) %all-gather.5.cloned.1.call-update) | async-done | bytes 9830416 | tf_op jit(solution)/shard_map/all_gather | solution.py:114
  417.7 4.9 convolution_convert_fusion.12
  427.2 6.9 convert_reduce_fusion
  435.2 4.9 convolution_convert_fusion.3
  444.3 4.6 fusion.9
  460.9 7.4 collective-permute-done.58
  469.0 5.4 collective-permute-done.49
  478.8 6.2 collective-permute-done.59
  487.9 8.8 convolution_convert_fusion
  562.2 13.2 %collective-permute-done.65 = bf16[512,640]{0,1:T(8,128)(2,1)S(1)} collective-permute-done((bf16[512,640]{0,1:T(8,128)(2,1)S(1)}, bf16[512,640]{0,1:T(8,128)(2,1)S(1)}, u32[]{:S(2)}, u32[]{:S(2)}) %collective-permute-start.65) | collective-permute-done | bytes 655392 | tf_op jit(solution)/shard_map/ppermute | solution.py:41
  590.4 4.3 collective-permute-done.99
  601.1 4.9 collective-permute-done.67
  642.2 11.6 %concatenate.647 = bf16[1280,2560]{1,0:T(8,128)(2,1)} concatenate(bf16[1280,960]{1,0:T(8,128)(2,1)S(1)} %copy.210, bf16[1280,320]{1,0:T(8,128)(2,1)} %copy.211, bf16[1280,320]{1,0:T(8,128)(2,1)} %copy.212, bf16[1280,320]{1,0:T(8,128)(2,1)} %copy.213, bf16[1280,320]{1,0:T(8,128)(2,1)} %copy.214, bf16[1280,320]{1,0:T(8,128)(2,1)} %copy.215), dimensions={1} | concatenate | bytes 13107200 | tf_op jit(solution)/shard_map/concatenate | solution.py:755
  657.7 6.7 collective-permute-done.72
  669.4 4.4 convolution_convert_fusion.5
  678.4 6.4 convolution_convert_fusion.2
  709.9 5.9 collective-permute-done.73
  715.9 17.4 %collective-permute-done.74 = bf16[160,1440]{1,0:T(8,128)(2,1)S(1)} collective-permute-done((bf16[160,1440]{1,0:T(8,128)(2,1)S(1)}, bf16[160,1440]{1,0:T(8,128)(2,1)S(1)}, u32[]{:S(2)}, u32[]{:S(2)}) %collective-permute-start.74) | collective-permute-done | bytes 460832 | tf_op jit(solution)/shard_map/ppermute | solution.py:58
  741.6 4.4 convolution_convert_fusion.4
  747.8 4.5 convolution_convert_fusion.1
  761.4 41.2 %collective-permute-done.91 = bf16[320,1440]{1,0:T(8,128)(2,1)S(1)} collective-permute-done((bf16[320,1440]{1,0:T(8,128)(2,1)S(1)}, bf16[320,1440]{1,0:T(8,128)(2,1)S(1)}, u32[]{:S(2)}, u32[]{:S(2)}) %collective-permute-start.91) | collective-permute-done | bytes 921632 | tf_op jit(solution)/shard_map/ppermute | solution.py:58
  813.9 10.4 %collective-permute-done.83 = bf16[2,160,512]{2,1,0:T(8,128)(2,1)S(1)} collective-permute-done((bf16[2,160,512]{2,1,0:T(8,128)(2,1)S(1)}, bf16[2,160,512]{2,1,0:T(8,128)(2,1)S(1)}, u32[]{:S(2)}, u32[]{:S(2)}) %collective-permute-start.83) | collective-permute-done | bytes 327712 | tf_op jit(solution)/shard_map/ppermute | solution.py:41
  835.7 5.2 collective-permute-start.89
  845.0 36.0 %collective-permute-done.95 = f32[2,9,160]{2,0,1:T(2,128)S(1)} collective-permute-done((f32[2,9,160]{2,0,1:T(2,128)S(1)}, f32[2,9,160]{2,0,1:T(2,128)S(1)}, u32[]{:S(2)}, u32[]{:S(2)}) %collective-permute-start.95) | collective-permute-done | bytes 11552 | tf_op jit(solution)/shard_map/ppermute | solution.py:41
  (920 shorter events, 421.1 us)
Async XLA Ops:
  7.2 274.1 %all-gather.3.cloned.1.call-start = ((), (), s32[]{:S(2)}) async-start(), calls=%async_computation.3 | async-start | bytes 7372800 | tf_op jit(solution)/shard_map/all_gather | solution.py:114
  9.4 15.7 %collective-permute-start.16 = (f32[4,320]{1,0:T(4,128)S(1)}, f32[4,320]{1,0:T(4,128)S(1)}, u32[]{:S(2)}, u32[]{:S(2)}) collective-permute-start(f32[4,320]{1,0:T(4,128)S(1)} %fusion.123), channel_id=1, source_target_pairs={{0,4},{4,0},{8,12},{12,8},{16,20},{20,16},{24,28},{28,24},{1,5},{5... | collective-permute-start | bytes 15368 | tf_op jit(solution)/shard_map/ppermute | solution.py:41
  14.4 263.7 %collective-permute-start.29 = (f32[9,320]{1,0:T(8,128)}, f32[9,320]{1,0:T(8,128)}, u32[]{:S(2)}, u32[]{:S(2)}) collective-permute-start(f32[9,320]{1,0:T(8,128)} %pad_maximum_fusion.19), channel_id=1, source_target_pairs={{0,1},{1,0},{2,3},{3,2},{4,5},{5,4},{6,7},{7,6},{8,9},{9,8},{10,11... | collective-permute-start | bytes 34568 | tf_op jit(solution)/shard_map/ppermute | solution.py:41
  16.4 16.5 %collective-permute-start = (bf16[160,512]{1,0:T(8,128)(2,1)}, bf16[160,512]{1,0:T(8,128)(2,1)}, u32[]{:S(2)}, u32[]{:S(2)}) collective-permute-start(bf16[160,512]{1,0:T(8,128)(2,1)} %get-tuple-element.262), channel_id=1, source_target_pairs={{0,4},{4,0},{8,12},{12,8},{16,20},{20,16},{24,28},{28,24},{1,5},{5... | collective-permute-start | bytes 491528 | tf_op jit(solution)/shard_map/ppermute | solution.py:41
  19.6 398.1 %all-gather.5.cloned.1.call-start = ((), (), s32[]{:S(2)}) async-start(), calls=%async_computation.4 | async-start | bytes 11059200 | tf_op jit(solution)/shard_map/all_gather | solution.py:114
  21.4 18.2 %collective-permute-start.6 = (bf16[160,1440]{1,0:T(8,128)(2,1)S(1)}, bf16[160,1440]{1,0:T(8,128)(2,1)}, u32[]{:S(2)}, u32[]{:S(2)}) collective-permute-start(bf16[160,1440]{1,0:T(8,128)(2,1)S(1)} %get-tuple-element.223), channel_id=1, source_target_pairs={{0,4},{4,0},{8,12},{12,8},{16,20},{20,16},{24,28},{28,24},{1,5},{5... | collective-permute-start | bytes 1382408 | tf_op jit(solution)/shard_map/ppermute | solution.py:41
  25.2 148.0 %collective-permute-start.1 = (bf16[160,1440]{1,0:T(8,128)(2,1)}, bf16[160,1440]{1,0:T(8,128)(2,1)}, u32[]{:S(2)}, u32[]{:S(2)}) collective-permute-start(bf16[160,1440]{1,0:T(8,128)(2,1)} %get-tuple-element.225), channel_id=1, source_target_pairs={{0,4},{4,0},{8,12},{12,8},{16,20},{20,16},{24,28},{28,24},{1,5},{5... | collective-permute-start | bytes 1382408 | tf_op jit(solution)/shard_map/ppermute | solution.py:41
  30.3 15.9 %collective-permute-start.18 = (f32[4,320]{1,0:T(4,128)}, f32[4,320]{1,0:T(4,128)}, u32[]{:S(2)}, u32[]{:S(2)}) collective-permute-start(f32[4,320]{1,0:T(4,128)} %add.732), channel_id=1, source_target_pairs={{0,16},{4,20},{8,24},{12,28},{16,0},{20,4},{24,8},{28,12},{1,17},{... | collective-permute-start | bytes 15368 | tf_op jit(solution)/shard_map/ppermute | solution.py:41
  47.1 36.2 %collective-permute-start.8 = (bf16[320,1440]{1,0:T(8,128)(2,1)S(1)}, bf16[320,1440]{1,0:T(8,128)(2,1)S(1)}, u32[]{:S(2)}, u32[]{:S(2)}) collective-permute-start(bf16[320,1440]{1,0:T(8,128)(2,1)S(1)} %maximum_select_fusion.11), channel_id=1, source_target_pairs={{0,24},{4,28},{8,0},{12,4},{16,8},{20,12},{24,16},{28,20},{1,25},{... | collective-permute-start | bytes 2764808 | tf_op jit(solution)/shard_map/ppermute | solution.py:58
  64.9 55.2 %collective-permute-start.7 = (bf16[320,1440]{1,0:T(8,128)(2,1)S(1)}, bf16[320,1440]{1,0:T(8,128)(2,1)S(1)}, u32[]{:S(2)}, u32[]{:S(2)}) collective-permute-start(bf16[320,1440]{1,0:T(8,128)(2,1)S(1)} %maximum_select_fusion.11), channel_id=1, source_target_pairs={{0,8},{4,12},{8,16},{12,20},{16,24},{20,28},{24,0},{28,4},{1,9},{5... | collective-permute-start | bytes 2764808 | tf_op jit(solution)/shard_map/ppermute | solution.py:58
  67.7 95.4 %collective-permute-start.15 = (bf16[2,2,160,1024]{3,2,0,1:T(8,128)(2,1)S(1)}, bf16[2,2,160,1024]{3,2,0,1:T(8,128)(2,1)S(1)}, u32[]{:S(2)}, u32[]{:S(2)}) collective-permute-start(bf16[2,2,160,1024]{3,2,0,1:T(8,128)(2,1)S(1)} %get-tuple-element.221), channel_id=1, source_target_pairs={{0,1},{1,0},{2,3},{3,2},{4,5},{5,4},{6,7},{7,6},{8,9},{9,8},{10,11... | collective-permute-start | bytes 3932168 | tf_op jit(solution)/shard_map/ppermute | solution.py:41
  83.3 56.2 %collective-permute-start.10 = (bf16[160,1440]{1,0:T(8,128)(2,1)S(1)}, bf16[160,1440]{1,0:T(8,128)(2,1)S(1)}, u32[]{:S(2)}, u32[]{:S(2)}) collective-permute-start(bf16[160,1440]{1,0:T(8,128)(2,1)S(1)} %slice.448), channel_id=1, source_target_pairs={{0,24},{4,28},{8,0},{12,4},{16,8},{20,12},{24,16},{28,20},{1,25},{... | collective-permute-start | bytes 1382408 | tf_op jit(solution)/shard_map/ppermute | solution.py:58
  120.1 42.9 %collective-permute-start.9 = (bf16[160,1440]{1,0:T(8,128)(2,1)S(1)}, bf16[160,1440]{1,0:T(8,128)(2,1)S(1)}, u32[]{:S(2)}, u32[]{:S(2)}) collective-permute-start(bf16[160,1440]{1,0:T(8,128)(2,1)S(1)} %slice.447), channel_id=1, source_target_pairs={{0,8},{4,12},{8,16},{12,20},{16,24},{20,28},{24,0},{28,4},{1,9},{5... | collective-permute-start | bytes 1382408 | tf_op jit(solution)/shard_map/ppermute | solution.py:58
  171.6 16.6 %collective-permute-start.21 = (bf16[160,512]{1,0:T(8,128)(2,1)S(1)}, bf16[160,512]{1,0:T(8,128)(2,1)S(1)}, u32[]{:S(2)}, u32[]{:S(2)}) collective-permute-start(bf16[160,512]{1,0:T(8,128)(2,1)S(1)} %get-tuple-element.254), channel_id=1, source_target_pairs={{0,2},{1,3},{2,0},{3,1},{4,6},{5,7},{6,4},{7,5},{8,10},{9,11},{10,... | collective-permute-start | bytes 491528 | tf_op jit(solution)/shard_map/ppermute | solution.py:41
  173.2 17.1 %collective-permute-start.19 = (bf16[160,512]{1,0:T(8,128)(2,1)S(1)}, bf16[160,512]{1,0:T(8,128)(2,1)S(1)}, u32[]{:S(2)}, u32[]{:S(2)}) collective-permute-start(bf16[160,512]{1,0:T(8,128)(2,1)S(1)} %get-tuple-element.255), channel_id=1, source_target_pairs={{0,4},{4,0},{8,12},{12,8},{16,20},{20,16},{24,28},{28,24},{1,5},{5... | collective-permute-start | bytes 491528 | tf_op jit(solution)/shard_map/ppermute | solution.py:41
  174.7 35.8 %collective-permute-start.2 = (bf16[320,1440]{1,0:T(8,128)(2,1)S(1)}, bf16[320,1440]{1,0:T(8,128)(2,1)S(1)}, u32[]{:S(2)}, u32[]{:S(2)}) collective-permute-start(bf16[320,1440]{1,0:T(8,128)(2,1)S(1)} %maximum_select_fusion.10), channel_id=1, source_target_pairs={{0,8},{4,12},{8,16},{12,20},{16,24},{20,28},{24,0},{28,4},{1,9},{5... | collective-permute-start | bytes 2764808 | tf_op jit(solution)/shard_map/ppermute | solution.py:58
  185.7 45.9 %collective-permute-start.3 = (bf16[320,1440]{1,0:T(8,128)(2,1)S(1)}, bf16[320,1440]{1,0:T(8,128)(2,1)S(1)}, u32[]{:S(2)}, u32[]{:S(2)}) collective-permute-start(bf16[320,1440]{1,0:T(8,128)(2,1)S(1)} %maximum_select_fusion.10), channel_id=1, source_target_pairs={{0,24},{4,28},{8,0},{12,4},{16,8},{20,12},{24,16},{28,20},{1,25},{... | collective-permute-start | bytes 2764808 | tf_op jit(solution)/shard_map/ppermute | solution.py:58
  198.1 52.5 %collective-permute-start.23 = (bf16[2,2,160,1024]{3,2,0,1:T(8,128)(2,1)S(1)}, bf16[2,2,160,1024]{3,2,0,1:T(8,128)(2,1)S(1)}, u32[]{:S(2)}, u32[]{:S(2)}) collective-permute-start(bf16[2,2,160,1024]{3,2,0,1:T(8,128)(2,1)S(1)} %get-tuple-element.219), channel_id=1, source_target_pairs={{0,1},{1,0},{2,3},{3,2},{4,5},{5,4},{6,7},{7,6},{8,9},{9,8},{10,11... | collective-permute-start | bytes 3932168 | tf_op jit(solution)/shard_map/ppermute | solution.py:41
  210.6 34.2 %collective-permute-start.4 = (bf16[160,1440]{1,0:T(8,128)(2,1)S(1)}, bf16[160,1440]{1,0:T(8,128)(2,1)S(1)}, u32[]{:S(2)}, u32[]{:S(2)}) collective-permute-start(bf16[160,1440]{1,0:T(8,128)(2,1)S(1)} %slice.445), channel_id=1, source_target_pairs={{0,8},{4,12},{8,16},{12,20},{16,24},{20,28},{24,0},{28,4},{1,9},{5... | collective-permute-start | bytes 1382408 | tf_op jit(solution)/shard_map/ppermute | solution.py:58
  231.6 18.9 %collective-permute-start.5 = (bf16[160,1440]{1,0:T(8,128)(2,1)S(1)}, bf16[160,1440]{1,0:T(8,128)(2,1)S(1)}, u32[]{:S(2)}, u32[]{:S(2)}) collective-permute-start(bf16[160,1440]{1,0:T(8,128)(2,1)S(1)} %slice.446), channel_id=1, source_target_pairs={{0,24},{4,28},{8,0},{12,4},{16,8},{20,12},{24,16},{28,20},{1,25},{... | collective-permute-start | bytes 1382408 | tf_op jit(solution)/shard_map/ppermute | solution.py:58
  262.2 32.6 %collective-permute-start.34 = (bf16[77,640]{1,0:T(8,128)(2,1)}, bf16[77,640]{1,0:T(8,128)(2,1)}, u32[]{:S(2)}, u32[]{:S(2)}) collective-permute-start(bf16[77,640]{1,0:T(8,128)(2,1)} %get-tuple-element.236), channel_id=1, source_target_pairs={{0,8},{4,12},{8,16},{12,20},{16,24},{20,28},{24,0},{28,4},{1,9},{5... | collective-permute-start | bytes 295688 | tf_op jit(solution)/shard_map/ppermute | solution.py:58
  262.8 32.1 %collective-permute-start.36 = (bf16[77,640]{1,0:T(8,128)(2,1)}, bf16[77,640]{1,0:T(8,128)(2,1)}, u32[]{:S(2)}, u32[]{:S(2)}) collective-permute-start(bf16[77,640]{1,0:T(8,128)(2,1)} %get-tuple-element.237), channel_id=1, source_target_pairs={{0,24},{4,28},{8,0},{12,4},{16,8},{20,12},{24,16},{28,20},{1,25},{... | collective-permute-start | bytes 295688 | tf_op jit(solution)/shard_map/ppermute | solution.py:58
  266.1 28.8 %collective-permute-start.35 = (bf16[77,640]{1,0:T(8,128)(2,1)}, bf16[77,640]{1,0:T(8,128)(2,1)}, u32[]{:S(2)}, u32[]{:S(2)}) collective-permute-start(bf16[77,640]{1,0:T(8,128)(2,1)} %get-tuple-element.238), channel_id=1, source_target_pairs={{0,16},{4,20},{8,24},{12,28},{16,0},{20,4},{24,8},{28,12},{1,17},{... | collective-permute-start | bytes 295688 | tf_op jit(solution)/shard_map/ppermute | solution.py:58
  276.2 400.2 %reduce-scatter.8.cloned.1.call-start = ((), (), s32[]{:S(2)}) async-start(), calls=%async_computation.7 | async-start | bytes 3686400 | tf_op jit(solution)/shard_map/reduce_scatter | solution.py:118
  315.4 21.3 %collective-permute-start.39 = (bf16[512,320]{0,1:T(8,128)(2,1)S(1)}, bf16[512,320]{0,1:T(8,128)(2,1)S(1)}, u32[]{:S(2)}, u32[]{:S(2)}) collective-permute-start(bf16[512,320]{0,1:T(8,128)(2,1)S(1)} %convolution_convert_fusion.27), channel_id=1, source_target_pairs={{0,4},{4,0},{8,12},{12,8},{16,20},{20,16},{24,28},{28,24},{1,5},{5... | collective-permute-start | bytes 983048 | tf_op jit(solution)/shard_map/ppermute | solution.py:41
  376.8 15.7 %collective-permute-start.45 = (bf16[128,1280]{0,1:T(8,128)(2,1)S(1)}, bf16[128,1280]{0,1:T(8,128)(2,1)S(1)}, u32[]{:S(2)}, u32[]{:S(2)}) collective-permute-start(bf16[128,1280]{0,1:T(8,128)(2,1)S(1)} %dynamic-slice_convert_fusion.12), channel_id=1, source_target_pairs={{0,2},{1,3},{2,0},{3,1},{4,6},{5,7},{6,4},{7,5},{8,10},{9,11},{10,... | collective-permute-start | bytes 983048 | tf_op jit(solution)/shard_map/ppermute | solution.py:41
  440.1 465.7 %reduce-scatter.6.cloned.1.call-start = ((), (), s32[]{:S(2)}) async-start(), calls=%async_computation.6 | async-start | bytes 7372800 | tf_op jit(solution)/shard_map/reduce_scatter | solution.py:118
  443.7 222.0 %collective-permute-start.52 = (bf16[160,512]{1,0:T(8,128)(2,1)}, bf16[160,512]{1,0:T(8,128)(2,1)}, u32[]{:S(2)}, u32[]{:S(2)}) collective-permute-start(bf16[160,512]{1,0:T(8,128)(2,1)} %get-tuple-element.242), channel_id=1, source_target_pairs={{0,4},{4,0},{8,12},{12,8},{16,20},{20,16},{24,28},{28,24},{1,5},{5... | collective-permute-start | bytes 491528 | tf_op jit(solution)/shard_map/ppermute | solution.py:41
  496.6 413.1 %reduce-scatter.4.cloned.1.call-start = ((), (), s32[]{:S(2)}) async-start(), calls=%async_computation.5 | async-start | bytes 7372800 | tf_op jit(solution)/shard_map/reduce_scatter | solution.py:118
  510.2 18.0 %collective-permute-start.51 = (bf16[256,1280]{0,1:T(8,128)(2,1)}, bf16[256,1280]{0,1:T(8,128)(2,1)}, u32[]{:S(2)}, u32[]{:S(2)}) collective-permute-start(bf16[256,1280]{0,1:T(8,128)(2,1)} %maximum_select_fusion.24), channel_id=1, source_target_pairs={{0,1},{1,0},{2,3},{3,2},{4,5},{5,4},{6,7},{7,6},{8,9},{9,8},{10,11... | collective-permute-start | bytes 1966088 | tf_op jit(solution)/shard_map/ppermute | solution.py:41
  515.1 28.2 %collective-permute-start.97 = (bf16[77,640]{1,0:T(8,128)(2,1)S(1)}, bf16[77,640]{1,0:T(8,128)(2,1)S(1)}, u32[]{:S(2)}, u32[]{:S(2)}) collective-permute-start(bf16[77,640]{1,0:T(8,128)(2,1)S(1)} %fusion.109), channel_id=1, source_target_pairs={{0,4},{4,0},{8,12},{12,8},{16,20},{20,16},{24,28},{28,24},{1,5},{5... | collective-permute-start | bytes 295688 | tf_op jit(solution)/shard_map/ppermute | solution.py:41
  544.9 43.9 %collective-permute-start.98 = (bf16[77,640]{1,0:T(8,128)(2,1)}, bf16[77,640]{1,0:T(8,128)(2,1)}, u32[]{:S(2)}, u32[]{:S(2)}) collective-permute-start(bf16[77,640]{1,0:T(8,128)(2,1)} %get-tuple-element.169), channel_id=1, source_target_pairs={{0,8},{4,12},{8,16},{12,20},{16,24},{20,28},{24,0},{28,4},{1,9},{5... | collective-permute-start | bytes 295688 | tf_op jit(solution)/shard_map/ppermute | solution.py:58
  557.6 17.7 %collective-permute-start.65 = (bf16[512,640]{0,1:T(8,128)(2,1)S(1)}, bf16[512,640]{0,1:T(8,128)(2,1)S(1)}, u32[]{:S(2)}, u32[]{:S(2)}) collective-permute-start(bf16[512,640]{0,1:T(8,128)(2,1)S(1)} %pad_maximum_fusion.12), channel_id=1, source_target_pairs={{0,4},{4,0},{8,12},{12,8},{16,20},{20,16},{24,28},{28,24},{1,5},{5... | collective-permute-start | bytes 1966088 | tf_op jit(solution)/shard_map/ppermute | solution.py:41
  578.9 16.4 %collective-permute-start.66 = (bf16[256,1280]{0,1:T(8,128)(2,1)}, bf16[256,1280]{0,1:T(8,128)(2,1)}, u32[]{:S(2)}, u32[]{:S(2)}) collective-permute-start(bf16[256,1280]{0,1:T(8,128)(2,1)} %constant_dynamic-slice_fusion.10), channel_id=1, source_target_pairs={{0,1},{1,0},{2,3},{3,2},{4,5},{5,4},{6,7},{7,6},{8,9},{9,8},{10,11... | collective-permute-start | bytes 1966088 | tf_op jit(solution)/shard_map/ppermute | solution.py:41
  620.5 15.7 %collective-permute-start.70 = (bf16[2,320,512]{2,1,0:T(8,128)(2,1)S(1)}, bf16[2,320,512]{2,1,0:T(8,128)(2,1)}, u32[]{:S(2)}, u32[]{:S(2)}) collective-permute-start(bf16[2,320,512]{2,1,0:T(8,128)(2,1)S(1)} %dynamic-slice_bitcast_fusion.2), channel_id=1, source_target_pairs={{0,1},{1,0},{2,3},{3,2},{4,5},{5,4},{6,7},{7,6},{8,9},{9,8},{10,11... | collective-permute-start | bytes 1966088 | tf_op jit(solution)/shard_map/ppermute | solution.py:41
  632.8 21.0 %collective-permute-start.105 = (f32[19,320]{1,0:T(8,128)S(1)}, f32[19,320]{1,0:T(8,128)S(1)}, u32[]{:S(2)}, u32[]{:S(2)}) collective-permute-start(f32[19,320]{1,0:T(8,128)S(1)} %add.869), channel_id=1, source_target_pairs={{0,16},{4,20},{8,24},{12,28},{16,0},{20,4},{24,8},{28,12},{1,17},{... | collective-permute-start | bytes 72968 | tf_op jit(solution)/shard_map/ppermute | solution.py:41
  639.5 15.7 %collective-permute-start.71 = (bf16[320,512]{1,0:T(8,128)(2,1)}, bf16[320,512]{1,0:T(8,128)(2,1)}, u32[]{:S(2)}, u32[]{:S(2)}) collective-permute-start(bf16[320,512]{1,0:T(8,128)(2,1)} %fusion.96), channel_id=1, source_target_pairs={{0,2},{1,3},{2,0},{3,1},{4,6},{5,7},{6,4},{7,5},{8,10},{9,11},{10,... | collective-permute-start | bytes 983048 | tf_op jit(solution)/shard_map/ppermute | solution.py:41
  689.4 26.4 %collective-permute-start.73 = (bf16[160,1440]{1,0:T(8,128)(2,1)S(1)}, bf16[160,1440]{1,0:T(8,128)(2,1)S(1)}, u32[]{:S(2)}, u32[]{:S(2)}) collective-permute-start(bf16[160,1440]{1,0:T(8,128)(2,1)S(1)} %get-tuple-element.197), channel_id=1, source_target_pairs={{0,8},{4,12},{8,16},{12,20},{16,24},{20,28},{24,0},{28,4},{1,9},{5... | collective-permute-start | bytes 1382408 | tf_op jit(solution)/shard_map/ppermute | solution.py:58
  689.5 43.7 %collective-permute-start.74 = (bf16[160,1440]{1,0:T(8,128)(2,1)S(1)}, bf16[160,1440]{1,0:T(8,128)(2,1)S(1)}, u32[]{:S(2)}, u32[]{:S(2)}) collective-permute-start(bf16[160,1440]{1,0:T(8,128)(2,1)S(1)} %get-tuple-element.198), channel_id=1, source_target_pairs={{0,24},{4,28},{8,0},{12,4},{16,8},{20,12},{24,16},{28,20},{1,25},{... | collective-permute-start | bytes 1382408 | tf_op jit(solution)/shard_map/ppermute | solution.py:58
  736.2 25.2 %collective-permute-start.92 = (bf16[320,1440]{1,0:T(8,128)(2,1)S(1)}, bf16[320,1440]{1,0:T(8,128)(2,1)S(1)}, u32[]{:S(2)}, u32[]{:S(2)}) collective-permute-start(bf16[320,1440]{1,0:T(8,128)(2,1)S(1)} %pad_maximum_fusion.10), channel_id=1, source_target_pairs={{0,24},{4,28},{8,0},{12,4},{16,8},{20,12},{24,16},{28,20},{1,25},{... | collective-permute-start | bytes 2764808 | tf_op jit(solution)/shard_map/ppermute | solution.py:58
  739.3 63.4 %collective-permute-start.91 = (bf16[320,1440]{1,0:T(8,128)(2,1)S(1)}, bf16[320,1440]{1,0:T(8,128)(2,1)S(1)}, u32[]{:S(2)}, u32[]{:S(2)}) collective-permute-start(bf16[320,1440]{1,0:T(8,128)(2,1)S(1)} %pad_maximum_fusion.9), channel_id=1, source_target_pairs={{0,8},{4,12},{8,16},{12,20},{16,24},{20,28},{24,0},{28,4},{1,9},{5... | collective-permute-start | bytes 2764808 | tf_op jit(solution)/shard_map/ppermute | solution.py:58
  746.1 58.1 %collective-permute-start.82 = (bf16[2,2,160,1024]{3,2,1,0:T(8,128)(2,1)S(1)}, bf16[2,2,160,1024]{3,2,1,0:T(8,128)(2,1)S(1)}, u32[]{:S(2)}, u32[]{:S(2)}) collective-permute-start(bf16[2,2,160,1024]{3,2,1,0:T(8,128)(2,1)S(1)} %dynamic-slice_bitcast_fusion), channel_id=1, source_target_pairs={{0,1},{1,0},{2,3},{3,2},{4,5},{5,4},{6,7},{7,6},{8,9},{9,8},{10,11... | collective-permute-start | bytes 3932168 | tf_op jit(solution)/shard_map/ppermute | solution.py:41
  753.5 76.5 %collective-permute-start.80 = (bf16[160,1440]{1,0:T(8,128)(2,1)S(1)}, bf16[160,1440]{1,0:T(8,128)(2,1)S(1)}, u32[]{:S(2)}, u32[]{:S(2)}) collective-permute-start(bf16[160,1440]{1,0:T(8,128)(2,1)S(1)} %get-tuple-element.203), channel_id=1, source_target_pairs={{0,8},{4,12},{8,16},{12,20},{16,24},{20,28},{24,0},{28,4},{1,9},{5... | collective-permute-start | bytes 1382408 | tf_op jit(solution)/shard_map/ppermute | solution.py:58
  755.0 75.1 %collective-permute-start.81 = (bf16[160,1440]{1,0:T(8,128)(2,1)S(1)}, bf16[160,1440]{1,0:T(8,128)(2,1)S(1)}, u32[]{:S(2)}, u32[]{:S(2)}) collective-permute-start(bf16[160,1440]{1,0:T(8,128)(2,1)S(1)} %get-tuple-element.204), channel_id=1, source_target_pairs={{0,24},{4,28},{8,0},{12,4},{16,8},{20,12},{24,16},{28,20},{1,25},{... | collective-permute-start | bytes 1382408 | tf_op jit(solution)/shard_map/ppermute | solution.py:58
  806.6 93.3 %collective-permute-start.93 = (bf16[160,1440]{1,0:T(8,128)(2,1)}, bf16[160,1440]{1,0:T(8,128)(2,1)S(1)}, u32[]{:S(2)}, u32[]{:S(2)}) collective-permute-start(bf16[160,1440]{1,0:T(8,128)(2,1)} %dynamic-slice_convert_fusion), channel_id=1, source_target_pairs={{0,4},{4,0},{8,12},{12,8},{16,20},{20,16},{24,28},{28,24},{1,5},{5... | collective-permute-start | bytes 1382408 | tf_op jit(solution)/shard_map/ppermute | solution.py:41
  835.7 51.1 %collective-permute-start.89 = (bf16[320,1440]{1,0:T(8,128)(2,1)S(1)}, bf16[320,1440]{1,0:T(8,128)(2,1)S(1)}, u32[]{:S(2)}, u32[]{:S(2)}) collective-permute-start(bf16[320,1440]{1,0:T(8,128)(2,1)S(1)} %pad_maximum_fusion.8), channel_id=1, source_target_pairs={{0,24},{4,28},{8,0},{12,4},{16,8},{20,12},{24,16},{28,20},{1,25},{... | collective-permute-start | bytes 2764808 | tf_op jit(solution)/shard_map/ppermute | solution.py:58
  841.0 45.8 %collective-permute-start.88 = (bf16[320,1440]{1,0:T(8,128)(2,1)S(1)}, bf16[320,1440]{1,0:T(8,128)(2,1)S(1)}, u32[]{:S(2)}, u32[]{:S(2)}) collective-permute-start(bf16[320,1440]{1,0:T(8,128)(2,1)S(1)} %pad_maximum_fusion.7), channel_id=1, source_target_pairs={{0,8},{4,12},{8,16},{12,20},{16,24},{20,28},{24,0},{28,4},{1,9},{5... | collective-permute-start | bytes 2764808 | tf_op jit(solution)/shard_map/ppermute | solution.py:58
  841.1 39.9 %collective-permute-start.95 = (f32[2,9,160]{2,0,1:T(2,128)S(1)}, f32[2,9,160]{2,0,1:T(2,128)S(1)}, u32[]{:S(2)}, u32[]{:S(2)}) collective-permute-start(f32[2,9,160]{2,0,1:T(2,128)S(1)} %maximum_select_fusion.59), channel_id=1, source_target_pairs={{0,16},{4,20},{8,24},{12,28},{16,0},{20,4},{24,8},{28,12},{1,17},{... | collective-permute-start | bytes 34568 | tf_op jit(solution)/shard_map/ppermute | solution.py:41
  (231 other events, 2523.4 us)
Sparse Core Ops, SparseCore 0:
  19.7 157.3 all-gather.2
  276.3 141.3 all-gather.4
  440.2 74.4 reduce-scatter.7
  518.6 124.4 reduce-scatter.5
  653.9 177.4 reduce-scatter.3
